TPU v7x, 32 devices: a whole 2x2x4 slice. The times are simulated.
32 devices in a mesh: fsdp: 16 (over z, y, core), tp: 2 (over x).
Axes of the slice: x: 2, y: 2, z: 4, core: 2. Of those that a mesh axis runs over, the one named last changes fastest.
Arguments:
- inputs: bfloat16 [17664, 1024], P(('fsdp', 'tp')), may hold values from -6 to 6
- skip_inputs: bfloat16 [2, 17664, 1024], P(None, ('fsdp', 'tp')), may hold values from -6 to 6
- skip_weight: bfloat16 [2, 2048, 1024], P(None, 'fsdp', 'tp'), may hold values from -0.125 to 0.125
- skip_bias: bfloat16 [2, 1024], P(None, ('fsdp', 'tp')), may hold values from -1.5 to 1.5
- first_gain: bfloat16 [2, 1024], P(None, ('fsdp', 'tp')), may hold values from 0.5 to 1.5
- first_shift: bfloat16 [2, 1024], P(None, ('fsdp', 'tp')), may hold values from -1.5 to 1.5
- attention_in: bfloat16 [2, 1024, 3, 1024], P(None, 'fsdp', None, 'tp'), may hold values from -0.1875 to 0.1875
- attention_out: bfloat16 [2, 1024, 1024], P(None, 'tp', 'fsdp'), may hold values from -0.75 to 0.75
- out_bias: bfloat16 [2, 1024], P(None, ('fsdp', 'tp')), may hold values from -1.5 to 1.5
- second_gain: bfloat16 [2, 1024], P(None, ('fsdp', 'tp')), may hold values from 0.5 to 1.5
- second_shift: bfloat16 [2, 1024], P(None, ('fsdp', 'tp')), may hold values from -1.5 to 1.5
- up_weight: bfloat16 [2, 1024, 4096], P(None, 'fsdp', 'tp'), may hold values from -0.1875 to 0.1875
- up_bias: bfloat16 [2, 4096], P(None, ('fsdp', 'tp')), may hold values from -2.5 to 2.5
- down_weight: bfloat16 [2, 4096, 1024], P(None, 'tp', 'fsdp'), may hold values from -0.1875 to 0.1875
- down_bias: bfloat16 [2, 1024], P(None, ('fsdp', 'tp')), may hold values from -1.5 to 1.5
- cotangent: bfloat16 [17664, 1024], P(('fsdp', 'tp')), may hold values from -6 to 6
Outputs:
- output: float32 [17664, 1024], P(('fsdp', 'tp'))
- input_grad: float32 [17664, 1024], P(('fsdp', 'tp'))
- skip_grad: float32 [2, 17664, 1024], P(None, ('fsdp', 'tp'))
- skip_weight_grad: float32 [2, 2048, 1024], P(None, 'fsdp', 'tp')
- skip_bias_grad: float32 [2, 1024], P(None, ('fsdp', 'tp'))
- first_gain_grad: float32 [2, 1024], P(None, ('fsdp', 'tp'))
- first_shift_grad: float32 [2, 1024], P(None, ('fsdp', 'tp'))
- attention_in_grad: float32 [2, 1024, 3, 1024], P(None, 'fsdp', None, 'tp')
- attention_out_grad: float32 [2, 1024, 1024], P(None, 'tp', 'fsdp')
- out_bias_grad: float32 [2, 1024], P(None, ('fsdp', 'tp'))
- second_gain_grad: float32 [2, 1024], P(None, ('fsdp', 'tp'))
- second_shift_grad: float32 [2, 1024], P(None, ('fsdp', 'tp'))
- up_weight_grad: float32 [2, 1024, 4096], P(None, 'fsdp', 'tp')
- up_bias_grad: float32 [2, 4096], P(None, ('fsdp', 'tp'))
- down_weight_grad: float32 [2, 4096, 1024], P(None, 'tp', 'fsdp')
- down_bias_grad: float32 [2, 1024], P(None, ('fsdp', 'tp'))
All inputs are finite; a program needn't handle non-finite values.
Results may differ from a plain program's by a relative error of at most 0.023.
Values may be sent and summed in bfloat16 or wider, within the bound.
No kernel may reach another device: no remote copies, remote signals or barrier semaphores. Data moves between devices by JAX's collectives and lax.ppermute only.
A program may use at most 384 MiB of HBM per device.

v0:
```python
import jax
import jax.numpy as jnp
from jax import lax
from jax.sharding import PartitionSpec as P

HEAD_DIM = 64
FF = 4096
SEQ_LEN = 1104
LAYERS = 2


epsilon = 1e-05


def norm_apply(values_in, gain, shift):
    center = values_in - jnp.mean(values_in, -1, keepdims=True)
    spread = jnp.mean(center * center, -1, keepdims=True)
    return center * lax.rsqrt(spread + epsilon) * gain + shift


def gelu_exact(values_in):
    return jax.nn.gelu(values_in, approximate=False)


def split_heads(triple_seq):
    head_count = triple_seq.shape[2] // HEAD_DIM
    return (triple_seq.reshape(SEQ_LEN, 3, head_count, HEAD_DIM), head_count)


def attend(triple_seq):
    heads_split, head_count = split_heads(triple_seq)
    query, key_rows, value_rows = (heads_split[:, 0], heads_split[:, 1], heads_split[:, 2])
    half_rows = SEQ_LEN // 2
    score_scale = HEAD_DIM ** (-0.5)
    outputs, totals = ([], [])
    for part_index in range(2):
        query_part = query[part_index * half_rows : (part_index + 1) * half_rows]
        scores = (
            jnp.einsum("qhd,khd->hqk", query_part, key_rows, preferred_element_type=jnp.float32)
            * score_scale
        )
        row_top = jnp.max(scores, -1, keepdims=True)
        exp_scores = jnp.exp(scores - row_top)
        row_total = jnp.sum(exp_scores, -1, keepdims=True)
        low_probs = (exp_scores / row_total).astype(jnp.bfloat16)
        mixed = jnp.einsum(
            "hqk,khd->qhd", low_probs, value_rows, preferred_element_type=jnp.float32
        )
        outputs.append(mixed.astype(jnp.bfloat16).reshape(half_rows, head_count * HEAD_DIM))
        totals.append((row_top + jnp.log(row_total))[..., 0])
    return (jnp.concatenate(outputs, 0), jnp.concatenate(totals, 1))


def attend_back(items):
    triple_seq, log_total, mixed_grad = items
    heads_split, head_count = split_heads(triple_seq)
    query, key_rows, value_rows = (heads_split[:, 0], heads_split[:, 1], heads_split[:, 2])
    grad_heads = mixed_grad.reshape(SEQ_LEN, head_count, HEAD_DIM)
    half_rows = SEQ_LEN // 2
    score_scale = HEAD_DIM ** (-0.5)
    key_grad = jnp.zeros((SEQ_LEN, head_count, HEAD_DIM), jnp.float32)
    value_grad = jnp.zeros((SEQ_LEN, head_count, HEAD_DIM), jnp.float32)
    query_grads = []
    for part_index in range(2):
        rows_here = slice(part_index * half_rows, (part_index + 1) * half_rows)
        query_part = query[rows_here]
        grad_part = grad_heads[rows_here]
        scores = (
            jnp.einsum("qhd,khd->hqk", query_part, key_rows, preferred_element_type=jnp.float32)
            * score_scale
        )
        probs = jnp.exp(scores - log_total[:, rows_here][..., None])
        low_probs = probs.astype(jnp.bfloat16)
        value_grad = value_grad + jnp.einsum(
            "hqk,qhd->khd", low_probs, grad_part, preferred_element_type=jnp.float32
        )
        prob_grad = jnp.einsum(
            "qhd,khd->hqk", grad_part, value_rows, preferred_element_type=jnp.float32
        )
        score_grad = (probs * (prob_grad - jnp.sum(prob_grad * probs, -1, keepdims=True))).astype(
            jnp.bfloat16
        )
        query_grads.append(
            jnp.einsum("hqk,khd->qhd", score_grad, key_rows, preferred_element_type=jnp.float32)
            * score_scale
        )
        key_grad = (
            key_grad
            + jnp.einsum("hqk,qhd->khd", score_grad, query_part, preferred_element_type=jnp.float32)
            * score_scale
        )
    stacked = jnp.stack([jnp.concatenate(query_grads, 0), key_grad, value_grad], 1)
    return stacked.reshape(SEQ_LEN, 3, head_count * HEAD_DIM).astype(jnp.bfloat16)


def body(
    inputs,
    skip_inputs,
    skip_weight,
    skip_bias,
    first_gain,
    first_shift,
    attention_in,
    attention_out,
    out_bias,
    second_gain,
    second_shift,
    up_weight,
    up_bias,
    down_weight,
    down_bias,
    cotangent,
):

    def fetch_layer(layer_index):
        small_params = (
            lax.all_gather(skip_bias[layer_index], ("fsdp", "tp"), axis=0, tiled=True),
            lax.all_gather(first_gain[layer_index], ("fsdp", "tp"), axis=0, tiled=True),
            lax.all_gather(first_shift[layer_index], ("fsdp", "tp"), axis=0, tiled=True),
            lax.all_gather(out_bias[layer_index], ("fsdp", "tp"), axis=0, tiled=True),
            lax.all_gather(second_gain[layer_index], ("fsdp", "tp"), axis=0, tiled=True),
            lax.all_gather(second_shift[layer_index], ("fsdp", "tp"), axis=0, tiled=True),
            lax.all_gather(up_bias[layer_index], ("fsdp", "tp"), axis=0, tiled=True),
            lax.all_gather(down_bias[layer_index], ("fsdp", "tp"), axis=0, tiled=True),
        )
        block = (
            lax.all_gather(skip_weight[layer_index], "fsdp", axis=0, tiled=True),
            lax.all_gather(attention_in[layer_index], "fsdp", axis=0, tiled=True),
            lax.all_gather(attention_out[layer_index], "fsdp", axis=1, tiled=True),
            lax.all_gather(up_weight[layer_index], "fsdp", axis=0, tiled=True),
            lax.all_gather(down_weight[layer_index], "fsdp", axis=1, tiled=True),
        )
        weight_up, weight_down = (block[3], block[4])
        unit_width = weight_up.shape[1]
        bias_up = lax.dynamic_slice_in_dim(
            small_params[6], lax.axis_index("tp") * unit_width, unit_width
        )
        return (small_params, block[0], block[1], block[2], weight_up, bias_up, weight_down)

    def rows_of(normed):
        return lax.all_gather(normed, "tp", axis=0, tiled=True)

    def sum_rows(partial_value):
        return lax.psum_scatter(
            partial_value.astype(jnp.bfloat16), "tp", scatter_dimension=0, tiled=True
        ).astype(jnp.float32)

    def grad_rows_of(grad_low):
        return lax.all_gather(grad_low, "tp", axis=0, tiled=True)

    def sum_row_grads(partial_value):
        return lax.psum_scatter(
            partial_value.astype(jnp.bfloat16), "tp", scatter_dimension=0, tiled=True
        ).astype(jnp.float32)

    def forward(stream, skip_rows, weights):
        small_params, weight_skip, weight_qkv, weight_out, weight_up, bias_up, weight_down = weights
        joined = jnp.concatenate([stream.astype(jnp.bfloat16), skip_rows], 1)
        rows_joined = rows_of(joined)
        hidden_part = jnp.dot(rows_joined, weight_skip, preferred_element_type=jnp.float32)
        hidden = (
            lax.all_to_all(
                hidden_part.astype(jnp.bfloat16), "tp", split_axis=0, concat_axis=1, tiled=True
            ).astype(hidden_part.dtype)
            + small_params[0]
        )
        first_norm = norm_apply(hidden, small_params[1], small_params[2]).astype(jnp.bfloat16)
        rows_first = rows_of(first_norm)
        triple = jnp.einsum(
            "td,dch->tch", rows_first, weight_qkv, preferred_element_type=jnp.float32
        ).astype(jnp.bfloat16)
        seq_count = rows_first.shape[0] // SEQ_LEN
        head_out, log_total = lax.map(attend, triple.reshape(seq_count, SEQ_LEN, 3, -1))
        head_out = head_out.reshape(rows_first.shape[0], -1)
        middle = (
            hidden
            + sum_rows(jnp.dot(head_out, weight_out, preferred_element_type=jnp.float32))
            + small_params[3]
        )
        second_norm = norm_apply(middle, small_params[4], small_params[5]).astype(jnp.bfloat16)
        rows_second = rows_of(second_norm)
        preact = jnp.dot(rows_second, weight_up, preferred_element_type=jnp.float32) + bias_up
        activated = gelu_exact(preact).astype(jnp.bfloat16)
        branch = sum_rows(jnp.dot(activated, weight_down, preferred_element_type=jnp.float32))
        result = middle + branch + small_params[7]
        kept = (
            rows_joined,
            hidden,
            rows_first,
            triple,
            head_out,
            log_total,
            middle,
            rows_second,
            preact,
            activated,
        )
        return (result, kept)

    streams = [inputs.astype(jnp.float32)]
    stored = []
    for layer_index in range(LAYERS):
        weights = fetch_layer(layer_index)
        result, kept_here = forward(streams[layer_index], skip_inputs[layer_index], weights)
        stored.append((weights, kept_here))
        streams.append(result)
    output = streams[LAYERS]
    stream_grad = cotangent.astype(jnp.float32)
    skip_parts = [None] * LAYERS
    small_parts = [None] * LAYERS
    block_parts = [None] * LAYERS
    for layer_index in reversed(range(LAYERS)):
        weights = fetch_layer(layer_index)
        unused_result, kept = forward(streams[layer_index], skip_inputs[layer_index], weights)
        (
            backward_small_params,
            backward_weight_skip,
            backward_weight_qkv,
            backward_weight_out,
            backward_weight_up,
            backward_bias_up,
            backward_weight_down,
        ) = weights
        (
            backward_rows_joined,
            backward_hidden,
            backward_rows_first,
            backward_triple,
            backward_head_out,
            backward_log_total,
            backward_middle,
            backward_rows_second,
            backward_preact,
            backward_activated,
        ) = kept
        down_bias_grad = jnp.sum(stream_grad, 0)
        grad_rows = grad_rows_of(stream_grad.astype(jnp.bfloat16))
        act_grad = jnp.einsum(
            "td,fd->tf", grad_rows, backward_weight_down, preferred_element_type=jnp.float32
        )
        down_weight_grad = jnp.einsum(
            "tf,td->fd", backward_activated, grad_rows, preferred_element_type=jnp.float32
        )
        gelu_unused, gelu_pull = jax.vjp(gelu_exact, backward_preact)
        pre_grad = gelu_pull(act_grad)[0]
        up_bias_part = jnp.sum(pre_grad, 0)
        pre_low = pre_grad.astype(jnp.bfloat16)
        up_weight_grad = jnp.einsum(
            "td,tf->df", backward_rows_second, pre_low, preferred_element_type=jnp.float32
        )
        second_grad = sum_row_grads(
            jnp.einsum("tf,df->td", pre_low, backward_weight_up, preferred_element_type=jnp.float32)
        )
        up_bias_full = lax.dynamic_update_slice_in_dim(
            jnp.zeros((FF,), jnp.float32),
            up_bias_part,
            lax.axis_index("tp") * up_bias_part.shape[0],
            0,
        )
        norm_unused, second_pull = jax.vjp(
            norm_apply, backward_middle, backward_small_params[4], backward_small_params[5]
        )
        middle_norm_grad, second_gain_grad, second_shift_grad = second_pull(second_grad)
        middle_grad = stream_grad + middle_norm_grad
        out_bias_grad = jnp.sum(middle_grad, 0)
        middle_rows = grad_rows_of(middle_grad.astype(jnp.bfloat16))
        mixed_grad = jnp.einsum(
            "td,hd->th", middle_rows, backward_weight_out, preferred_element_type=jnp.float32
        ).astype(jnp.bfloat16)
        out_weight_grad = jnp.einsum(
            "th,td->hd", backward_head_out, middle_rows, preferred_element_type=jnp.float32
        )
        backward_seq_count = backward_rows_first.shape[0] // SEQ_LEN
        triple_grad = lax.map(
            attend_back,
            (
                backward_triple.reshape(backward_seq_count, SEQ_LEN, 3, -1),
                backward_log_total,
                mixed_grad.reshape(backward_seq_count, SEQ_LEN, -1),
            ),
        )
        triple_grad = triple_grad.reshape(backward_triple.shape)
        qkv_weight_grad = jnp.einsum(
            "td,tch->dch", backward_rows_first, triple_grad, preferred_element_type=jnp.float32
        )
        first_grad = sum_row_grads(
            jnp.einsum(
                "tch,dch->td", triple_grad, backward_weight_qkv, preferred_element_type=jnp.float32
            )
        )
        norm_unused_two, first_pull = jax.vjp(
            norm_apply, backward_hidden, backward_small_params[1], backward_small_params[2]
        )
        hidden_norm_grad, first_gain_grad, first_shift_grad = first_pull(first_grad)
        hidden_grad = middle_grad + hidden_norm_grad
        skip_bias_grad = jnp.sum(hidden_grad, 0)
        hidden_low = hidden_grad.astype(jnp.bfloat16)
        hidden_cols = lax.all_to_all(hidden_low, "tp", split_axis=1, concat_axis=0, tiled=True)
        joined_grad = sum_row_grads(
            jnp.einsum(
                "te,ce->tc", hidden_cols, backward_weight_skip, preferred_element_type=jnp.float32
            )
        )
        skip_weight_grad = jnp.einsum(
            "tc,te->ce", backward_rows_joined, hidden_cols, preferred_element_type=jnp.float32
        )
        small_grads = (
            lax.psum_scatter(skip_bias_grad, ("fsdp", "tp"), scatter_dimension=0, tiled=True),
            lax.psum_scatter(
                first_gain_grad.astype(jnp.float32), ("fsdp", "tp"), scatter_dimension=0, tiled=True
            ),
            lax.psum_scatter(
                first_shift_grad.astype(jnp.float32),
                ("fsdp", "tp"),
                scatter_dimension=0,
                tiled=True,
            ),
            lax.psum_scatter(out_bias_grad, ("fsdp", "tp"), scatter_dimension=0, tiled=True),
            lax.psum_scatter(
                second_gain_grad.astype(jnp.float32),
                ("fsdp", "tp"),
                scatter_dimension=0,
                tiled=True,
            ),
            lax.psum_scatter(
                second_shift_grad.astype(jnp.float32),
                ("fsdp", "tp"),
                scatter_dimension=0,
                tiled=True,
            ),
            lax.psum_scatter(up_bias_full, ("fsdp", "tp"), scatter_dimension=0, tiled=True),
            lax.psum_scatter(down_bias_grad, ("fsdp", "tp"), scatter_dimension=0, tiled=True),
        )
        block_grads = (
            lax.psum_scatter(
                skip_weight_grad.astype(jnp.bfloat16), "fsdp", scatter_dimension=0, tiled=True
            ).astype(jnp.float32),
            lax.psum_scatter(
                qkv_weight_grad.astype(jnp.bfloat16), "fsdp", scatter_dimension=0, tiled=True
            ).astype(jnp.float32),
            lax.psum_scatter(
                out_weight_grad.astype(jnp.bfloat16), "fsdp", scatter_dimension=1, tiled=True
            ).astype(jnp.float32),
            lax.psum_scatter(
                up_weight_grad.astype(jnp.bfloat16), "fsdp", scatter_dimension=0, tiled=True
            ).astype(jnp.float32),
            lax.psum_scatter(
                down_weight_grad.astype(jnp.bfloat16), "fsdp", scatter_dimension=1, tiled=True
            ).astype(jnp.float32),
        )
        width = backward_weight_skip.shape[0] // 2
        stream_grad, skip_part, small_grads, block_grads = (
            joined_grad[:, :width],
            joined_grad[:, width:],
            small_grads,
            block_grads,
        )
        skip_parts[layer_index] = skip_part
        small_parts[layer_index] = small_grads
        block_parts[layer_index] = block_grads

    def stack_small(position):
        return jnp.stack([small_parts[index_layer][position] for index_layer in range(LAYERS)])

    def stack_block(position):
        return jnp.stack([block_parts[index_layer][position] for index_layer in range(LAYERS)])

    return (
        output,
        stream_grad,
        jnp.stack(skip_parts),
        stack_block(0),
        stack_small(0),
        stack_small(1),
        stack_small(2),
        stack_block(1),
        stack_block(2),
        stack_small(3),
        stack_small(4),
        stack_small(5),
        stack_block(3),
        stack_small(6),
        stack_block(4),
        stack_small(7),
    )


def solution(mesh):
    placed = (
        P(("fsdp", "tp"), None),
        P(None, ("fsdp", "tp"), None),
        P(None, "fsdp", "tp"),
        P(None, ("fsdp", "tp")),
        P(None, ("fsdp", "tp")),
        P(None, ("fsdp", "tp")),
        P(None, "fsdp", None, "tp"),
        P(None, "tp", "fsdp"),
        P(None, ("fsdp", "tp")),
        P(None, ("fsdp", "tp")),
        P(None, ("fsdp", "tp")),
        P(None, "fsdp", "tp"),
        P(None, ("fsdp", "tp")),
        P(None, "tp", "fsdp"),
        P(None, ("fsdp", "tp")),
        P(("fsdp", "tp"), None),
    )
    return jax.shard_map(
        body,
        mesh=mesh,
        in_specs=placed,
        out_specs=(
            P(("fsdp", "tp"), None),
            P(("fsdp", "tp"), None),
            P(None, ("fsdp", "tp"), None),
            P(None, "fsdp", "tp"),
            P(None, ("fsdp", "tp")),
            P(None, ("fsdp", "tp")),
            P(None, ("fsdp", "tp")),
            P(None, "fsdp", None, "tp"),
            P(None, "tp", "fsdp"),
            P(None, ("fsdp", "tp")),
            P(None, ("fsdp", "tp")),
            P(None, ("fsdp", "tp")),
            P(None, "fsdp", "tp"),
            P(None, ("fsdp", "tp")),
            P(None, "tp", "fsdp"),
            P(None, ("fsdp", "tp")),
        ),
        check_vma=False,
    )
```

profile of v0, /device:TPU:1, one launch (start us, length us, event | category | flops | bytes accessed | tf_op | source)
XLA Modules:
  0.0 2376.6 jit_solution(7424419993216299713)
XLA Ops:
  15.4 39.3 %all-gather.67.cloned.1.call-done = bf16[1,2048,512]{2,1,0:T(8,128)(2,1)} async-done(((bf16[1,128,512]{2,1,0:T(8,128)(2,1)}), bf16[1,2048,512]{2,1,0:T(8,128)(2,1)}) %all-gather.67.cloned.1.call-update) | async-done | bytes 2097168 | tf_op jit(solution)/shard_map/all_gather | solution.py:127
  54.7 60.9 %all-gather.47.cloned.1.call-done = bf16[1104,2048]{1,0:T(8,128)(2,1)} async-done(((bf16[552,2048]{1,0:T(8,128)(2,1)}), bf16[1104,2048]{1,0:T(8,128)(2,1)}) %all-gather.47.cloned.1.call-update) | async-done | bytes 4522000 | tf_op jit(solution)/shard_map/all_gather | solution.py:141
  128.0 47.0 %all-reduce.31 = (bf16[1024]{0:T(1024)(128)(2,1)S(1)}, bf16[1024]{0:T(1024)(128)(2,1)S(1)}, bf16[1024]{0:T(1024)(128)(2,1)S(1)}, bf16[1024]{0:T(1024)(128)(2,1)S...) all-reduce(bf16[1024]{0:T(1024)(128)(2,1)S(1)} %dynamic-update-slic, ...), channel_id=5, replica_groups=mesh['fsdp'=16,'tp'=2] {'fsdp','tp'}, use_global_device_ids=true, to_apply=%add.2 | all-reduce | flops 14336 | bytes 57344
  179.4 34.3 %all-gather.49.cloned.1.call-done = bf16[1104,1024]{1,0:T(8,128)(2,1)} async-done(((bf16[552,1024]{1,0:T(8,128)(2,1)}), bf16[1104,1024]{1,0:T(8,128)(2,1)}) %all-gather.49.cloned.1.call-update) | async-done | bytes 2261008 | tf_op jit(solution)/shard_map/all_gather | solution.py:141
  280.8 32.8 %reduce-scatter.21.cloned.1.call-done = bf16[552,1024]{1,0:T(8,128)(2,1)} async-done(((bf16[1104,1024]{1,0:T(8,128)(2,1)}), bf16[552,1024]{1,0:T(8,128)(2,1)}) %reduce-scatter.21.cloned.1.call-update) | async-done | bytes 1130512 | tf_op jit(solution)/shard_map/reduce_scatter | solution.py:144
  320.6 64.7 %all-gather.10 = bf16[1,4096]{1,0:T(2,128)(2,1)S(1)} all-gather(bf16[1,128]{1,0:T(2,128)(2,1)S(1)} %get-tuple-element.171), channel_id=12, replica_groups=mesh['fsdp'=16,'tp'=2] {'fsdp','tp'}, dimensions={1}, use_global_device_ids=true | all-gather | bytes 8448 | tf_op jit(solution)/shard_map/all_gather | solution.py:123
  385.3 17.3 all-gather.51.cloned.1.call-done
  402.6 28.2 %multiply_convert_fusion.5 = (bf16[1104,2048]{1,0:T(8,128)(2,1)}, f32[1104,2048]{1,0:T(8,128)}, f32[1104,2048]{1,0:T(8,128)}) fusion(f32[2048]{0:T(1024)S(1)} %bitcast.396, bf16[1104,1024]{1,0:T(8,128)(2,1)} %all-gather.51.cloned.1.call-done, bf16[1,1024,2048]{2,1,0:T(8,128)(2,1)} %all-gather.73.cloned.1.call-done), kind=kOutput, calls=%fused_computation.65 | convolution fusion | flops 4779737088 | bytes 29073408 | tf_op jit(solution)/shard_map/dot_general | solution.py:182
  430.8 25.7 %all-gather.75.cloned.1.call-done = bf16[1,2048,1024]{1,2,0:T(8,128)(2,1)} async-done(((bf16[1,2048,64]{1,2,0:T(8,128)(2,1)}), bf16[1,2048,1024]{1,2,0:T(8,128)(2,1)}) %all-gather.75.cloned.1.call-update) | async-done | bytes 4194320 | tf_op jit(solution)/shard_map/all_gather | solution.py:131
  467.2 31.1 %reduce-scatter.23.cloned.1.call-done = bf16[552,1024]{1,0:T(8,128)(2,1)} async-done(((bf16[1104,1024]{1,0:T(8,128)(2,1)}), bf16[552,1024]{1,0:T(8,128)(2,1)}) %reduce-scatter.23.cloned.1.call-update) | async-done | bytes 1130512 | tf_op jit(solution)/shard_map/reduce_scatter | solution.py:144
  502.3 40.0 %all-gather.77.cloned.1.call-done = bf16[1,2048,512]{2,1,0:T(8,128)(2,1)} async-done(((bf16[1,128,512]{2,1,0:T(8,128)(2,1)}), bf16[1,2048,512]{2,1,0:T(8,128)(2,1)}) %all-gather.77.cloned.1.call-update) | async-done | bytes 2097168 | tf_op jit(solution)/shard_map/all_gather | solution.py:127
  542.3 60.8 %all-gather.53.cloned.1.call-done = bf16[1104,2048]{1,0:T(8,128)(2,1)} async-done(((bf16[552,2048]{1,0:T(8,128)(2,1)}), bf16[1104,2048]{1,0:T(8,128)(2,1)}) %all-gather.53.cloned.1.call-update) | async-done | bytes 4522000 | tf_op jit(solution)/shard_map/all_gather | solution.py:141
  631.1 19.8 all-gather.79.cloned.1.call-done
  650.9 35.4 %all-gather.55.cloned.1.call-done = bf16[1104,1024]{1,0:T(8,128)(2,1)} async-done(((bf16[552,1024]{1,0:T(8,128)(2,1)}), bf16[1104,1024]{1,0:T(8,128)(2,1)}) %all-gather.55.cloned.1.call-update) | async-done | bytes 2261008 | tf_op jit(solution)/shard_map/all_gather | solution.py:141
  752.4 33.1 %reduce-scatter.25.cloned.1.call-done = bf16[552,1024]{1,0:T(8,128)(2,1)} async-done(((bf16[1104,1024]{1,0:T(8,128)(2,1)}), bf16[552,1024]{1,0:T(8,128)(2,1)}) %reduce-scatter.25.cloned.1.call-update) | async-done | bytes 1130512 | tf_op jit(solution)/shard_map/reduce_scatter | solution.py:144
  791.2 64.4 %all-gather.23 = bf16[1,4096]{1,0:T(2,128)(2,1)S(1)} all-gather(bf16[1,128]{1,0:T(2,128)(2,1)S(1)} %copy-done.125), channel_id=25, replica_groups=mesh['fsdp'=16,'tp'=2] {'fsdp','tp'}, dimensions={1}, use_global_device_ids=true | all-gather | bytes 8448 | tf_op jit(solution)/shard_map/all_gather | solution.py:123
  855.6 18.7 all-gather.57.cloned.1.call-done
  874.3 28.4 %multiply_convert_fusion.4 = (bf16[1104,2048]{1,0:T(8,128)(2,1)}, f32[1104,2048]{1,0:T(8,128)}, f32[1104,2048]{1,0:T(8,128)}) fusion(f32[2048]{0:T(1024)S(1)} %bitcast.397, bf16[1104,1024]{1,0:T(8,128)(2,1)} %all-gather.57.cloned.1.call-done, bf16[1,1024,2048]{2,1,0:T(8,128)(2,1)} %all-gather.83.cloned.1.call-done), kind=kOutput, calls=%fused_computation.52 | convolution fusion | flops 4779737088 | bytes 29073408 | tf_op jit(solution)/shard_map/dot_general | solution.py:182
  910.9 53.2 %all-gather.85.cloned.1.call-done = bf16[1,2048,1024]{1,2,0:T(8,128)(2,1)} async-done(((bf16[1,2048,64]{1,2,0:T(8,128)(2,1)}), bf16[1,2048,1024]{1,2,0:T(8,128)(2,1)}) %all-gather.85.cloned.1.call-update) | async-done | bytes 4194320 | tf_op jit(solution)/shard_map/all_gather | solution.py:131
  964.0 14.7 fusion.184
  997.1 21.7 reduce-scatter.29.cloned.1.call-done
  1022.4 32.9 %reduce-scatter.27.cloned.1.call-done = bf16[552,1024]{1,0:T(8,128)(2,1)} async-done(((bf16[1104,1024]{1,0:T(8,128)(2,1)}), bf16[552,1024]{1,0:T(8,128)(2,1)}) %reduce-scatter.27.cloned.1.call-update) | async-done | bytes 1130512 | tf_op jit(solution)/shard_map/reduce_scatter | solution.py:144
  1061.6 33.8 %all-gather.61.cloned.1.call-done = bf16[1104,1024]{1,0:T(8,128)(2,1)} async-done(((bf16[552,1024]{1,0:T(8,128)(2,1)}), bf16[1104,1024]{1,0:T(8,128)(2,1)}) %all-gather.61.cloned.1.call-update) | async-done | bytes 2261008 | tf_op jit(solution)/shard_map/all_gather | solution.py:149
  1102.1 16.3 multiply_reduce_fusion.3
  1118.4 13.8 multiply_convert_fusion.3
  1177.0 13.9 multiply_convert_fusion.2
  1208.5 33.3 %reduce-scatter.31.cloned.1.call-done = bf16[552,1024]{1,0:T(8,128)(2,1)} async-done(((bf16[1104,1024]{1,0:T(8,128)(2,1)}), bf16[552,1024]{1,0:T(8,128)(2,1)}) %reduce-scatter.31.cloned.1.call-update) | async-done | bytes 1130512 | tf_op jit(solution)/shard_map/reduce_scatter | solution.py:152
  1247.6 16.5 all_to_all.74
  1269.8 58.8 %reduce-scatter.33.cloned.1.call-done = bf16[552,2048]{1,0:T(8,128)(2,1)} async-done(((bf16[1104,2048]{1,0:T(8,128)(2,1)}), bf16[552,2048]{1,0:T(8,128)(2,1)}) %reduce-scatter.33.cloned.1.call-update) | async-done | bytes 2261008 | tf_op jit(solution)/shard_map/reduce_scatter | solution.py:152
  1331.0 35.1 %all-gather.63.cloned.1.call-done = bf16[1104,1024]{1,0:T(8,128)(2,1)} async-done(((bf16[552,1024]{1,0:T(8,128)(2,1)}), bf16[1104,1024]{1,0:T(8,128)(2,1)}) %all-gather.63.cloned.1.call-update) | async-done | bytes 2261008 | tf_op jit(solution)/shard_map/all_gather | solution.py:149
  1366.1 14.7 fusion.185
  1393.6 29.2 %reduce-scatter.35.cloned.1.call-done = bf16[552,1024]{1,0:T(8,128)(2,1)} async-done(((bf16[1104,1024]{1,0:T(8,128)(2,1)}), bf16[552,1024]{1,0:T(8,128)(2,1)}) %reduce-scatter.35.cloned.1.call-update) | async-done | bytes 1130512 | tf_op jit(solution)/shard_map/reduce_scatter | solution.py:152
  1431.6 33.8 %all-gather.65.cloned.1.call-done = bf16[1104,1024]{1,0:T(8,128)(2,1)} async-done(((bf16[552,1024]{1,0:T(8,128)(2,1)}), bf16[1104,1024]{1,0:T(8,128)(2,1)}) %all-gather.65.cloned.1.call-update) | async-done | bytes 2261008 | tf_op jit(solution)/shard_map/all_gather | solution.py:149
  1472.0 16.0 multiply_reduce_fusion.1
  1488.1 13.8 multiply_convert_fusion.1
  1546.6 13.9 multiply_convert_fusion
  1660.0 16.5 all_to_all.75
  1687.8 74.2 %reduce-scatter.57.cloned.1.call-done = bf16[2048,64]{0,1:T(8,128)(2,1)} async-done(((bf16[2048,1024]{0,1:T(8,128)(2,1)}), bf16[2048,64]{0,1:T(8,128)(2,1)}) %reduce-scatter.57.cloned.1.call-update) | async-done | bytes 262160 | tf_op jit(solution)/shard_map/reduce_scatter | solution.py:347
  1764.1 72.7 %reduce-scatter.55.cloned.1.call-done = bf16[64,2048]{1,0:T(8,128)(2,1)} async-done(((bf16[1024,2048]{1,0:T(8,128)(2,1)}), bf16[64,2048]{1,0:T(8,128)(2,1)}) %reduce-scatter.55.cloned.1.call-update) | async-done | bytes 262160 | tf_op jit(solution)/shard_map/reduce_scatter | solution.py:344
  1836.7 75.5 %reduce-scatter.53.cloned.1.call-done = bf16[64,2048]{1,0:T(8,128)(2,1)} async-done(((bf16[1024,2048]{1,0:T(8,128)(2,1)}), bf16[64,2048]{1,0:T(8,128)(2,1)}) %reduce-scatter.53.cloned.1.call-update) | async-done | bytes 262160 | tf_op jit(solution)/shard_map/reduce_scatter | solution.py:344
  1914.3 57.8 %reduce-scatter.51.cloned.1.call-done = bf16[512,64]{0,1:T(8,128)(2,1)} async-done(((bf16[512,1024]{0,1:T(8,128)(2,1)}), bf16[512,64]{0,1:T(8,128)(2,1)}) %reduce-scatter.51.cloned.1.call-update) | async-done | bytes 65552 | tf_op jit(solution)/shard_map/reduce_scatter | solution.py:341
  1972.1 60.5 %reduce-scatter.49.cloned.1.call-done = bf16[512,64]{0,1:T(8,128)(2,1)} async-done(((bf16[512,1024]{0,1:T(8,128)(2,1)}), bf16[512,64]{0,1:T(8,128)(2,1)}) %reduce-scatter.49.cloned.1.call-update) | async-done | bytes 65552 | tf_op jit(solution)/shard_map/reduce_scatter | solution.py:341
  2034.5 43.6 %all-reduce.33 = (f32[1024]{0:T(1024)S(1)}, f32[1024]{0:T(1024)S(1)}, f32[1024]{0:T(1024)S(1)}, f32[1024]{0:T(1024)S(1)}, f32[1024]{0:T(1024)S(1)}, /*index=5*/f...) all-reduce(f32[1024]{0:T(1024)S(1)} %copy-done.102, ...), channel_id=41, replica_groups=mesh['fsdp'=16,'tp'=2] {'fsdp','tp'}, use_global_device_ids=true, to_apply=%region_43.44.clone | all-reduce | flops 22528 | bytes 163840
  2083.3 19.4 reduce-scatter.47.cloned.1.call-done
  2102.7 68.7 %reduce-scatter.45.cloned.1.call-done = bf16[64,3,512]{2,0,1:T(8,128)(2,1)} async-done(((bf16[1024,3,512]{2,0,1:T(8,128)(2,1)}), bf16[64,3,512]{2,0,1:T(8,128)(2,1)}) %reduce-scatter.45.cloned.1.call-update) | async-done | bytes 196624 | tf_op jit(solution)/shard_map/reduce_scatter | solution.py:338
  2173.4 61.8 %reduce-scatter.43.cloned.1.call-done = bf16[128,512]{1,0:T(8,128)(2,1)} async-done(((bf16[2048,512]{1,0:T(8,128)(2,1)}), bf16[128,512]{1,0:T(8,128)(2,1)}) %reduce-scatter.43.cloned.1.call-update) | async-done | bytes 131088 | tf_op jit(solution)/shard_map/reduce_scatter | solution.py:335
  2235.2 64.7 %reduce-scatter.41.cloned.1.call-done = bf16[128,512]{1,0:T(8,128)(2,1)} async-done(((bf16[2048,512]{1,0:T(8,128)(2,1)}), bf16[128,512]{1,0:T(8,128)(2,1)}) %reduce-scatter.41.cloned.1.call-update) | async-done | bytes 131088 | tf_op jit(solution)/shard_map/reduce_scatter | solution.py:335
  2301.7 59.6 %reduce-scatter.39.cloned.1.call-done = bf16[552,2048]{1,0:T(8,128)(2,1)} async-done(((bf16[1104,2048]{1,0:T(8,128)(2,1)}), bf16[552,2048]{1,0:T(8,128)(2,1)}) %reduce-scatter.39.cloned.1.call-update) | async-done | bytes 2261008 | tf_op jit(solution)/shard_map/reduce_scatter | solution.py:152
  (587 shorter events, 538.0 us)
Async XLA Ops:
  7.2 47.5 %all-gather.67.cloned.1.call-start = ((), (), s32[]{:S(2)}) async-start(), calls=%async_computation.54 | async-start | bytes 2228224 | tf_op jit(solution)/shard_map/all_gather | solution.py:127
  9.0 106.6 %all-gather.47.cloned.1.call-start = ((), (), s32[]{:S(2)}) async-start(), calls=%async_computation.24 | async-start | bytes 6782976 | tf_op jit(solution)/shard_map/all_gather | solution.py:141
  13.5 165.9 %all-gather.69.cloned.1.call-start = ((), (), s32[]{:S(2)}) async-start(), calls=%async_computation.55 | async-start | bytes 3342336 | tf_op jit(solution)/shard_map/all_gather | solution.py:128
  122.1 52.9 %all-to-all-start = ((bf16[2,552,512]{2,1,0:T(8,128)(2,1)}), bf16[2,552,512]{2,1,0:T(8,128)(2,1)S(1)}, u32[]{:S(2)}, u32[]{:S(2)}) async-start(bf16[2,552,512]{2,1,0:T(8,128)(2,1)} %bitcast.2), calls=%async_computation | async-start | bytes 2260992 | tf_op jit(solution)/shard_map/all_to_all | solution.py:162
  125.7 87.9 %all-gather.49.cloned.1.call-start = ((), (), s32[]{:S(2)}) async-start(), calls=%async_computation.25 | async-start | bytes 3391488 | tf_op jit(solution)/shard_map/all_gather | solution.py:141
  178.5 96.3 %all-gather.71.cloned.1.call-start = ((), (), s32[]{:S(2)}) async-start(), calls=%async_computation.56 | async-start | bytes 1114112 | tf_op jit(solution)/shard_map/all_gather | solution.py:129
  179.3 134.3 %reduce-scatter.21.cloned.1.call-start = ((), (), s32[]{:S(2)}) async-start(), calls=%async_computation.26 | async-start | bytes 3391488 | tf_op jit(solution)/shard_map/reduce_scatter | solution.py:144
  279.8 105.5 %all-gather.73.cloned.1.call-start = ((), (), s32[]{:S(2)}) async-start(), calls=%async_computation.57 | async-start | bytes 4456448 | tf_op jit(solution)/shard_map/all_gather | solution.py:130
  280.7 121.9 %all-gather.51.cloned.1.call-start = ((), (), s32[]{:S(2)}) async-start(), calls=%async_computation.27 | async-start | bytes 3391488 | tf_op jit(solution)/shard_map/all_gather | solution.py:141
  319.1 137.4 %all-gather.75.cloned.1.call-start = ((), (), s32[]{:S(2)}) async-start(), calls=%async_computation.58 | async-start | bytes 4456448 | tf_op jit(solution)/shard_map/all_gather | solution.py:131
  320.0 178.2 %reduce-scatter.23.cloned.1.call-start = ((), (), s32[]{:S(2)}) async-start(), calls=%async_computation.28 | async-start | bytes 3391488 | tf_op jit(solution)/shard_map/reduce_scatter | solution.py:144
  466.4 75.9 %all-gather.77.cloned.1.call-start = ((), (), s32[]{:S(2)}) async-start(), calls=%async_computation.59 | async-start | bytes 2228224 | tf_op jit(solution)/shard_map/all_gather | solution.py:127
  467.1 135.9 %all-gather.53.cloned.1.call-start = ((), (), s32[]{:S(2)}) async-start(), calls=%async_computation.29 | async-start | bytes 6782976 | tf_op jit(solution)/shard_map/all_gather | solution.py:141
  501.5 149.4 %all-gather.79.cloned.1.call-start = ((), (), s32[]{:S(2)}) async-start(), calls=%async_computation.60 | async-start | bytes 3342336 | tf_op jit(solution)/shard_map/all_gather | solution.py:128
  609.5 17.4 all-to-all-start.1
  613.1 73.1 %all-gather.55.cloned.1.call-start = ((), (), s32[]{:S(2)}) async-start(), calls=%async_computation.30 | async-start | bytes 3391488 | tf_op jit(solution)/shard_map/all_gather | solution.py:141
  630.4 116.4 %all-gather.81.cloned.1.call-start = ((), (), s32[]{:S(2)}) async-start(), calls=%async_computation.61 | async-start | bytes 1114112 | tf_op jit(solution)/shard_map/all_gather | solution.py:129
  631.0 154.5 %reduce-scatter.25.cloned.1.call-start = ((), (), s32[]{:S(2)}) async-start(), calls=%async_computation.31 | async-start | bytes 3391488 | tf_op jit(solution)/shard_map/reduce_scatter | solution.py:144
  751.7 103.9 %all-gather.83.cloned.1.call-start = ((), (), s32[]{:S(2)}) async-start(), calls=%async_computation.62 | async-start | bytes 4456448 | tf_op jit(solution)/shard_map/all_gather | solution.py:130
  752.3 122.1 %all-gather.57.cloned.1.call-start = ((), (), s32[]{:S(2)}) async-start(), calls=%async_computation.32 | async-start | bytes 3391488 | tf_op jit(solution)/shard_map/all_gather | solution.py:141
  789.8 121.1 %all-gather.59.cloned.1.call-start = ((), (), s32[]{:S(2)}) async-start(), calls=%async_computation.34 | async-start | bytes 3391488 | tf_op jit(solution)/shard_map/all_gather | solution.py:149
  790.5 173.5 %all-gather.85.cloned.1.call-start = ((), (), s32[]{:S(2)}) async-start(), calls=%async_computation.63 | async-start | bytes 4456448 | tf_op jit(solution)/shard_map/all_gather | solution.py:131
  791.1 227.6 %reduce-scatter.29.cloned.1.call-start = ((), (), s32[]{:S(2)}) async-start(), calls=%async_computation.35 | async-start | bytes 3391488 | tf_op jit(solution)/shard_map/reduce_scatter | solution.py:152
  986.9 68.3 %reduce-scatter.27.cloned.1.call-start = ((), (), s32[]{:S(2)}) async-start(), calls=%async_computation.33 | async-start | bytes 3391488 | tf_op jit(solution)/shard_map/reduce_scatter | solution.py:144
  997.0 98.4 %all-gather.61.cloned.1.call-start = ((), (), s32[]{:S(2)}) async-start(), calls=%async_computation.36 | async-start | bytes 3391488 | tf_op jit(solution)/shard_map/all_gather | solution.py:149
  1060.3 181.6 %reduce-scatter.31.cloned.1.call-start = ((), (), s32[]{:S(2)}) async-start(), calls=%async_computation.37 | async-start | bytes 3391488 | tf_op jit(solution)/shard_map/reduce_scatter | solution.py:152
  1208.1 120.6 %reduce-scatter.33.cloned.1.call-start = ((), (), s32[]{:S(2)}) async-start(), calls=%async_computation.38 | async-start | bytes 6782976 | tf_op jit(solution)/shard_map/reduce_scatter | solution.py:152
  1269.8 96.3 %all-gather.63.cloned.1.call-start = ((), (), s32[]{:S(2)}) async-start(), calls=%async_computation.39 | async-start | bytes 3391488 | tf_op jit(solution)/shard_map/all_gather | solution.py:149
  1331.0 91.8 %reduce-scatter.35.cloned.1.call-start = ((), (), s32[]{:S(2)}) async-start(), calls=%async_computation.40 | async-start | bytes 3391488 | tf_op jit(solution)/shard_map/reduce_scatter | solution.py:152
  1389.0 76.4 %all-gather.65.cloned.1.call-start = ((), (), s32[]{:S(2)}) async-start(), calls=%async_computation.41 | async-start | bytes 3391488 | tf_op jit(solution)/shard_map/all_gather | solution.py:149
  1430.3 225.0 %reduce-scatter.37.cloned.1.call-start = ((), (), s32[]{:S(2)}) async-start(), calls=%async_computation.42 | async-start | bytes 3391488 | tf_op jit(solution)/shard_map/reduce_scatter | solution.py:152
  1577.2 110.6 %reduce-scatter.59.cloned.1.call-start = ((), (), s32[]{:S(2)}) async-start(), calls=%async_computation.53 | async-start | bytes 4456448 | tf_op jit(solution)/shard_map/reduce_scatter | solution.py:347
  1587.5 174.5 %reduce-scatter.57.cloned.1.call-start = ((), (), s32[]{:S(2)}) async-start(), calls=%async_computation.52 | async-start | bytes 4456448 | tf_op jit(solution)/shard_map/reduce_scatter | solution.py:347
  1598.7 238.1 %reduce-scatter.55.cloned.1.call-start = ((), (), s32[]{:S(2)}) async-start(), calls=%async_computation.51 | async-start | bytes 4456448 | tf_op jit(solution)/shard_map/reduce_scatter | solution.py:344
  1609.8 302.4 %reduce-scatter.53.cloned.1.call-start = ((), (), s32[]{:S(2)}) async-start(), calls=%async_computation.50 | async-start | bytes 4456448 | tf_op jit(solution)/shard_map/reduce_scatter | solution.py:344
  1621.1 351.1 %reduce-scatter.51.cloned.1.call-start = ((), (), s32[]{:S(2)}) async-start(), calls=%async_computation.49 | async-start | bytes 1114112 | tf_op jit(solution)/shard_map/reduce_scatter | solution.py:341
  1626.7 405.9 %reduce-scatter.49.cloned.1.call-start = ((), (), s32[]{:S(2)}) async-start(), calls=%async_computation.48 | async-start | bytes 1114112 | tf_op jit(solution)/shard_map/reduce_scatter | solution.py:341
  1631.8 470.9 %reduce-scatter.47.cloned.1.call-start = ((), (), s32[]{:S(2)}) async-start(), calls=%async_computation.47 | async-start | bytes 3342336 | tf_op jit(solution)/shard_map/reduce_scatter | solution.py:338
  1639.5 532.0 %reduce-scatter.45.cloned.1.call-start = ((), (), s32[]{:S(2)}) async-start(), calls=%async_computation.46 | async-start | bytes 3342336 | tf_op jit(solution)/shard_map/reduce_scatter | solution.py:338
  1648.3 586.9 %reduce-scatter.43.cloned.1.call-start = ((), (), s32[]{:S(2)}) async-start(), calls=%async_computation.45 | async-start | bytes 2228224 | tf_op jit(solution)/shard_map/reduce_scatter | solution.py:335
  1655.1 644.8 %reduce-scatter.41.cloned.1.call-start = ((), (), s32[]{:S(2)}) async-start(), calls=%async_computation.44 | async-start | bytes 2228224 | tf_op jit(solution)/shard_map/reduce_scatter | solution.py:335
  1680.6 680.6 %reduce-scatter.39.cloned.1.call-start = ((), (), s32[]{:S(2)}) async-start(), calls=%async_computation.43 | async-start | bytes 6782976 | tf_op jit(solution)/shard_map/reduce_scatter | solution.py:152
  1687.0 347.4 %copy-start.101 = (f32[1024]{0:T(1024)S(1)}, f32[1024]{0:T(1024)}, u32[]{:S(2)}) copy-start(f32[1024]{0:T(1024)} %get-tuple-element.98) | copy-start | bytes 12292
  1687.0 347.4 %copy-start.102 = (f32[1024]{0:T(1024)S(1)}, f32[1024]{0:T(1024)}, u32[]{:S(2)}) copy-start(f32[1024]{0:T(1024)} %get-tuple-element.99) | copy-start | bytes 12292
  1687.0 347.4 %copy-start.103 = (f32[1024]{0:T(1024)S(1)}, f32[1024]{0:T(1024)}, u32[]{:S(2)}) copy-start(f32[1024]{0:T(1024)} %get-tuple-element.148) | copy-start | bytes 12292
  1687.0 347.4 %copy-start.104 = (bf16[1024]{0:T(1024)(128)(2,1)S(1)}, bf16[1024]{0:T(1024)(128)(2,1)}, u32[]{:S(2)}) copy-start(bf16[1024]{0:T(1024)(128)(2,1)} %get-tuple-element.80) | copy-start | bytes 6148
  1687.0 347.4 %copy-start.105 = (bf16[1024]{0:T(1024)(128)(2,1)S(1)}, bf16[1024]{0:T(1024)(128)(2,1)}, u32[]{:S(2)}) copy-start(bf16[1024]{0:T(1024)(128)(2,1)} %get-tuple-element.89) | copy-start | bytes 6148
  1687.0 347.4 %copy-start.106 = (bf16[1024]{0:T(1024)(128)(2,1)S(1)}, bf16[1024]{0:T(1024)(128)(2,1)}, u32[]{:S(2)}) copy-start(bf16[1024]{0:T(1024)(128)(2,1)} %get-tuple-element.78) | copy-start | bytes 6148
  (133 other events, 3442.6 us)
Sparse Core Ops, SparseCore 0:
  10.8 43.8 all-gather.66
  56.8 58.7 all-gather.46
  118.4 46.6 all-gather.68
  178.7 34.9 all-gather.48
  216.2 38.3 all-gather.70
  279.9 33.6 reduce-scatter.20
  316.3 51.0 all-gather.72
  369.5 33.0 all-gather.50
  405.3 51.1 all-gather.74
  466.5 31.6 reduce-scatter.22
  500.4 41.8 all-gather.76
  544.2 58.7 all-gather.52
  605.2 45.6 all-gather.78
  652.9 33.3 all-gather.54
  688.3 38.3 all-gather.80
  751.8 33.6 reduce-scatter.24
  788.1 51.1 all-gather.82
  841.2 33.0 all-gather.56
  875.9 34.9 all-gather.58
  912.9 51.1 all-gather.84
  987.0 31.6 reduce-scatter.28
  1021.6 33.6 reduce-scatter.26
  1060.4 34.9 all-gather.60
  1208.2 33.6 reduce-scatter.30
  1269.9 58.6 reduce-scatter.32
  1331.1 34.9 all-gather.62
  1389.1 33.6 reduce-scatter.34
  1430.4 34.9 all-gather.64
  1577.3 33.6 reduce-scatter.36
  1614.7 70.7 reduce-scatter.58
  1689.8 72.1 reduce-scatter.56
  1765.9 70.8 reduce-scatter.54
  1840.9 71.2 reduce-scatter.52
  1915.9 56.1 reduce-scatter.50
  1976.2 56.3 reduce-scatter.48
  2036.2 66.4 reduce-scatter.46
  2106.4 65.0 reduce-scatter.44
  2175.2 59.9 reduce-scatter.42
  2239.3 60.6 reduce-scatter.40
  2302.8 58.4 reduce-scatter.38
where the time goes:
time: 2390 us; the launch traced here: 2380 us
  waiting for transfers between devices  1420 us (59%)
  matrix products  451 us (19%)
  blocking collectives  253 us (11%)
  other arithmetic  150 us (6%)
  local copies, waits for them, and re-layouts  74.2 us (3%)
    all_gather x6, waiting for transfers between devices, rows_of(): return lax.all_gather(normed, 'tp', axis=0, tiled=True)  227 us
    reduce_scatter x6, waiting for transfers between devices, sum_row_grads(): lax.psum_scatter(partial_value.astype(jnp.bfloat16), 'tp', scatter_dimens...  203 us
    reduce_scatter x2, waiting for transfers between devices, body(): lax.psum_scatter(up_weight_grad.astype(jnp.bfloat16), 'fsdp', scatter_dim...  148 us
    reduce_scatter x4, waiting for transfers between devices, sum_rows(): lax.psum_scatter(partial_value.astype(jnp.bfloat16), 'tp', scatter_dimens...  130 us
    all_gather x2, blocking collectives, fetch_layer(): lax.all_gather(up_bias[layer_index], ('fsdp', 'tp'), axis=0, tiled=True)  129 us
    reduce_scatter x2, waiting for transfers between devices, body(): lax.psum_scatter(skip_weight_grad.astype(jnp.bfloat16), 'fsdp', scatter_d...  127 us
    reduce_scatter x2, waiting for transfers between devices, body(): lax.psum_scatter(out_weight_grad.astype(jnp.bfloat16), 'fsdp', scatter_di...  118 us
    all_gather x4, waiting for transfers between devices, grad_rows_of(): return lax.all_gather(grad_low, 'tp', axis=0, tiled=True)  111 us
  transfers between devices with their start and end apart: 42, of which 34 were waited for; matrix products, arithmetic and copies ran while one was open for 14% of the time, Pallas kernels for 0%

commit v1 on v0

--- a/solution.py
+++ b/solution.py
@@ -1,6 +1,8 @@
 import jax
 import jax.numpy as jnp
 from jax import lax
+from jax.experimental import pallas as pl
+from jax.experimental.pallas import tpu as pltpu
 from jax.sharding import PartitionSpec as P
 
 HEAD_DIM = 64
@@ -93,7 +95,7 @@
     return stacked.reshape(SEQ_LEN, 3, head_count * HEAD_DIM).astype(jnp.bfloat16)
 
 
-def body(
+def general_body(
     inputs,
     skip_inputs,
     skip_weight,
@@ -385,6 +387,682 @@
     )
 
 
+BOTH = ("fsdp", "tp")
+GAUSS = 0.3989422804014327
+
+
+def ring_order(chips):
+    half = chips // 2
+    return [2 * i for i in range(half)] + [2 * i + 1 for i in reversed(range(half))]
+
+
+def choose_body(mesh):
+    fsdp_size, tp_size = (mesh.shape["fsdp"], mesh.shape["tp"])
+    if tp_size != 2 or fsdp_size < 4 or fsdp_size & (fsdp_size - 1):
+        return general_body
+    return lambda *arrays: fast_body(fsdp_size, *arrays)
+
+
+def row_chunks(count):
+    return [(begin, min(384, count - begin)) for begin in range(0, count, 384)]
+
+
+NT = (((1,), (1,)), ((), ()))
+TN = (((0,), (0,)), ((), ()))
+
+
+def head_lanes(value, head):
+    lane = lax.broadcasted_iota(jnp.int32, value.shape, 1)
+    return jnp.where((lane >= HEAD_DIM) == (head == 1), value, jnp.zeros_like(value))
+
+
+def attention_forward(triple):
+    tokens, width = (triple.shape[0], triple.shape[1] // 3)
+    pairs = width // (2 * HEAD_DIM)
+
+    def kernel(query_ref, key_ref, value_ref, out_ref, total_ref):
+        keys = key_ref[...]
+        values = value_ref[...]
+        for begin, rows in row_chunks(tokens):
+            query = query_ref[begin : begin + rows, :] * jnp.bfloat16(HEAD_DIM**-0.5)
+            mixed, totals = ([], [])
+            for head in range(2):
+                scores = lax.dot_general(
+                    head_lanes(query, head), keys, NT, preferred_element_type=jnp.float32
+                )
+                top = jnp.max(scores, -1, keepdims=True)
+                grown = jnp.exp(scores - top)
+                total = jnp.sum(grown, -1, keepdims=True)
+                mixed.append(
+                    jnp.dot(
+                        grown.astype(jnp.bfloat16), values, preferred_element_type=jnp.float32
+                    )
+                    / total
+                )
+                totals.append(top + jnp.log(total))
+            lane = lax.broadcasted_iota(jnp.int32, mixed[0].shape, 1)
+            out_ref[begin : begin + rows, :] = jnp.where(
+                lane < HEAD_DIM, mixed[0], mixed[1]
+            ).astype(jnp.bfloat16)
+            both = jnp.where(lane < HEAD_DIM, totals[0], totals[1]).T
+            total_ref[0, 0:1, begin : begin + rows] = both[0:1, :]
+            total_ref[0, 1:2, begin : begin + rows] = both[HEAD_DIM : HEAD_DIM + 1, :]
+
+    def part(index):
+        return pl.BlockSpec((tokens, 2 * HEAD_DIM), lambda i: (0, index * pairs + i))
+
+    return pl.pallas_call(
+        kernel,
+        grid=(pairs,),
+        in_specs=[part(0), part(1), part(2)],
+        out_specs=[part(0), pl.BlockSpec((1, 2, tokens), lambda i: (i, 0, 0))],
+        out_shape=[
+            jax.ShapeDtypeStruct((tokens, width), jnp.bfloat16),
+            jax.ShapeDtypeStruct((pairs, 2, tokens), jnp.float32),
+        ],
+        compiler_params=pltpu.CompilerParams(vmem_limit_bytes=48 << 20),
+        cost_estimate=pl.CostEstimate(
+            flops=16 * pairs * tokens * tokens * HEAD_DIM,
+            bytes_accessed=8 * tokens * width,
+            transcendentals=2 * pairs * tokens * tokens,
+        ),
+    )(triple, triple, triple)
+
+
+def attention_backward(triple, head_out, log_total, mixed_grad):
+    tokens, width = (triple.shape[0], triple.shape[1] // 3)
+    pairs = width // (2 * HEAD_DIM)
+    score_scale = HEAD_DIM**-0.5
+
+    def kernel(
+        query_ref, key_ref, value_ref, out_ref, total_ref, grad_ref, dq_ref, dk_ref, dv_ref, sum_ref
+    ):
+        query = query_ref[...] * jnp.bfloat16(score_scale)
+        grad = grad_ref[...]
+        product = grad.astype(jnp.float32) * out_ref[...].astype(jnp.float32)
+        ones = jnp.ones((8, 2 * HEAD_DIM), jnp.float32)
+        deltas = [
+            lax.dot_general(
+                head_lanes(ones, head),
+                product,
+                NT,
+                precision=lax.Precision.HIGHEST,
+                preferred_element_type=jnp.float32,
+            )[0:1, :]
+            for head in range(2)
+        ]
+        for begin, rows in row_chunks(tokens):
+            keys = key_ref[begin : begin + rows, :]
+            values = value_ref[begin : begin + rows, :]
+            key_grads, value_grads = ([], [])
+            for head in range(2):
+                keys_here = head_lanes(keys, head)
+                scores = lax.dot_general(
+                    keys_here, query, NT, preferred_element_type=jnp.float32
+                )
+                probs = jnp.exp(scores - total_ref[0, head : head + 1, :])
+                prob_grad = lax.dot_general(
+                    head_lanes(values, head), grad, NT, preferred_element_type=jnp.float32
+                )
+                score_grad = (probs * (prob_grad - deltas[head])).astype(jnp.bfloat16)
+                value_grads.append(
+                    jnp.dot(
+                        probs.astype(jnp.bfloat16), grad, preferred_element_type=jnp.float32
+                    )
+                )
+                key_grads.append(jnp.dot(score_grad, query, preferred_element_type=jnp.float32))
+                query_grad = lax.dot_general(
+                    score_grad, keys_here, TN, preferred_element_type=jnp.float32
+                )
+                if begin == 0 and head == 0:
+                    sum_ref[...] = query_grad
+                else:
+                    sum_ref[...] += query_grad
+            lane = lax.broadcasted_iota(jnp.int32, key_grads[0].shape, 1)
+            dk_ref[begin : begin + rows, :] = jnp.where(
+                lane < HEAD_DIM, key_grads[0], key_grads[1]
+            ).astype(jnp.bfloat16)
+            dv_ref[begin : begin + rows, :] = jnp.where(
+                lane < HEAD_DIM, value_grads[0], value_grads[1]
+            ).astype(jnp.bfloat16)
+        dq_ref[...] = (sum_ref[...] * score_scale).astype(jnp.bfloat16)
+
+    def part(index):
+        return pl.BlockSpec((tokens, 2 * HEAD_DIM), lambda i: (0, index * pairs + i))
+
+    grads = pl.pallas_call(
+        kernel,
+        grid=(pairs,),
+        in_specs=[
+            part(0),
+            part(1),
+            part(2),
+            part(0),
+            pl.BlockSpec((1, 2, tokens), lambda i: (i, 0, 0)),
+            part(0),
+        ],
+        out_specs=[part(0)] * 3,
+        out_shape=[jax.ShapeDtypeStruct((tokens, width), jnp.bfloat16)] * 3,
+        scratch_shapes=[pltpu.VMEM((tokens, 2 * HEAD_DIM), jnp.float32)],
+        compiler_params=pltpu.CompilerParams(vmem_limit_bytes=48 << 20),
+        cost_estimate=pl.CostEstimate(
+            flops=40 * pairs * tokens * tokens * HEAD_DIM,
+            bytes_accessed=16 * tokens * width,
+            transcendentals=2 * pairs * tokens * tokens,
+        ),
+    )(triple, triple, triple, head_out, log_total, mixed_grad)
+    return jnp.concatenate(grads, 1)
+
+
+def fast_body(
+    fsdp_size,
+    inputs,
+    skip_inputs,
+    skip_weight,
+    skip_bias,
+    first_gain,
+    first_shift,
+    attention_in,
+    attention_out,
+    out_bias,
+    second_gain,
+    second_shift,
+    up_weight,
+    up_bias,
+    down_weight,
+    down_bias,
+    cotangent,
+):
+    chips = fsdp_size // 2
+    order = ring_order(chips)
+    core = lax.axis_index("fsdp") % 2
+    chip = lax.axis_index("fsdp") // 2
+    column = lax.axis_index("tp")
+    place_of = [order.index(q) for q in range(chips)]
+    place = jnp.asarray(place_of, jnp.int32)[chip]
+    order_table = jnp.asarray(order, jnp.int32)
+
+    core_pairs = [(i, i ^ 1) for i in range(fsdp_size)]
+    diagonal_pairs = []
+    for q in range(chips):
+        one, two = (q * 4 + 2, q * 4 + 1)
+        diagonal_pairs += [(one, two), (two, one)]
+    ring_pairs = {}
+    for step in (1, -1):
+        ring_pairs[step] = [
+            (order[i] * 2 + c, order[(i + step) % chips] * 2 + c)
+            for i in range(chips)
+            for c in range(2)
+        ]
+
+    def to_core(value):
+        return lax.ppermute(value, "fsdp", core_pairs)
+
+    def to_column(value):
+        return lax.ppermute(value, "tp", [(0, 1), (1, 0)])
+
+    def diagonal(value):
+        return jnp.where(core == column, value, lax.ppermute(value, BOTH, diagonal_pairs))
+
+    def along_ring(value, step):
+        return lax.ppermute(value, "fsdp", ring_pairs[step])
+
+    def chip_at(offset):
+        return order_table[(place + offset) % chips]
+
+    def pack_of(layer_index):
+        skip_rows = skip_weight[layer_index]
+        half_rows = skip_rows.shape[0] // 2
+        qkv_rows = attention_in[layer_index]
+        first = jnp.concatenate(
+            [
+                skip_rows[:half_rows],
+                skip_rows[half_rows:],
+                qkv_rows.reshape(qkv_rows.shape[0], -1),
+                attention_out[layer_index].T,
+            ],
+            1,
+        )
+        second = jnp.concatenate([up_weight[layer_index], down_weight[layer_index].T], 1)
+        return first, second
+
+    def in_pair(value):
+        other = to_column(value)
+        return jnp.where(
+            column == 0,
+            jnp.concatenate([value, other], 0),
+            jnp.concatenate([other, value], 0),
+        )
+
+    def gather(packed):
+        pair = in_pair(diagonal(packed))
+        middle_column = pair.shape[1] // 2
+        ahead, behind = (pair, pair)
+        blocks = {0: pair}
+        for step in range(1, chips // 2):
+            ahead = along_ring(ahead, 1)
+            behind = along_ring(behind, -1)
+            blocks[-step] = ahead
+            blocks[step] = behind
+        blocks[chips // 2] = (
+            along_ring(ahead[:, :middle_column], 1),
+            along_ring(behind[:, middle_column:], -1),
+        )
+        return blocks
+
+    def assemble(blocks, pieces):
+        offsets = sorted(blocks)
+        operands, jobs, shapes = ([], [], [])
+        for begin, width, slabs in pieces:
+            shapes.append((chips * blocks[0].shape[0] * slabs, width))
+        pair_rows = blocks[0].shape[0]
+        half_rows = pair_rows // 2
+        for at, offset in enumerate(offsets):
+            held = blocks[offset] if isinstance(blocks[offset], tuple) else (blocks[offset],)
+            start = 0
+            for part in held:
+                stop = start + part.shape[1]
+                for which, (begin, width, slabs) in enumerate(pieces):
+                    for slab in range(slabs):
+                        low = max(start, begin + slab * width)
+                        high = min(stop, begin + (slab + 1) * width)
+                        if low >= high:
+                            continue
+                        to = low - begin - slab * width
+                        spans = (
+                            [(0, pair_rows, 0)]
+                            if slabs == 1
+                            else [
+                                (i * half_rows, half_rows, (i * slabs + slab) * half_rows)
+                                for i in range(2)
+                            ]
+                        )
+                        for row, rows, to_row in spans:
+                            jobs.append(
+                                (len(operands), row, rows, low - start, high - low, which, at)
+                                + (to_row, to)
+                            )
+                operands.append(part)
+                start = stop
+
+        def kernel(at_ref, *refs):
+            sources, targets = (refs[: len(operands)], refs[len(operands) :][: len(shapes)])
+            buffers = refs[len(operands) + len(shapes) : -2]
+            sems, out_sems = refs[-2:]
+            copies = [[] for _ in shapes]
+            for which in range(len(shapes)):
+                for index, job in enumerate(jobs):
+                    source, row, rows, col, width, target, at, to_row, to = job
+                    if target != which:
+                        continue
+                    block_rows = pair_rows * pieces[which][2]
+                    begin = pl.multiple_of(at_ref[at] * block_rows + to_row, 16)
+                    copy = pltpu.make_async_copy(
+                        sources[source].at[pl.ds(row, rows), pl.ds(col, width)],
+                        buffers[which].at[pl.ds(begin, rows), pl.ds(to, width)],
+                        sems.at[index],
+                    )
+                    copy.start()
+                    copies[which].append(copy)
+            outs = []
+            for which in range(len(shapes)):
+                for copy in copies[which]:
+                    copy.wait()
+                out = pltpu.make_async_copy(buffers[which], targets[which], out_sems.at[which])
+                out.start()
+                outs.append(out)
+            for out in outs:
+                out.wait()
+
+        places = jnp.stack([chip_at(offset) for offset in offsets])
+        moved = sum(2 * 2 * r * w for r, w in shapes)
+        return pl.pallas_call(
+            kernel,
+            out_shape=[jax.ShapeDtypeStruct(shape, jnp.bfloat16) for shape in shapes],
+            in_specs=[pl.BlockSpec(memory_space=pltpu.SMEM)]
+            + [pl.BlockSpec(memory_space=pl.ANY)] * len(operands),
+            out_specs=[pl.BlockSpec(memory_space=pl.ANY)] * len(shapes),
+            scratch_shapes=[pltpu.VMEM(shape, jnp.bfloat16) for shape in shapes]
+            + [pltpu.SemaphoreType.DMA((len(jobs),)), pltpu.SemaphoreType.DMA((len(shapes),))],
+            compiler_params=pltpu.CompilerParams(vmem_limit_bytes=24 << 20),
+            cost_estimate=pl.CostEstimate(flops=0, bytes_accessed=moved, transcendentals=0),
+        )(places, *operands)
+
+    def weights_of(layer_index):
+        first, second = pack_of(layer_index)
+        skip_width = skip_weight.shape[2]
+        qkv_width = attention_in.shape[2] * attention_in.shape[3]
+        out_width = attention_out.shape[1]
+        up_width = up_weight.shape[2]
+        begin = 2 * skip_width
+        weight_skip, weight_qkv, weight_out = assemble(
+            gather(first),
+            [
+                (0, skip_width, 2),
+                (begin, qkv_width, 1),
+                (begin + qkv_width, out_width, 1),
+            ],
+        )
+        weight_up, weight_down = assemble(
+            gather(second), [(0, up_width, 1), (up_width, down_weight.shape[1], 1)]
+        )
+        return weight_skip, weight_qkv, weight_out, weight_up, weight_down
+
+    def scatter(tensors):
+        def block(offset):
+            at = chip_at(offset)
+            parts = []
+            for tensor in tensors:
+                rows = tensor.shape[0] // chips
+                parts.append(lax.dynamic_slice_in_dim(tensor, at * rows, rows, 0))
+            return jnp.concatenate(parts, 1).astype(jnp.float32)
+
+        width = sum(t.shape[1] for t in tensors)
+        middle_column = width // 2
+        half = chips // 2
+        far = block(half)
+        sums = []
+        for step in (1, -1):
+            if step == 1:
+                got = along_ring(far[:, :middle_column].astype(jnp.bfloat16), step)
+                empty = jnp.zeros((got.shape[0], width - middle_column), got.dtype)
+                got = jnp.concatenate([got, empty], 1)
+            else:
+                got = along_ring(far[:, middle_column:].astype(jnp.bfloat16), step)
+                empty = jnp.zeros((got.shape[0], middle_column), got.dtype)
+                got = jnp.concatenate([empty, got], 1)
+            for distance in range(half - 1, 0, -1):
+                got = along_ring(
+                    (block(step * distance) + got.astype(jnp.float32)).astype(jnp.bfloat16), step
+                )
+            sums.append(got.astype(jnp.float32))
+        mine = block(0) + sums[0] + sums[1]
+        half_rows = mine.shape[0] // 2
+        keep = lax.dynamic_slice_in_dim(mine, column * half_rows, half_rows, 0)
+        send = lax.dynamic_slice_in_dim(mine, (1 - column) * half_rows, half_rows, 0)
+        total = keep + to_column(send.astype(jnp.bfloat16)).astype(jnp.float32)
+        return diagonal(total.astype(jnp.bfloat16)).astype(jnp.float32)
+
+    small_names = (
+        skip_bias,
+        first_gain,
+        first_shift,
+        out_bias,
+        second_gain,
+        second_shift,
+        up_bias,
+        down_bias,
+    )
+    small_widths = [value.shape[1] for value in small_names]
+    small_total = sum(small_widths) * LAYERS
+    packed_small = jnp.concatenate([value.reshape(-1) for value in small_names])
+    padded = -(-small_total // 1024) * 1024
+    packed_small = jnp.pad(packed_small, (0, padded - small_total)).reshape(1, -1, 128)
+
+    bits = chips.bit_length() - 1
+
+    def to_partner(value, bit):
+        if bit == 0:
+            return to_column(value)
+        if bit == 1:
+            return to_core(value)
+        flip = 1 << (bit - 2)
+        pairs = [(q * 2 + c, (q ^ flip) * 2 + c) for q in range(chips) for c in range(2)]
+        return lax.ppermute(value, "fsdp", pairs)
+
+    def side_of(bit):
+        return column if bit == 0 else core if bit == 1 else (chip >> (bit - 2)) & 1
+
+    all_small = packed_small
+    for bit in range(bits + 2):
+        other = to_partner(all_small, bit)
+        all_small = jnp.where(
+            side_of(bit) == 0,
+            jnp.concatenate([all_small, other], 0),
+            jnp.concatenate([other, all_small], 0),
+        )
+    all_small = all_small.reshape(2 * fsdp_size, -1)
+
+    def sum_small(packed):
+        for bit in reversed(range(bits + 2)):
+            count = packed.shape[0] // 2
+            side = side_of(bit)
+            keep = jnp.where(side == 0, packed[:count], packed[count:])
+            send = jnp.where(side == 0, packed[count:], packed[:count])
+            packed = keep + to_partner(send, bit)
+        return packed[0]
+
+    def small_of(layer_index):
+        values, begin = ([], 0)
+        for width in small_widths:
+            values.append(
+                all_small[
+                    :, begin + layer_index * width : begin + (layer_index + 1) * width
+                ].reshape(-1)
+            )
+            begin += LAYERS * width
+        unit_width = up_weight.shape[2]
+        values[6] = lax.dynamic_slice_in_dim(values[6], core * unit_width, unit_width)
+        return values
+
+    def rows_of(value):
+        return jnp.concatenate([value, to_core(value)], 0)
+
+    def sum_rows(partial_value):
+        count = partial_value.shape[0] // 2
+        return partial_value[:count] + to_core(partial_value[count:].astype(jnp.bfloat16)).astype(
+            jnp.float32
+        )
+
+    def forward(stream_low, stream, skip_rows, weights, small):
+        weight_skip, weight_qkv, weight_out, weight_up, weight_down = weights
+        joined = jnp.concatenate([stream_low, skip_rows], 1)
+        rows_joined = rows_of(joined)
+        hidden_part = jnp.dot(rows_joined, weight_skip, preferred_element_type=jnp.float32)
+        count = joined.shape[0]
+        own_part = hidden_part[:count]
+        other_part = to_core(hidden_part[count:].astype(jnp.bfloat16)).astype(jnp.float32)
+        hidden = (
+            jnp.where(
+                core == 0,
+                jnp.concatenate([own_part, other_part], 1),
+                jnp.concatenate([other_part, own_part], 1),
+            )
+            + small[0]
+        )
+        first_norm = norm_apply(hidden, small[1], small[2]).astype(jnp.bfloat16)
+        rows_first = rows_of(first_norm)
+        triple = jnp.dot(rows_first, weight_qkv, preferred_element_type=jnp.float32).astype(
+            jnp.bfloat16
+        )
+        head_out, log_total = attention_forward(triple)
+        middle = (
+            hidden
+            + sum_rows(
+                jnp.einsum("th,dh->td", head_out, weight_out, preferred_element_type=jnp.float32)
+            )
+            + small[3]
+        )
+        second_norm = norm_apply(middle, small[4], small[5]).astype(jnp.bfloat16)
+        rows_second = rows_of(second_norm)
+        preact = jnp.dot(rows_second, weight_up, preferred_element_type=jnp.float32) + small[6]
+        below = 0.5 + 0.5 * lax.erf(preact * (0.5**0.5))
+        activated = (preact * below).astype(jnp.bfloat16)
+        slope = (below + preact * jnp.exp(-0.5 * preact * preact) * GAUSS).astype(jnp.bfloat16)
+        branch = sum_rows(
+            jnp.einsum("tf,df->td", activated, weight_down, preferred_element_type=jnp.float32)
+        )
+        result = middle + branch + small[7]
+        kept = (
+            rows_joined,
+            hidden,
+            rows_first,
+            triple,
+            head_out,
+            log_total,
+            middle,
+            rows_second,
+            slope,
+            activated,
+        )
+        return result, kept
+
+    def backward(stream_grad, weights, small, kept):
+        weight_skip, weight_qkv, weight_out, weight_up, weight_down = weights
+        (
+            rows_joined,
+            hidden,
+            rows_first,
+            triple,
+            head_out,
+            log_total,
+            middle,
+            rows_second,
+            slope,
+            activated,
+        ) = kept
+        down_bias_grad = jnp.sum(stream_grad, 0)
+        grad_rows = rows_of(stream_grad.astype(jnp.bfloat16))
+        act_grad = jnp.dot(grad_rows, weight_down, preferred_element_type=jnp.float32)
+        down_grad = jnp.einsum(
+            "td,tf->df", grad_rows, activated, preferred_element_type=jnp.float32
+        ).astype(jnp.bfloat16)
+        pre_grad = act_grad * slope
+        up_bias_part = jnp.sum(pre_grad, 0)
+        pre_low = pre_grad.astype(jnp.bfloat16)
+        up_grad = jnp.einsum(
+            "td,tf->df", rows_second, pre_low, preferred_element_type=jnp.float32
+        ).astype(jnp.bfloat16)
+        second_grad = sum_rows(
+            jnp.einsum("tf,df->td", pre_low, weight_up, preferred_element_type=jnp.float32)
+        )
+        up_bias_full = lax.dynamic_update_slice_in_dim(
+            jnp.zeros((2 * up_bias_part.shape[0],), jnp.float32),
+            up_bias_part,
+            core * up_bias_part.shape[0],
+            0,
+        )
+        norm_unused, second_pull = jax.vjp(norm_apply, middle, small[4], small[5])
+        middle_norm_grad, second_gain_grad, second_shift_grad = second_pull(second_grad)
+        middle_grad = stream_grad + middle_norm_grad
+        out_bias_grad = jnp.sum(middle_grad, 0)
+        middle_rows = rows_of(middle_grad.astype(jnp.bfloat16))
+        mixed_grad = jnp.dot(
+            middle_rows, weight_out, preferred_element_type=jnp.float32
+        ).astype(jnp.bfloat16)
+        out_grad = jnp.einsum(
+            "td,th->dh", middle_rows, head_out, preferred_element_type=jnp.float32
+        ).astype(jnp.bfloat16)
+        triple_grad = attention_backward(triple, head_out, log_total, mixed_grad)
+        qkv_grad = jnp.einsum(
+            "td,tc->dc", rows_first, triple_grad, preferred_element_type=jnp.float32
+        ).astype(jnp.bfloat16)
+        first_grad = sum_rows(
+            jnp.einsum("tc,dc->td", triple_grad, weight_qkv, preferred_element_type=jnp.float32)
+        )
+        norm_unused_two, first_pull = jax.vjp(norm_apply, hidden, small[1], small[2])
+        hidden_norm_grad, first_gain_grad, first_shift_grad = first_pull(first_grad)
+        hidden_grad = middle_grad + hidden_norm_grad
+        skip_bias_grad = jnp.sum(hidden_grad, 0)
+        hidden_low = hidden_grad.astype(jnp.bfloat16)
+        half_width = hidden_low.shape[1] // 2
+        keep = lax.dynamic_slice_in_dim(hidden_low, core * half_width, half_width, 1)
+        send = lax.dynamic_slice_in_dim(hidden_low, (1 - core) * half_width, half_width, 1)
+        hidden_cols = jnp.concatenate([keep, to_core(send)], 0)
+        joined_grad = sum_rows(
+            jnp.einsum("te,ce->tc", hidden_cols, weight_skip, preferred_element_type=jnp.float32)
+        )
+        skip_grad = jnp.einsum(
+            "tc,te->ce", rows_joined, hidden_cols, preferred_element_type=jnp.float32
+        ).astype(jnp.bfloat16)
+        shard_rows = skip_weight.shape[1]
+        slabs = skip_grad.reshape(2 * chips, 2, shard_rows // 2, -1)
+        slabs = [slabs[:, i].reshape(-1, skip_grad.shape[1]) for i in range(2)]
+        second_total = scatter([up_grad, down_grad])
+        first_total = scatter([slabs[0], slabs[1], qkv_grad, out_grad])
+        small_grads = [
+            skip_bias_grad,
+            first_gain_grad.astype(jnp.float32),
+            first_shift_grad.astype(jnp.float32),
+            out_bias_grad,
+            second_gain_grad.astype(jnp.float32),
+            second_shift_grad.astype(jnp.float32),
+            up_bias_full,
+            down_bias_grad,
+        ]
+        return joined_grad, first_total, second_total, small_grads
+
+    stream_low = diagonal(inputs)
+    stream = stream_low.astype(jnp.float32)
+    skips = [diagonal(skip_inputs[i]) for i in range(LAYERS)]
+    weights = [weights_of(i) for i in range(LAYERS)]
+    smalls = [small_of(i) for i in range(LAYERS)]
+    kept = []
+    for layer_index in range(LAYERS):
+        stream, kept_here = forward(
+            stream_low, stream, skips[layer_index], weights[layer_index], smalls[layer_index]
+        )
+        stream_low = stream.astype(jnp.bfloat16)
+        kept.append(kept_here)
+    output = diagonal(stream_low).astype(jnp.float32)
+    stream_grad = diagonal(cotangent).astype(jnp.float32)
+    skip_parts = [None] * LAYERS
+    firsts = [None] * LAYERS
+    seconds = [None] * LAYERS
+    small_sums = [None] * LAYERS
+    for layer_index in reversed(range(LAYERS)):
+        joined_grad, firsts[layer_index], seconds[layer_index], small_grads = backward(
+            stream_grad, weights[layer_index], smalls[layer_index], kept[layer_index]
+        )
+        width = joined_grad.shape[1] // 2
+        stream_grad = joined_grad[:, :width]
+        skip_parts[layer_index] = diagonal(joined_grad[:, width:].astype(jnp.bfloat16)).astype(
+            jnp.float32
+        )
+        small_sums[layer_index] = jnp.concatenate(
+            [value.reshape(2 * fsdp_size, -1) for value in small_grads], 1
+        )
+    input_grad = diagonal(stream_grad.astype(jnp.bfloat16)).astype(jnp.float32)
+
+    small_sums = sum_small(jnp.concatenate(small_sums, 1))
+    small_sums = small_sums.reshape(LAYERS, -1)
+    skip_width = skip_weight.shape[2]
+    qkv_width = attention_in.shape[2] * attention_in.shape[3]
+    up_width = up_weight.shape[2]
+    begin = 2 * skip_width
+    skip_weight_grad = jnp.stack(
+        [jnp.concatenate([v[:, :skip_width], v[:, skip_width:begin]], 0) for v in firsts]
+    )
+    qkv_weight_grad = jnp.stack(
+        [v[:, begin : begin + qkv_width].reshape(attention_in.shape[1:]) for v in firsts]
+    )
+    out_weight_grad = jnp.stack([v[:, begin + qkv_width :].T for v in firsts])
+    up_weight_grad = jnp.stack([v[:, :up_width] for v in seconds])
+    down_weight_grad = jnp.stack([v[:, up_width:].T for v in seconds])
+    small_out, begin = ([], 0)
+    for width in small_widths:
+        small_out.append(small_sums[:, begin : begin + width])
+        begin += width
+    return (
+        output,
+        input_grad,
+        jnp.stack(skip_parts),
+        skip_weight_grad,
+        small_out[0],
+        small_out[1],
+        small_out[2],
+        qkv_weight_grad,
+        out_weight_grad,
+        small_out[3],
+        small_out[4],
+        small_out[5],
+        up_weight_grad,
+        small_out[6],
+        down_weight_grad,
+        small_out[7],
+    )
+
+
 def solution(mesh):
     placed = (
         P(("fsdp", "tp"), None),
@@ -405,7 +1083,7 @@
         P(("fsdp", "tp"), None),
     )
     return jax.shard_map(
-        body,
+        choose_body(mesh),
         mesh=mesh,
         in_specs=placed,
         out_specs=(

time: 2390 us -> 1040 us (0.44)
  waiting for transfers between devices: 1420 us -> 383 us
  matrix products: 451 us -> 166 us
  blocking collectives: 253 us -> 0 us
  starting transfers between devices: 10.2 us -> 158 us
  Pallas kernels: 0 us -> 124 us
  other arithmetic: 150 us -> 102 us
    reduce_scatter x20 -> x0, waiting for transfers between devices: 888 us -> none  [the longest x6 203 us: sum_row_grads(): lax.psum_scatter(partial_value.astype(jnp.bfloat16), 'tp', scatter_dimens...]
    all_gather x20 -> x0, waiting for transfers between devices: 516 us -> none  [the longest x6 227 us: rows_of(): return lax.all_gather(normed, 'tp', axis=0, tiled=True)]
    ppermute x0 -> x122, waiting for transfers between devices: none -> 383 us  [the longest x64 238 us: along_ring(): return lax.ppermute(value, 'fsdp', ring_pairs[step])]
    dot_general x50 -> x26, matrix products: 381 us -> 135 us  [the longest x2 21.9 us: backward(): jnp.dot(grad_rows, weight_down, preferred_element_type=jnp.float32)]
    ppermute x0 -> x122, starting transfers between devices: none -> 158 us  [the longest x16 63.7 us: diagonal(): lax.ppermute(value, BOTH, diagonal_pairs)]
    all_gather x2 -> x0, blocking collectives: 129 us -> none  [fetch_layer(): lax.all_gather(up_bias[layer_index], ('fsdp', 'tp'), axis=0, tiled=True)]
    pallas_call x0 -> x8, Pallas kernels: none -> 124 us  [the longest x2 74.6 us: attention_backward(): pl.pallas_call(kernel, grid=(pairs,), in_specs=[part(0), part(1), part(2)...]
    unnamed x2 -> x0, blocking collectives: 90.6 us -> none
  transfers between devices with their start and end apart: 42 -> 122, of which waited for: 34 -> 51; matrix products, arithmetic and copies ran while one was open for 14% -> 29% of each run, Pallas kernels for 0% -> 12%
where the time goes in v1:
time: 1040 us; the launch traced here: 1030 us
  waiting for transfers between devices  383 us (37%)
  matrix products  166 us (16%)
  starting transfers between devices  158 us (15%)
  Pallas kernels  124 us (12%)
  other arithmetic  102 us (10%)
  local copies, waits for them, and re-layouts  82.9 us (8%)
  between operations  16.2 us (2%)
    ppermute x64, waiting for transfers between devices, along_ring(): return lax.ppermute(value, 'fsdp', ring_pairs[step])  238 us
    pallas_call x2, Pallas kernels, attention_backward(): pl.pallas_call(kernel, grid=(pairs,), in_specs=[part(0), part(1), part(2)...  74.6 us
    ppermute x16, starting transfers between devices, diagonal(): lax.ppermute(value, BOTH, diagonal_pairs)  63.7 us
    ppermute x10, waiting for transfers between devices, to_column(): return lax.ppermute(value, 'tp', [(0, 1), (1, 0)])  55.8 us
    ppermute x64, starting transfers between devices, along_ring(): return lax.ppermute(value, 'fsdp', ring_pairs[step])  48.2 us
    ppermute x16, waiting for transfers between devices, diagonal(): lax.ppermute(value, BOTH, diagonal_pairs)  46.9 us
    ppermute x6, waiting for transfers between devices, to_partner(): return lax.ppermute(value, 'fsdp', pairs)  41.6 us
    pallas_call x2, Pallas kernels, attention_forward(): pl.pallas_call(kernel, grid=(pairs,), in_specs=[part(0), part(1), part(2)...  37.9 us
  transfers between devices with their start and end apart: 122, of which 51 were waited for; matrix products, arithmetic and copies ran while one was open for 29% of the time, Pallas kernels for 12%

profile of v1, /device:TPU:1, one launch (start us, length us, event | category | flops | bytes accessed | tf_op | source)
XLA Modules:
  0.0 1031.6 jit_solution(6657621838301919458)
XLA Ops:
  22.6 12.5 %collective-permute-done.4 = bf16[64,3072]{1,0:T(8,128)(2,1)S(1)} collective-permute-done((bf16[64,3072]{1,0:T(8,128)(2,1)S(1)}, bf16[64,3072]{1,0:T(8,128)(2,1)S(1)}, u32[]{:S(2)}, u32[]{:S(2)}) %collective-permute-start.4) | collective-permute-done | bytes 393248 | tf_op jit(solution)/shard_map/ppermute | solution.py:602
  38.1 10.1 collective-permute-done.1
  48.2 12.2 %collective-permute-done.33 = bf16[552,1024]{1,0:T(8,128)(2,1)} collective-permute-done((bf16[552,1024]{1,0:T(8,128)(2,1)}, bf16[552,1024]{1,0:T(8,128)(2,1)}, u32[]{:S(2)}, u32[]{:S(2)}) %collective-permute-start.33) | collective-permute-done | bytes 1130528 | tf_op jit(solution)/shard_map/ppermute | solution.py:605
  69.4 7.8 collective-permute-done.6.refs_1_
  81.6 6.0 collective-permute-start.22
  104.1 7.3 collective-permute-done.16
  115.5 9.4 fusion.30
  139.2 12.5 %collective-permute-done.23 = bf16[64,4096]{1,0:T(8,128)(2,1)S(1)} collective-permute-done((bf16[64,4096]{1,0:T(8,128)(2,1)S(1)}, bf16[64,4096]{1,0:T(8,128)(2,1)S(1)}, u32[]{:S(2)}, u32[]{:S(2)}) %collective-permute-start.23) | collective-permute-done | bytes 524320 | tf_op jit(solution)/shard_map/ppermute | solution.py:602
  158.6 19.0 %shard_map.298 = (bf16[1104,512]{1,0:T(8,128)(2,1)S(1)}, f32[4,2,1104]{2,1,0:T(2,128)S(1)}) custom-call(bf16[1104,1536]{1,0:T(8,128)(2,1)S(1)} %convolution_convert_fusion.1.query_ref.key_ref.value_ref, bf16[1104,1536]{1,0:T(8,128)(2,1)S(1)} %convolution_convert_fusion.1.query_ref.key_ref.value_ref, ...), custom_call_target="tpu_custom_call" | custom-call | flops 4992270336 | bytes 4521984 | tf_op jit(solution)/shard_map/pallas_call | solution.py:454
  187.5 17.6 %collective-permute-done.25.refs_1_ = bf16[128,4096]{1,0:T(8,128)(2,1)} collective-permute-done((bf16[128,4096]{1,0:T(8,128)(2,1)S(1)}, bf16[128,4096]{1,0:T(8,128)(2,1)}, u32[]{:S(2)}, u32[]{:S(2)}) %collective-permute-start.25) | collective-permute-done | bytes 1048608 | tf_op jit(solution)/shard_map/ppermute | solution.py:608
  215.8 13.0 %collective-permute-done.26.refs_0_ = bf16[128,4096]{1,0:T(8,128)(2,1)S(1)} collective-permute-done((bf16[128,4096]{1,0:T(8,128)(2,1)}, bf16[128,4096]{1,0:T(8,128)(2,1)S(1)}, u32[]{:S(2)}, u32[]{:S(2)}) %collective-permute-start.26) | collective-permute-done | bytes 1048608 | tf_op jit(solution)/shard_map/ppermute | solution.py:608
  233.4 6.7 collective-permute-start.35
  250.3 9.9 multiply_convert_fusion.1
  272.6 10.9 %collective-permute-done.36 = bf16[64,3072]{1,0:T(8,128)(2,1)} collective-permute-done((bf16[64,3072]{1,0:T(8,128)(2,1)S(1)}, bf16[64,3072]{1,0:T(8,128)(2,1)}, u32[]{:S(2)}, u32[]{:S(2)}) %collective-permute-start.36) | collective-permute-done | bytes 393248 | tf_op jit(solution)/shard_map/ppermute | solution.py:602
  290.1 13.4 %collective-permute-done.37.refs_2_ = bf16[128,3072]{1,0:T(8,128)(2,1)S(1)} collective-permute-done((bf16[128,3072]{1,0:T(8,128)(2,1)S(1)}, bf16[128,3072]{1,0:T(8,128)(2,1)S(1)}, u32[]{:S(2)}, u32[]{:S(2)}) %collective-permute-start.37) | collective-permute-done | bytes 786464 | tf_op jit(solution)/shard_map/ppermute | solution.py:608
  305.0 16.3 %collective-permute-done.38.refs_1_ = bf16[128,3072]{1,0:T(8,128)(2,1)S(1)} collective-permute-done((bf16[128,3072]{1,0:T(8,128)(2,1)S(1)}, bf16[128,3072]{1,0:T(8,128)(2,1)S(1)}, u32[]{:S(2)}, u32[]{:S(2)}) %collective-permute-start.38) | collective-permute-done | bytes 786464 | tf_op jit(solution)/shard_map/ppermute | solution.py:608
  322.8 15.4 %collective-permute-done.39.refs_0_ = bf16[128,3072]{1,0:T(8,128)(2,1)S(1)} collective-permute-done((bf16[128,3072]{1,0:T(8,128)(2,1)S(1)}, bf16[128,3072]{1,0:T(8,128)(2,1)S(1)}, u32[]{:S(2)}, u32[]{:S(2)}) %collective-permute-start.39) | collective-permute-done | bytes 786464 | tf_op jit(solution)/shard_map/ppermute | solution.py:608
  339.8 6.0 collective-permute-done.43.refs_7_
  363.5 6.3 collective-permute-done.49
  371.1 12.5 %collective-permute-done.50 = bf16[64,4096]{1,0:T(8,128)(2,1)S(1)} collective-permute-done((bf16[64,4096]{1,0:T(8,128)(2,1)S(1)}, bf16[64,4096]{1,0:T(8,128)(2,1)S(1)}, u32[]{:S(2)}, u32[]{:S(2)}) %collective-permute-start.50) | collective-permute-done | bytes 524320 | tf_op jit(solution)/shard_map/ppermute | solution.py:602
  390.3 19.0 %shard_map.301 = (bf16[1104,512]{1,0:T(8,128)(2,1)S(1)}, f32[4,2,1104]{2,1,0:T(2,128)S(1)}) custom-call(bf16[1104,1536]{1,0:T(8,128)(2,1)S(1)} %convolution_convert_fusion.query_ref.key_ref.value_ref, bf16[1104,1536]{1,0:T(8,128)(2,1)S(1)} %convolution_convert_fusion.query_ref.key_ref.value_ref, ...), custom_call_target="tpu_custom_call" | custom-call | flops 4992270336 | bytes 4521984 | tf_op jit(solution)/shard_map/pallas_call | solution.py:454
  420.6 16.3 %collective-permute-done.52.refs_1_ = bf16[128,4096]{1,0:T(8,128)(2,1)} collective-permute-done((bf16[128,4096]{1,0:T(8,128)(2,1)S(1)}, bf16[128,4096]{1,0:T(8,128)(2,1)}, u32[]{:S(2)}, u32[]{:S(2)}) %collective-permute-start.52) | collective-permute-done | bytes 1048608 | tf_op jit(solution)/shard_map/ppermute | solution.py:608
  446.7 14.0 %collective-permute-done.53.refs_0_ = bf16[128,4096]{1,0:T(8,128)(2,1)S(1)} collective-permute-done((bf16[128,4096]{1,0:T(8,128)(2,1)}, bf16[128,4096]{1,0:T(8,128)(2,1)S(1)}, u32[]{:S(2)}, u32[]{:S(2)}) %collective-permute-start.53) | collective-permute-done | bytes 1048608 | tf_op jit(solution)/shard_map/ppermute | solution.py:608
  477.0 9.3 multiply_convert_fusion
  486.3 10.8 %fusion.90 = (f32[2048]{0:T(1024)S(1)}, bf16[1104,2048]{1,0:T(8,128)(2,1)S(1)}) fusion(f32[1104,2048]{1,0:T(8,128)} %get-tuple-element.279, bf16[1024,2048]{1,0:T(8,128)(2,1)S(1)} %get-tuple-element.47, bf16[552,1024]{1,0:T(8,128)(2,1)S(1)} %collective-permute-done.62, bf16[552,1024]{1,0:T(8,128)(2,1)S(1)} %broadcast_select_fusion), kind=kOutput, calls=%fused_computation.442 | convolution fusion | flops 4664424448 | bytes 20029440 | tf_op jit(solution)/shard_map/dot_general | solution.py:926
  505.4 6.0 convolution_convert_fusion.2
  513.1 8.0 convolution_convert_fusion.3
  530.1 6.1 collective-permute-done.116
  542.4 6.1 collective-permute-start.60
  551.2 10.3 collective-permute-done.117
  571.4 37.2 %shard_map.303 = (bf16[1104,512]{1,0:T(8,128)(2,1)S(1)}, bf16[1104,512]{1,0:T(8,128)(2,1)S(1)}, bf16[1104,512]{1,0:T(8,128)(2,1)S(1)}) custom-call(bf16[1104,1536]{1,0:T(8,128)(2,1)} %copy-done.35, bf16[1104,1536]{1,0:T(8,128)(2,1)} %copy-done.35, bf16[1104,1536]{1,0:T(8,128)(2,1)} %copy-done.35, bf16[1104,512]{1,0:T(8,128)(2,1)S(1)} %copy-done.33, ...), custom_call_target="tpu_custom_call" | custom-call | flops 12480675840 | bytes 9043968 | tf_op jit(solution)/shard_map/pallas_call | solution.py:533
  641.7 16.5 %collective-permute-done.119 = bf16[128,4096]{1,0:T(8,128)(2,1)S(1)} collective-permute-done((bf16[128,4096]{1,0:T(8,128)(2,1)}, bf16[128,4096]{1,0:T(8,128)(2,1)S(1)}, u32[]{:S(2)}, u32[]{:S(2)}) %collective-permute-start.119) | collective-permute-done | bytes 1048608 | tf_op jit(solution)/shard_map/ppermute | solution.py:608
  671.4 10.8 %convolution_convert_fusion.8 = bf16[2048,512]{1,0:T(8,128)(2,1)S(1)} fusion(bf16[552,2048]{1,0:T(8,128)(2,1)S(1)} %copy-done.188, bf16[552,1024]{1,0:T(8,128)(2,1)S(1)} %copy-done.58, bf16[552,1024]{1,0:T(8,128)(2,1)S(1)} %copy-done.60, bf16[552,512]{1,0:T(8,128)(2,1)} %collective-permute-done.66, bf16[552,512]{1,0:T(8,128)(2,1)S(1)} %get-tuple-element.169), kind=kOutput, calls=%fused_computation.39 | convolution fusion | flops 2332131328 | bytes 7749632 | tf_op jit(solution)/shard_map/tc,te->ce/dot_general | solution.py:975
  700.4 11.1 %fusion.89 = (f32[2048]{0:T(1024)S(1)}, bf16[1104,2048]{1,0:T(8,128)(2,1)S(1)}) fusion(f32[1104,2048]{1,0:T(8,128)} %get-tuple-element.277, bf16[1024,2048]{1,0:T(8,128)(2,1)S(1)} %copy-done.13, bf16[552,1024]{1,0:T(8,128)(2,1)S(1)} %collective-permute-done.68, bf16[552,1024]{1,0:T(8,128)(2,1)S(1)} %get-tuple-element.107), kind=kOutput, calls=%fused_computation.441 | convolution fusion | flops 4664424448 | bytes 20029440 | tf_op jit(solution)/shard_map/dot_general | solution.py:926
  716.7 6.1 convolution_convert_fusion.4
  724.9 7.6 convolution_convert_fusion.5
  739.1 7.9 collective-permute-done.102
  756.0 6.6 collective-permute-done.107
  764.6 7.0 collective-permute-done.103
  777.8 37.4 %shard_map.304 = (bf16[1104,512]{1,0:T(8,128)(2,1)S(1)}, bf16[1104,512]{1,0:T(8,128)(2,1)S(1)}, bf16[1104,512]{1,0:T(8,128)(2,1)S(1)}) custom-call(bf16[1104,1536]{1,0:T(8,128)(2,1)} %copy-done.34, bf16[1104,1536]{1,0:T(8,128)(2,1)} %copy-done.34, bf16[1104,1536]{1,0:T(8,128)(2,1)} %copy-done.34, bf16[1104,512]{1,0:T(8,128)(2,1)S(1)} %copy-done.31, ...), custom_call_target="tpu_custom_call" | custom-call | flops 12480675840 | bytes 9043968 | tf_op jit(solution)/shard_map/pallas_call | solution.py:533
  848.1 16.0 %collective-permute-done.97 = f32[16,704]{1,0:T(8,128)S(1)} collective-permute-done((f32[16,704]{1,0:T(8,128)S(1)}, f32[16,704]{1,0:T(8,128)S(1)}, u32[]{:S(2)}, u32[]{:S(2)}) %collective-permute-start.97) | collective-permute-done | bytes 45088 | tf_op jit(solution)/shard_map/ppermute | solution.py:811
  866.8 14.4 %collective-permute-done.98 = f32[8,704]{1,0:T(8,128)S(1)} collective-permute-done((f32[8,704]{1,0:T(8,128)S(1)}, f32[8,704]{1,0:T(8,128)S(1)}, u32[]{:S(2)}, u32[]{:S(2)}) %collective-permute-start.98) | collective-permute-done | bytes 22560 | tf_op jit(solution)/shard_map/ppermute | solution.py:811
  924.6 10.9 %collective-permute-done.94 = bf16[128,3072]{1,0:T(8,128)(2,1)S(1)} collective-permute-done((bf16[128,3072]{1,0:T(8,128)(2,1)S(1)}, bf16[128,3072]{1,0:T(8,128)(2,1)S(1)}, u32[]{:S(2)}, u32[]{:S(2)}) %collective-permute-start.94) | collective-permute-done | bytes 786464 | tf_op jit(solution)/shard_map/ppermute | solution.py:608
  935.7 16.5 %collective-permute-done.82 = bf16[128,3072]{1,0:T(8,128)(2,1)S(1)} collective-permute-done((bf16[128,3072]{1,0:T(8,128)(2,1)S(1)}, bf16[128,3072]{1,0:T(8,128)(2,1)S(1)}, u32[]{:S(2)}, u32[]{:S(2)}) %collective-permute-start.82) | collective-permute-done | bytes 786464 | tf_op jit(solution)/shard_map/ppermute | solution.py:608
  955.2 14.3 %collective-permute-done.83 = bf16[128,3072]{1,0:T(8,128)(2,1)S(1)} collective-permute-done((bf16[128,3072]{1,0:T(8,128)(2,1)S(1)}, bf16[128,3072]{1,0:T(8,128)(2,1)S(1)}, u32[]{:S(2)}, u32[]{:S(2)}) %collective-permute-start.83) | collective-permute-done | bytes 786464 | tf_op jit(solution)/shard_map/ppermute | solution.py:608
  971.6 6.2 collective-permute-start.96
  996.1 6.7 collective-permute-done.85
  1021.1 7.5 collective-permute-done.74
  (897 shorter events, 444.1 us)
Async XLA Ops:
  9.8 26.9 %collective-permute-start = (bf16[552,1024]{1,0:T(8,128)(2,1)}, bf16[552,1024]{1,0:T(8,128)(2,1)}, u32[]{:S(2)}, u32[]{:S(2)}) collective-permute-start(bf16[552,1024]{1,0:T(8,128)(2,1)} %param.18), channel_id=1, source_target_pairs={{2,1},{1,2},{6,5},{5,6},{10,9},{9,10},{14,13},{13,14},{18,17},{17,... | collective-permute-start | bytes 3391496 | tf_op jit(solution)/shard_map/ppermute | solution.py:605
  17.0 31.2 %collective-permute-start.1 = (bf16[552,1024]{1,0:T(8,128)(2,1)}, bf16[552,1024]{1,0:T(8,128)(2,1)}, u32[]{:S(2)}, u32[]{:S(2)}) collective-permute-start(bf16[552,1024]{1,0:T(8,128)(2,1)} %get-tuple-element.161), channel_id=1, source_target_pairs={{2,1},{1,2},{6,5},{5,6},{10,9},{9,10},{14,13},{13,14},{18,17},{17,... | collective-permute-start | bytes 3391496 | tf_op jit(solution)/shard_map/ppermute | solution.py:605
  20.6 39.8 %collective-permute-start.33 = (bf16[552,1024]{1,0:T(8,128)(2,1)}, bf16[552,1024]{1,0:T(8,128)(2,1)}, u32[]{:S(2)}, u32[]{:S(2)}) collective-permute-start(bf16[552,1024]{1,0:T(8,128)(2,1)} %get-tuple-element.162), channel_id=1, source_target_pairs={{2,1},{1,2},{6,5},{5,6},{10,9},{9,10},{14,13},{13,14},{18,17},{17,... | collective-permute-start | bytes 3391496 | tf_op jit(solution)/shard_map/ppermute | solution.py:605
  35.2 28.1 %collective-permute-start.5 = (bf16[128,3072]{1,0:T(8,128)(2,1)S(1)}, bf16[128,3072]{1,0:T(8,128)(2,1)S(1)}, u32[]{:S(2)}, u32[]{:S(2)}) collective-permute-start(bf16[128,3072]{1,0:T(8,128)(2,1)S(1)} %maximum_select_fusion.4.refs_3_), channel_id=1, source_target_pairs={{0,8},{2,10},{8,16},{10,18},{16,24},{18,26},{24,28},{26,30},{28,20... | collective-permute-start | bytes 2359304 | tf_op jit(solution)/shard_map/ppermute | solution.py:608
  36.5 28.1 %collective-permute-start.8 = (bf16[128,3072]{1,0:T(8,128)(2,1)S(1)}, bf16[128,3072]{1,0:T(8,128)(2,1)S(1)}, u32[]{:S(2)}, u32[]{:S(2)}) collective-permute-start(bf16[128,3072]{1,0:T(8,128)(2,1)S(1)} %maximum_select_fusion.4.refs_3_), channel_id=1, source_target_pairs={{0,4},{2,6},{8,0},{10,2},{16,8},{18,10},{24,16},{26,18},{28,24},{3... | collective-permute-start | bytes 2359304 | tf_op jit(solution)/shard_map/ppermute | solution.py:608
  66.4 49.1 %collective-permute-start.2 = (bf16[552,2048]{1,0:T(8,128)(2,1)}, bf16[552,2048]{1,0:T(8,128)(2,1)}, u32[]{:S(2)}, u32[]{:S(2)}) collective-permute-start(bf16[552,2048]{1,0:T(8,128)(2,1)} %pad_maximum_fusion.2), channel_id=1, source_target_pairs={{0,2},{2,0},{4,6},{6,4},{8,10},{10,8},{12,14},{14,12},{16,18},{18,... | collective-permute-start | bytes 6782984 | tf_op jit(solution)/shard_map/ppermute | solution.py:599
  67.2 33.6 %collective-permute-start.14 = (bf16[1,8,128]{2,1,0:T(8,128)(2,1)S(1)}, bf16[1,8,128]{2,1,0:T(8,128)(2,1)S(1)}, u32[]{:S(2)}, u32[]{:S(2)}) collective-permute-start(bf16[1,8,128]{2,1,0:T(8,128)(2,1)S(1)} %pad_bitcast_fusion), channel_id=1, source_target_pairs={{0,1},{1,0},{2,3},{3,2},{4,5},{5,4},{6,7},{7,6},{8,9},{9,8},{10,11... | collective-permute-start | bytes 6152 | tf_op jit(solution)/shard_map/ppermute | solution.py:602
  77.2 23.7 %collective-permute-start.7 = (bf16[128,3072]{1,0:T(8,128)(2,1)}, bf16[128,3072]{1,0:T(8,128)(2,1)S(1)}, u32[]{:S(2)}, u32[]{:S(2)}) collective-permute-start(bf16[128,3072]{1,0:T(8,128)(2,1)} %collective-permute-done.6.refs_1_), channel_id=1, source_target_pairs={{0,8},{2,10},{8,16},{10,18},{16,24},{18,26},{24,28},{26,30},{28,20... | collective-permute-start | bytes 2359304 | tf_op jit(solution)/shard_map/ppermute | solution.py:608
  81.6 55.6 %collective-permute-start.22 = (bf16[64,4096]{1,0:T(8,128)(2,1)}, bf16[64,4096]{1,0:T(8,128)(2,1)}, u32[]{:S(2)}, u32[]{:S(2)}) collective-permute-start(bf16[64,4096]{1,0:T(8,128)(2,1)} %pad_maximum_fusion.41), channel_id=1, source_target_pairs={{2,1},{1,2},{6,5},{5,6},{10,9},{9,10},{14,13},{13,14},{18,17},{17,... | collective-permute-start | bytes 1572872 | tf_op jit(solution)/shard_map/ppermute | solution.py:605
  151.9 28.6 %collective-permute-start.24 = (bf16[128,4096]{1,0:T(8,128)(2,1)S(1)}, bf16[128,4096]{1,0:T(8,128)(2,1)S(1)}, u32[]{:S(2)}, u32[]{:S(2)}) collective-permute-start(bf16[128,4096]{1,0:T(8,128)(2,1)S(1)} %maximum_select_fusion.2.refs_3_), channel_id=1, source_target_pairs={{0,8},{2,10},{8,16},{10,18},{16,24},{18,26},{24,28},{26,30},{28,20... | collective-permute-start | bytes 3145736 | tf_op jit(solution)/shard_map/ppermute | solution.py:608
  152.0 30.8 %collective-permute-start.27 = (bf16[128,4096]{1,0:T(8,128)(2,1)S(1)}, bf16[128,4096]{1,0:T(8,128)(2,1)S(1)}, u32[]{:S(2)}, u32[]{:S(2)}) collective-permute-start(bf16[128,4096]{1,0:T(8,128)(2,1)S(1)} %maximum_select_fusion.2.refs_3_), channel_id=1, source_target_pairs={{0,4},{2,6},{8,0},{10,2},{16,8},{18,10},{24,16},{26,18},{28,24},{3... | collective-permute-start | bytes 3145736 | tf_op jit(solution)/shard_map/ppermute | solution.py:608
  180.3 27.4 %collective-permute-start.20 = (bf16[552,1024]{1,0:T(8,128)(2,1)}, bf16[552,1024]{1,0:T(8,128)(2,1)}, u32[]{:S(2)}, u32[]{:S(2)}) collective-permute-start(bf16[552,1024]{1,0:T(8,128)(2,1)} %slice.715), channel_id=1, source_target_pairs={{0,2},{2,0},{4,6},{6,4},{8,10},{10,8},{12,14},{14,12},{16,18},{18,... | collective-permute-start | bytes 3391496 | tf_op jit(solution)/shard_map/ppermute | solution.py:599
  180.6 24.6 %collective-permute-start.25 = (bf16[128,4096]{1,0:T(8,128)(2,1)S(1)}, bf16[128,4096]{1,0:T(8,128)(2,1)}, u32[]{:S(2)}, u32[]{:S(2)}) collective-permute-start(bf16[128,4096]{1,0:T(8,128)(2,1)S(1)} %collective-permute-done.24.refs_2_), channel_id=1, source_target_pairs={{0,8},{2,10},{8,16},{10,18},{16,24},{18,26},{24,28},{26,30},{28,20... | collective-permute-start | bytes 3145736 | tf_op jit(solution)/shard_map/ppermute | solution.py:608
  182.8 25.0 %collective-permute-start.28 = (bf16[128,4096]{1,0:T(8,128)(2,1)S(1)}, bf16[128,4096]{1,0:T(8,128)(2,1)}, u32[]{:S(2)}, u32[]{:S(2)}) collective-permute-start(bf16[128,4096]{1,0:T(8,128)(2,1)S(1)} %collective-permute-done.27.refs_4_), channel_id=1, source_target_pairs={{0,4},{2,6},{8,0},{10,2},{16,8},{18,10},{24,16},{26,18},{28,24},{3... | collective-permute-start | bytes 3145736 | tf_op jit(solution)/shard_map/ppermute | solution.py:608
  205.1 23.7 %collective-permute-start.26 = (bf16[128,4096]{1,0:T(8,128)(2,1)}, bf16[128,4096]{1,0:T(8,128)(2,1)S(1)}, u32[]{:S(2)}, u32[]{:S(2)}) collective-permute-start(bf16[128,4096]{1,0:T(8,128)(2,1)} %collective-permute-done.25.refs_1_), channel_id=1, source_target_pairs={{0,8},{2,10},{8,16},{10,18},{16,24},{18,26},{24,28},{26,30},{28,20... | collective-permute-start | bytes 3145736 | tf_op jit(solution)/shard_map/ppermute | solution.py:608
  207.8 23.9 %collective-permute-start.29 = (bf16[128,4096]{1,0:T(8,128)(2,1)}, bf16[128,4096]{1,0:T(8,128)(2,1)S(1)}, u32[]{:S(2)}, u32[]{:S(2)}) collective-permute-start(bf16[128,4096]{1,0:T(8,128)(2,1)} %collective-permute-done.28.refs_5_), channel_id=1, source_target_pairs={{0,4},{2,6},{8,0},{10,2},{16,8},{18,10},{24,16},{26,18},{28,24},{3... | collective-permute-start | bytes 3145736 | tf_op jit(solution)/shard_map/ppermute | solution.py:608
  214.3 35.9 %collective-permute-start.21 = (bf16[552,1024]{1,0:T(8,128)(2,1)}, bf16[552,1024]{1,0:T(8,128)(2,1)}, u32[]{:S(2)}, u32[]{:S(2)}) collective-permute-start(bf16[552,1024]{1,0:T(8,128)(2,1)} %add_convert_fusion.2), channel_id=1, source_target_pairs={{0,2},{2,0},{4,6},{6,4},{8,10},{10,8},{12,14},{14,12},{16,18},{18,... | collective-permute-start | bytes 3391496 | tf_op jit(solution)/shard_map/ppermute | solution.py:599
  233.4 37.6 %collective-permute-start.35 = (bf16[64,3072]{1,0:T(8,128)(2,1)}, bf16[64,3072]{1,0:T(8,128)(2,1)}, u32[]{:S(2)}, u32[]{:S(2)}) collective-permute-start(bf16[64,3072]{1,0:T(8,128)(2,1)} %pad_maximum_fusion.51), channel_id=1, source_target_pairs={{2,1},{1,2},{6,5},{5,6},{10,9},{9,10},{14,13},{13,14},{18,17},{17,... | collective-permute-start | bytes 1179656 | tf_op jit(solution)/shard_map/ppermute | solution.py:605
  289.1 60.5 %collective-permute-start.34 = (bf16[552,2048]{1,0:T(8,128)(2,1)S(1)}, bf16[552,2048]{1,0:T(8,128)(2,1)S(1)}, u32[]{:S(2)}, u32[]{:S(2)}) collective-permute-start(bf16[552,2048]{1,0:T(8,128)(2,1)S(1)} %pad_maximum_fusion.5), channel_id=1, source_target_pairs={{0,2},{2,0},{4,6},{6,4},{8,10},{10,8},{12,14},{14,12},{16,18},{18,... | collective-permute-start | bytes 6782984 | tf_op jit(solution)/shard_map/ppermute | solution.py:599
  383.8 28.5 %collective-permute-start.51 = (bf16[128,4096]{1,0:T(8,128)(2,1)S(1)}, bf16[128,4096]{1,0:T(8,128)(2,1)S(1)}, u32[]{:S(2)}, u32[]{:S(2)}) collective-permute-start(bf16[128,4096]{1,0:T(8,128)(2,1)S(1)} %maximum_select_fusion.3.refs_3_), channel_id=1, source_target_pairs={{0,8},{2,10},{8,16},{10,18},{16,24},{18,26},{24,28},{26,30},{28,20... | collective-permute-start | bytes 3145736 | tf_op jit(solution)/shard_map/ppermute | solution.py:608
  383.9 29.7 %collective-permute-start.54 = (bf16[128,4096]{1,0:T(8,128)(2,1)S(1)}, bf16[128,4096]{1,0:T(8,128)(2,1)S(1)}, u32[]{:S(2)}, u32[]{:S(2)}) collective-permute-start(bf16[128,4096]{1,0:T(8,128)(2,1)S(1)} %maximum_select_fusion.3.refs_3_), channel_id=1, source_target_pairs={{0,4},{2,6},{8,0},{10,2},{16,8},{18,10},{24,16},{26,18},{28,24},{3... | collective-permute-start | bytes 3145736 | tf_op jit(solution)/shard_map/ppermute | solution.py:608
  412.1 26.9 %collective-permute-start.47 = (bf16[552,1024]{1,0:T(8,128)(2,1)}, bf16[552,1024]{1,0:T(8,128)(2,1)}, u32[]{:S(2)}, u32[]{:S(2)}) collective-permute-start(bf16[552,1024]{1,0:T(8,128)(2,1)} %slice.713), channel_id=1, source_target_pairs={{0,2},{2,0},{4,6},{6,4},{8,10},{10,8},{12,14},{14,12},{16,18},{18,... | collective-permute-start | bytes 3391496 | tf_op jit(solution)/shard_map/ppermute | solution.py:599
  412.3 24.6 %collective-permute-start.52 = (bf16[128,4096]{1,0:T(8,128)(2,1)S(1)}, bf16[128,4096]{1,0:T(8,128)(2,1)}, u32[]{:S(2)}, u32[]{:S(2)}) collective-permute-start(bf16[128,4096]{1,0:T(8,128)(2,1)S(1)} %collective-permute-done.51.refs_2_), channel_id=1, source_target_pairs={{0,8},{2,10},{8,16},{10,18},{16,24},{18,26},{24,28},{26,30},{28,20... | collective-permute-start | bytes 3145736 | tf_op jit(solution)/shard_map/ppermute | solution.py:608
  413.5 24.4 %collective-permute-start.55 = (bf16[128,4096]{1,0:T(8,128)(2,1)S(1)}, bf16[128,4096]{1,0:T(8,128)(2,1)}, u32[]{:S(2)}, u32[]{:S(2)}) collective-permute-start(bf16[128,4096]{1,0:T(8,128)(2,1)S(1)} %collective-permute-done.54.refs_4_), channel_id=1, source_target_pairs={{0,4},{2,6},{8,0},{10,2},{16,8},{18,10},{24,16},{26,18},{28,24},{3... | collective-permute-start | bytes 3145736 | tf_op jit(solution)/shard_map/ppermute | solution.py:608
  415.8 53.5 %collective-permute-start.61 = (bf16[552,1024]{1,0:T(8,128)(2,1)}, bf16[552,1024]{1,0:T(8,128)(2,1)}, u32[]{:S(2)}, u32[]{:S(2)}) collective-permute-start(bf16[552,1024]{1,0:T(8,128)(2,1)} %param.33), channel_id=1, source_target_pairs={{2,1},{1,2},{6,5},{5,6},{10,9},{9,10},{14,13},{13,14},{18,17},{17,... | collective-permute-start | bytes 3391496 | tf_op jit(solution)/shard_map/ppermute | solution.py:605
  444.9 32.0 %collective-permute-start.48 = (bf16[552,1024]{1,0:T(8,128)(2,1)}, bf16[552,1024]{1,0:T(8,128)(2,1)}, u32[]{:S(2)}, u32[]{:S(2)}) collective-permute-start(bf16[552,1024]{1,0:T(8,128)(2,1)} %add_convert_fusion), channel_id=1, source_target_pairs={{0,2},{2,0},{4,6},{6,4},{8,10},{10,8},{12,14},{14,12},{16,18},{18,... | collective-permute-start | bytes 3391496 | tf_op jit(solution)/shard_map/ppermute | solution.py:599
  502.2 37.8 %collective-permute-start.63 = (bf16[552,1024]{1,0:T(8,128)(2,1)S(1)}, bf16[552,1024]{1,0:T(8,128)(2,1)S(1)}, u32[]{:S(2)}, u32[]{:S(2)}) collective-permute-start(bf16[552,1024]{1,0:T(8,128)(2,1)S(1)} %slice.711), channel_id=1, source_target_pairs={{0,2},{2,0},{4,6},{6,4},{8,10},{10,8},{12,14},{14,12},{16,18},{18,... | collective-permute-start | bytes 3391496 | tf_op jit(solution)/shard_map/ppermute | solution.py:599
  537.3 24.2 %collective-permute-start.117 = (bf16[128,4096]{1,0:T(8,128)(2,1)}, bf16[128,4096]{1,0:T(8,128)(2,1)}, u32[]{:S(2)}, u32[]{:S(2)}) collective-permute-start(bf16[128,4096]{1,0:T(8,128)(2,1)} %add_convert_fusion.6), channel_id=1, source_target_pairs={{0,4},{2,6},{8,0},{10,2},{16,8},{18,10},{24,16},{26,18},{28,24},{3... | collective-permute-start | bytes 3145736 | tf_op jit(solution)/shard_map/ppermute | solution.py:608
  539.9 25.8 %collective-permute-start.113 = (bf16[128,4096]{1,0:T(8,128)(2,1)}, bf16[128,4096]{1,0:T(8,128)(2,1)}, u32[]{:S(2)}, u32[]{:S(2)}) collective-permute-start(bf16[128,4096]{1,0:T(8,128)(2,1)} %add_convert_fusion.9), channel_id=1, source_target_pairs={{0,8},{2,10},{8,16},{10,18},{16,24},{18,26},{24,28},{26,30},{28,20... | collective-permute-start | bytes 3145736 | tf_op jit(solution)/shard_map/ppermute | solution.py:608
  542.4 78.5 %collective-permute-start.60 = (bf16[552,1024]{1,0:T(8,128)(2,1)S(1)}, bf16[552,1024]{1,0:T(8,128)(2,1)}, u32[]{:S(2)}, u32[]{:S(2)}) collective-permute-start(bf16[552,1024]{1,0:T(8,128)(2,1)S(1)} %get-tuple-element.158), channel_id=1, source_target_pairs={{2,1},{1,2},{6,5},{5,6},{10,9},{9,10},{14,13},{13,14},{18,17},{17,... | collective-permute-start | bytes 3391496 | tf_op jit(solution)/shard_map/ppermute | solution.py:605
  564.3 66.1 %collective-permute-start.118 = (bf16[128,4096]{1,0:T(8,128)(2,1)}, bf16[128,4096]{1,0:T(8,128)(2,1)}, u32[]{:S(2)}, u32[]{:S(2)}) collective-permute-start(bf16[128,4096]{1,0:T(8,128)(2,1)} %add_convert_fusion.5), channel_id=1, source_target_pairs={{0,4},{2,6},{8,0},{10,2},{16,8},{18,10},{24,16},{26,18},{28,24},{3... | collective-permute-start | bytes 3145736 | tf_op jit(solution)/shard_map/ppermute | solution.py:608
  568.2 66.2 %collective-permute-start.114 = (bf16[128,4096]{1,0:T(8,128)(2,1)}, bf16[128,4096]{1,0:T(8,128)(2,1)}, u32[]{:S(2)}, u32[]{:S(2)}) collective-permute-start(bf16[128,4096]{1,0:T(8,128)(2,1)} %add_convert_fusion.8), channel_id=1, source_target_pairs={{0,8},{2,10},{8,16},{10,18},{16,24},{18,26},{24,28},{26,30},{28,20... | collective-permute-start | bytes 3145736 | tf_op jit(solution)/shard_map/ppermute | solution.py:608
  632.9 25.3 %collective-permute-start.119 = (bf16[128,4096]{1,0:T(8,128)(2,1)}, bf16[128,4096]{1,0:T(8,128)(2,1)S(1)}, u32[]{:S(2)}, u32[]{:S(2)}) collective-permute-start(bf16[128,4096]{1,0:T(8,128)(2,1)} %add_convert_fusion.4), channel_id=1, source_target_pairs={{0,4},{2,6},{8,0},{10,2},{16,8},{18,10},{24,16},{26,18},{28,24},{3... | collective-permute-start | bytes 3145736 | tf_op jit(solution)/shard_map/ppermute | solution.py:608
  636.8 25.8 %collective-permute-start.115 = (bf16[128,4096]{1,0:T(8,128)(2,1)}, bf16[128,4096]{1,0:T(8,128)(2,1)}, u32[]{:S(2)}, u32[]{:S(2)}) collective-permute-start(bf16[128,4096]{1,0:T(8,128)(2,1)} %add_convert_fusion.7), channel_id=1, source_target_pairs={{0,8},{2,10},{8,16},{10,18},{16,24},{18,26},{24,28},{26,30},{28,20... | collective-permute-start | bytes 3145736 | tf_op jit(solution)/shard_map/ppermute | solution.py:608
  640.7 23.8 %collective-permute-start.66 = (bf16[552,512]{1,0:T(8,128)(2,1)S(1)}, bf16[552,512]{1,0:T(8,128)(2,1)}, u32[]{:S(2)}, u32[]{:S(2)}) collective-permute-start(bf16[552,512]{1,0:T(8,128)(2,1)S(1)} %get-tuple-element.170), channel_id=1, source_target_pairs={{0,2},{2,0},{4,6},{6,4},{8,10},{10,8},{12,14},{14,12},{16,18},{18,... | collective-permute-start | bytes 1695752 | tf_op jit(solution)/shard_map/ppermute | solution.py:599
  696.9 38.5 %collective-permute-start.76 = (bf16[552,1024]{1,0:T(8,128)(2,1)S(1)}, bf16[552,1024]{1,0:T(8,128)(2,1)S(1)}, u32[]{:S(2)}, u32[]{:S(2)}) collective-permute-start(bf16[552,1024]{1,0:T(8,128)(2,1)S(1)} %get-tuple-element.106), channel_id=1, source_target_pairs={{2,1},{1,2},{6,5},{5,6},{10,9},{9,10},{14,13},{13,14},{18,17},{17,... | collective-permute-start | bytes 3391496 | tf_op jit(solution)/shard_map/ppermute | solution.py:605
  716.6 32.8 %collective-permute-start.69 = (bf16[552,1024]{1,0:T(8,128)(2,1)S(1)}, bf16[552,1024]{1,0:T(8,128)(2,1)S(1)}, u32[]{:S(2)}, u32[]{:S(2)}) collective-permute-start(bf16[552,1024]{1,0:T(8,128)(2,1)S(1)} %slice.709), channel_id=1, source_target_pairs={{0,2},{2,0},{4,6},{6,4},{8,10},{10,8},{12,14},{14,12},{16,18},{18,... | collective-permute-start | bytes 3391496 | tf_op jit(solution)/shard_map/ppermute | solution.py:599
  764.3 72.9 %collective-permute-start.108 = (bf16[128,4096]{1,0:T(8,128)(2,1)S(1)}, bf16[128,4096]{1,0:T(8,128)(2,1)S(1)}, u32[]{:S(2)}, u32[]{:S(2)}) collective-permute-start(bf16[128,4096]{1,0:T(8,128)(2,1)S(1)} %add_convert_fusion.11), channel_id=1, source_target_pairs={{0,4},{2,6},{8,0},{10,2},{16,8},{18,10},{24,16},{26,18},{28,24},{3... | collective-permute-start | bytes 3145736 | tf_op jit(solution)/shard_map/ppermute | solution.py:608
  773.1 65.7 %collective-permute-start.104 = (bf16[128,4096]{1,0:T(8,128)(2,1)S(1)}, bf16[128,4096]{1,0:T(8,128)(2,1)S(1)}, u32[]{:S(2)}, u32[]{:S(2)}) collective-permute-start(bf16[128,4096]{1,0:T(8,128)(2,1)S(1)} %add_convert_fusion.14), channel_id=1, source_target_pairs={{0,8},{2,10},{8,16},{10,18},{16,24},{18,26},{24,28},{26,30},{28,20... | collective-permute-start | bytes 3145736 | tf_op jit(solution)/shard_map/ppermute | solution.py:608
  829.5 34.7 %collective-permute-start.87 = (bf16[128,1536]{1,0:T(8,128)(2,1)}, bf16[128,1536]{1,0:T(8,128)(2,1)}, u32[]{:S(2)}, u32[]{:S(2)}) collective-permute-start(bf16[128,1536]{1,0:T(8,128)(2,1)} %get-tuple-element.235), channel_id=1, source_target_pairs={{0,8},{2,10},{8,16},{10,18},{16,24},{18,26},{24,28},{26,30},{28,20... | collective-permute-start | bytes 1179656 | tf_op jit(solution)/shard_map/ppermute | solution.py:608
  838.5 55.6 %collective-permute-start.109 = (bf16[128,4096]{1,0:T(8,128)(2,1)}, bf16[128,4096]{1,0:T(8,128)(2,1)}, u32[]{:S(2)}, u32[]{:S(2)}) collective-permute-start(bf16[128,4096]{1,0:T(8,128)(2,1)} %add_convert_fusion.10), channel_id=1, source_target_pairs={{0,4},{2,6},{8,0},{10,2},{16,8},{18,10},{24,16},{26,18},{28,24},{3... | collective-permute-start | bytes 3145736 | tf_op jit(solution)/shard_map/ppermute | solution.py:608
  840.0 54.1 %collective-permute-start.105 = (bf16[128,4096]{1,0:T(8,128)(2,1)}, bf16[128,4096]{1,0:T(8,128)(2,1)}, u32[]{:S(2)}, u32[]{:S(2)}) collective-permute-start(bf16[128,4096]{1,0:T(8,128)(2,1)} %add_convert_fusion.13), channel_id=1, source_target_pairs={{0,8},{2,10},{8,16},{10,18},{16,24},{18,26},{24,28},{26,30},{28,20... | collective-permute-start | bytes 3145736 | tf_op jit(solution)/shard_map/ppermute | solution.py:608
  847.9 38.7 %collective-permute-start.92 = (bf16[128,3072]{1,0:T(8,128)(2,1)S(1)}, bf16[128,3072]{1,0:T(8,128)(2,1)S(1)}, u32[]{:S(2)}, u32[]{:S(2)}) collective-permute-start(bf16[128,3072]{1,0:T(8,128)(2,1)S(1)} %add_convert_fusion.18), channel_id=1, source_target_pairs={{0,4},{2,6},{8,0},{10,2},{16,8},{18,10},{24,16},{26,18},{28,24},{3... | collective-permute-start | bytes 2359304 | tf_op jit(solution)/shard_map/ppermute | solution.py:608
  890.7 24.7 %collective-permute-start.89 = (bf16[128,3072]{1,0:T(8,128)(2,1)}, bf16[128,3072]{1,0:T(8,128)(2,1)}, u32[]{:S(2)}, u32[]{:S(2)}) collective-permute-start(bf16[128,3072]{1,0:T(8,128)(2,1)} %add_convert_fusion.20), channel_id=1, source_target_pairs={{0,8},{2,10},{8,16},{10,18},{16,24},{18,26},{24,28},{26,30},{28,20... | collective-permute-start | bytes 2359304 | tf_op jit(solution)/shard_map/ppermute | solution.py:608
  901.0 76.8 %collective-permute-start.73 = (bf16[552,2048]{1,0:T(8,128)(2,1)S(1)}, bf16[552,2048]{1,0:T(8,128)(2,1)S(1)}, u32[]{:S(2)}, u32[]{:S(2)}) collective-permute-start(bf16[552,2048]{1,0:T(8,128)(2,1)S(1)} %slice.705), channel_id=1, source_target_pairs={{0,2},{2,0},{4,6},{6,4},{8,10},{10,8},{12,14},{14,12},{16,18},{18,... | collective-permute-start | bytes 6782984 | tf_op jit(solution)/shard_map/ppermute | solution.py:599
  918.7 33.5 %collective-permute-start.82 = (bf16[128,3072]{1,0:T(8,128)(2,1)S(1)}, bf16[128,3072]{1,0:T(8,128)(2,1)S(1)}, u32[]{:S(2)}, u32[]{:S(2)}) collective-permute-start(bf16[128,3072]{1,0:T(8,128)(2,1)S(1)} %add_convert_fusion.24), channel_id=1, source_target_pairs={{0,4},{2,6},{8,0},{10,2},{16,8},{18,10},{24,16},{26,18},{28,24},{3... | collective-permute-start | bytes 2359304 | tf_op jit(solution)/shard_map/ppermute | solution.py:608
  922.2 30.7 %collective-permute-start.78 = (bf16[128,3072]{1,0:T(8,128)(2,1)S(1)}, bf16[128,3072]{1,0:T(8,128)(2,1)S(1)}, u32[]{:S(2)}, u32[]{:S(2)}) collective-permute-start(bf16[128,3072]{1,0:T(8,128)(2,1)S(1)} %add_convert_fusion.27), channel_id=1, source_target_pairs={{0,8},{2,10},{8,16},{10,18},{16,24},{18,26},{24,28},{26,30},{28,20... | collective-permute-start | bytes 2359304 | tf_op jit(solution)/shard_map/ppermute | solution.py:608
  979.7 29.1 %collective-permute-start.75 = (bf16[552,1024]{1,0:T(8,128)(2,1)}, bf16[552,1024]{1,0:T(8,128)(2,1)}, u32[]{:S(2)}, u32[]{:S(2)}) collective-permute-start(bf16[552,1024]{1,0:T(8,128)(2,1)} %slice.529), channel_id=1, source_target_pairs={{2,1},{1,2},{6,5},{5,6},{10,9},{9,10},{14,13},{13,14},{18,17},{17,... | collective-permute-start | bytes 3391496 | tf_op jit(solution)/shard_map/ppermute | solution.py:605
  (278 other events, 2957.1 us)

commit v2 on v0

--- a/solution.py
+++ b/solution.py
@@ -1,6 +1,8 @@
 import jax
 import jax.numpy as jnp
 from jax import lax
+from jax.experimental import pallas as pl
+from jax.experimental.pallas import tpu as pltpu
 from jax.sharding import PartitionSpec as P
 
 HEAD_DIM = 64
@@ -93,7 +95,7 @@
     return stacked.reshape(SEQ_LEN, 3, head_count * HEAD_DIM).astype(jnp.bfloat16)
 
 
-def body(
+def general_body(
     inputs,
     skip_inputs,
     skip_weight,
@@ -385,6 +387,1034 @@
     )
 
 
+BOTH = ("fsdp", "tp")
+GAUSS = 0.3989422804014327
+
+
+def choose_body(mesh):
+    fsdp_size, tp_size = (mesh.shape["fsdp"], mesh.shape["tp"])
+    if tp_size != 2 or fsdp_size < 4 or fsdp_size & (fsdp_size - 1):
+        return general_body
+    return lambda *arrays: fast_body(fsdp_size, *arrays)
+
+
+class Sequence:
+    def __init__(self):
+        self.last = None
+
+    def at(self, value):
+        if self.last is None:
+            return value
+        return lax.optimization_barrier((value, self.last))[0]
+
+    def mark(self, value):
+        self.last = value
+        return value
+
+
+class RingGather:
+    def __init__(self, net, block):
+        self.net, self.round = (net, 0)
+        self.blocks = {0: block}
+        self.ahead, self.behind = (block, block)
+        self.send()
+
+    def send(self):
+        ahead, behind = (self.ahead, self.behind)
+        if self.round + 1 == self.net.half_ring:
+            middle = ahead.shape[1] // 256 * 128
+            ahead, behind = (ahead[:, :middle], behind[:, middle:])
+        self.coming = (self.net.along_ring(ahead, 1), self.net.along_ring(behind, -1))
+
+    def advance(self, sequence):
+        got = sequence.mark(sequence.at(self.coming))
+        self.round += 1
+        if self.round == self.net.half_ring:
+            self.blocks[self.round] = got
+            return
+        self.ahead, self.behind = got
+        self.blocks[-self.round], self.blocks[self.round] = got
+        self.send()
+
+    def whole(self, pieces):
+        net, offsets = (self.net, sorted(self.blocks))
+        operands, jobs = ([], [])
+        pair_rows = self.blocks[0].shape[0]
+        half_rows = pair_rows // 2
+        shapes = [(net.chips * pair_rows * slabs, width) for begin, width, slabs in pieces]
+        for at, offset in enumerate(offsets):
+            held = self.blocks[offset]
+            start = 0
+            for part in held if isinstance(held, tuple) else (held,):
+                stop = start + part.shape[1]
+                for which, (begin, width, slabs) in enumerate(pieces):
+                    for slab in range(slabs):
+                        low = max(start, begin + slab * width)
+                        high = min(stop, begin + (slab + 1) * width)
+                        if low >= high:
+                            continue
+                        to = low - begin - slab * width
+                        spans = [(0, pair_rows, 0)]
+                        if slabs > 1:
+                            spans = [
+                                (i * half_rows, half_rows, (i * slabs + slab) * half_rows)
+                                for i in range(2)
+                            ]
+                        for row, rows, to_row in spans:
+                            jobs.append(
+                                (len(operands), row, rows, low - start, high - low, which, at)
+                                + (pair_rows * slabs, to_row, to)
+                            )
+                operands.append(part)
+                start = stop
+        table = [
+            [net.order[(net.order.index(q) + offset) % net.chips] for offset in offsets]
+            for q in range(net.chips)
+        ]
+        places = lax.dynamic_index_in_dim(jnp.asarray(table, jnp.int32), net.chip, 0, False)
+        return copy_kernel(places, operands, jobs, shapes)
+
+
+class RingSum:
+    def __init__(self, net, tensors, columns_first):
+        self.net, self.columns_first = (net, columns_first)
+        self.views = [t.reshape(net.chips, 2, -1, t.shape[1]) for t in tensors]
+        if columns_first:
+            self.stage = "columns"
+            self.coming = [
+                net.to_column(lax.dynamic_index_in_dim(v, 1 - net.column, 1, False))
+                for v in self.views
+            ]
+        else:
+            self.views = [v.reshape(net.chips, -1, v.shape[3]) for v in self.views]
+            self.begin()
+
+    def block(self, offset):
+        at = self.net.chip_at(offset)
+        parts = [lax.dynamic_index_in_dim(v, at, 0, False) for v in self.views]
+        return jnp.concatenate(parts, 1)
+
+    def begin(self):
+        self.stage, self.distance = ("ring", self.net.half_ring)
+        far = self.block(self.net.half_ring)
+        middle = far.shape[1] // 256 * 128
+        self.coming = (
+            self.net.along_ring(far[:, :middle], 1),
+            self.net.along_ring(far[:, middle:], -1),
+        )
+
+    def advance(self, sequence):
+        net, got = (self.net, sequence.at(self.coming))
+        if self.stage == "columns":
+            self.views = [
+                (
+                    lax.dynamic_index_in_dim(v, net.column, 1, False).astype(jnp.float32)
+                    + other.astype(jnp.float32)
+                ).astype(jnp.bfloat16)
+                for v, other in zip(self.views, got)
+            ]
+            sequence.mark(self.views)
+            self.begin()
+            return
+        if self.stage == "last":
+            total = self.keep + got.astype(jnp.float32)
+            self.total = sequence.mark(total.astype(jnp.bfloat16))
+            return
+        ahead, behind = got
+        if self.distance == net.half_ring:
+            low, high = (ahead, behind)
+            ahead = jnp.concatenate([low, jnp.zeros(high.shape, low.dtype)], 1)
+            behind = jnp.concatenate([jnp.zeros(low.shape, low.dtype), high], 1)
+        ahead, behind = (ahead.astype(jnp.float32), behind.astype(jnp.float32))
+        self.distance -= 1
+        if self.distance:
+            ahead = (self.block(self.distance).astype(jnp.float32) + ahead).astype(jnp.bfloat16)
+            behind = (self.block(-self.distance).astype(jnp.float32) + behind).astype(jnp.bfloat16)
+            sequence.mark((ahead, behind))
+            self.coming = (net.along_ring(ahead, 1), net.along_ring(behind, -1))
+            return
+        total = self.block(0).astype(jnp.float32) + ahead + behind
+        if self.columns_first:
+            self.total = sequence.mark(total.astype(jnp.bfloat16))
+            return
+        half_rows = total.shape[0] // 2
+        self.keep = lax.dynamic_slice_in_dim(total, net.column * half_rows, half_rows, 0)
+        send = lax.dynamic_slice_in_dim(total, (1 - net.column) * half_rows, half_rows, 0)
+        send = sequence.mark(send.astype(jnp.bfloat16))
+        self.stage, self.coming = ("last", net.to_column(send))
+
+
+class HalvingSum:
+    def __init__(self, net, tensors, bits):
+        self.net, self.bits, self.round = (net, bits, 0)
+        count = len(bits)
+        self.views = [t.reshape((2,) * count + (-1, t.shape[1])) for t in tensors]
+        self.left = list(reversed(range(count)))
+        self.cut()
+
+    def cut(self):
+        bit = self.bits[self.round]
+        axis = self.left.index(bit)
+        self.left.remove(bit)
+        side = self.net.side(bit)
+
+        def half(which):
+            parts = [lax.dynamic_index_in_dim(v, which, axis, False) for v in self.views]
+            return jnp.concatenate(parts, -1)
+
+        self.keep = half(side)
+        self.coming = self.net.to_partner(half(1 - side), bit)
+
+    def advance(self, sequence):
+        got = sequence.at(self.coming)
+        total = self.keep.astype(jnp.float32) + got.astype(jnp.float32)
+        self.round += 1
+        self.total = sequence.mark(total.astype(jnp.bfloat16))
+        if self.round < len(self.bits):
+            self.views = [self.total]
+            self.cut()
+
+
+class Swap:
+    def __init__(self, net, tensors):
+        self.net, self.tensors = (net, tensors)
+        self.coming = [net.diagonal_other(value) for value in tensors]
+
+    def advance(self, sequence):
+        self.coming = sequence.mark(sequence.at(self.coming))
+
+
+class CoreNetwork:
+    def __init__(self, fsdp_size):
+        self.chips = fsdp_size // 2
+        self.core = lax.axis_index("fsdp") % 2
+        self.chip = lax.axis_index("fsdp") // 2
+        self.column = lax.axis_index("tp")
+        self.bits = self.chips.bit_length()
+        half = self.chips // 2
+        self.half_ring = half
+        self.order = [2 * i for i in range(half)] + [2 * i + 1 for i in reversed(range(half))]
+        table = [
+            [self.order[(self.order.index(q) + offset) % self.chips] for offset in range(self.chips)]
+            for q in range(self.chips)
+        ]
+        self.chips_here = lax.dynamic_index_in_dim(
+            jnp.asarray(table, jnp.int32), self.chip, 0, False
+        )
+        self.ring_pairs = {}
+        for step in (1, -1):
+            self.ring_pairs[step] = [
+                (self.order[i] * 2 + c, self.order[(i + step) % self.chips] * 2 + c)
+                for i in range(self.chips)
+                for c in range(2)
+            ]
+        self.core_pairs = [(i, i ^ 1) for i in range(fsdp_size)]
+        self.diagonal_pairs = []
+        for q in range(self.chips):
+            one, two = (q * 4 + 2, q * 4 + 1)
+            self.diagonal_pairs += [(one, two), (two, one)]
+
+    def to_core(self, value):
+        return lax.ppermute(value, "fsdp", self.core_pairs)
+
+    def chip_at(self, offset):
+        return self.chips_here[offset % self.chips]
+
+    def along_ring(self, value, step):
+        return lax.ppermute(value, "fsdp", self.ring_pairs[step])
+
+    def to_column(self, value):
+        return self.to_partner(value, 0)
+
+    def diagonal_other(self, value):
+        return lax.ppermute(value, BOTH, self.diagonal_pairs)
+
+    def choose(self, own, other):
+        return jnp.where(self.core == self.column, own, other)
+
+    def diagonal(self, value):
+        return self.choose(value, self.diagonal_other(value))
+
+    def to_partner(self, value, bit):
+        if bit == 0:
+            return lax.ppermute(value, "tp", [(0, 1), (1, 0)])
+        flip = 1 << (bit - 1)
+        pairs = [(q * 2 + c, (q ^ flip) * 2 + c) for q in range(self.chips) for c in range(2)]
+        return lax.ppermute(value, "fsdp", pairs)
+
+    def side(self, bit):
+        return self.column if bit == 0 else (self.chip >> (bit - 1)) & 1
+
+    def sum_small(self, packed):
+        for bit in reversed(range(self.bits + 1)):
+            count = packed.shape[0] // 2
+            if bit == 1:
+                side, send_to = (self.core, self.to_core)
+            else:
+                wire = max(bit - 1, 0)
+                side = self.side(wire)
+                send_to = lambda value, wire=wire: self.to_partner(value, wire)
+            keep = jnp.where(side == 0, packed[:count], packed[count:])
+            send = jnp.where(side == 0, packed[count:], packed[:count])
+            packed = keep + send_to(send)
+        return packed[0]
+
+
+def copy_kernel(places, operands, jobs, shapes):
+    def kernel(at_ref, *refs):
+        sources, targets = (refs[: len(operands)], refs[len(operands) :][: len(shapes)])
+        buffers = refs[len(operands) + len(shapes) : -2]
+        sems, out_sems = refs[-2:]
+        copies = [[] for _ in shapes]
+        for which in range(len(shapes)):
+            for index, job in enumerate(jobs):
+                source, row, rows, col, width, target, at, scale, offset, to = job
+                if target != which:
+                    continue
+                begin = pl.multiple_of(at_ref[at] * scale + offset, 16)
+                copy = pltpu.make_async_copy(
+                    sources[source].at[pl.ds(row, rows), pl.ds(col, width)],
+                    buffers[which].at[pl.ds(begin, rows), pl.ds(to, width)],
+                    sems.at[index],
+                )
+                copy.start()
+                copies[which].append(copy)
+        outs = []
+        for which in range(len(shapes)):
+            for copy in copies[which]:
+                copy.wait()
+            out = pltpu.make_async_copy(buffers[which], targets[which], out_sems.at[which])
+            out.start()
+            outs.append(out)
+        for out in outs:
+            out.wait()
+
+    moved = sum(2 * 2 * r * w for r, w in shapes)
+    return pl.pallas_call(
+        kernel,
+        out_shape=[jax.ShapeDtypeStruct(shape, jnp.bfloat16) for shape in shapes],
+        in_specs=[pl.BlockSpec(memory_space=pltpu.SMEM)]
+        + [pl.BlockSpec(memory_space=pl.ANY)] * len(operands),
+        out_specs=[pl.BlockSpec(memory_space=pl.ANY)] * len(shapes),
+        scratch_shapes=[pltpu.VMEM(shape, jnp.bfloat16) for shape in shapes]
+        + [pltpu.SemaphoreType.DMA((len(jobs),)), pltpu.SemaphoreType.DMA((len(shapes),))],
+        compiler_params=pltpu.CompilerParams(vmem_limit_bytes=24 << 20),
+        cost_estimate=pl.CostEstimate(flops=0, bytes_accessed=moved, transcendentals=0),
+    )(places, *operands)
+
+
+def row_chunks(count):
+    return [(begin, min(384, count - begin)) for begin in range(0, count, 384)]
+
+
+NT = (((1,), (1,)), ((), ()))
+TN = (((0,), (0,)), ((), ()))
+
+
+def head_lanes(value, head):
+    lane = lax.broadcasted_iota(jnp.int32, value.shape, 1)
+    return jnp.where((lane >= HEAD_DIM) == (head == 1), value, jnp.zeros_like(value))
+
+
+def attention_forward(triple):
+    tokens, width = (triple.shape[0], triple.shape[1] // 3)
+    pairs = width // (2 * HEAD_DIM)
+
+    def kernel(query_ref, key_ref, value_ref, out_ref, total_ref):
+        keys = key_ref[...]
+        values = value_ref[...]
+        for begin, rows in row_chunks(tokens):
+            query = query_ref[begin : begin + rows, :] * jnp.bfloat16(HEAD_DIM**-0.5)
+            mixed, totals = ([], [])
+            for head in range(2):
+                scores = lax.dot_general(
+                    head_lanes(query, head), keys, NT, preferred_element_type=jnp.float32
+                )
+                top = jnp.max(scores, -1, keepdims=True)
+                grown = jnp.exp(scores - top)
+                total = jnp.sum(grown, -1, keepdims=True)
+                mixed.append(
+                    jnp.dot(
+                        grown.astype(jnp.bfloat16), values, preferred_element_type=jnp.float32
+                    )
+                    / total
+                )
+                totals.append(top + jnp.log(total))
+            lane = lax.broadcasted_iota(jnp.int32, mixed[0].shape, 1)
+            out_ref[begin : begin + rows, :] = jnp.where(
+                lane < HEAD_DIM, mixed[0], mixed[1]
+            ).astype(jnp.bfloat16)
+            both = jnp.where(lane < HEAD_DIM, totals[0], totals[1]).T
+            total_ref[0, 0:1, begin : begin + rows] = both[0:1, :]
+            total_ref[0, 1:2, begin : begin + rows] = both[HEAD_DIM : HEAD_DIM + 1, :]
+
+    def part(index):
+        return pl.BlockSpec((tokens, 2 * HEAD_DIM), lambda i: (0, index * pairs + i))
+
+    return pl.pallas_call(
+        kernel,
+        grid=(pairs,),
+        in_specs=[part(0), part(1), part(2)],
+        out_specs=[part(0), pl.BlockSpec((1, 2, tokens), lambda i: (i, 0, 0))],
+        out_shape=[
+            jax.ShapeDtypeStruct((tokens, width), jnp.bfloat16),
+            jax.ShapeDtypeStruct((pairs, 2, tokens), jnp.float32),
+        ],
+        compiler_params=pltpu.CompilerParams(vmem_limit_bytes=48 << 20),
+        cost_estimate=pl.CostEstimate(
+            flops=16 * pairs * tokens * tokens * HEAD_DIM,
+            bytes_accessed=8 * tokens * width,
+            transcendentals=2 * pairs * tokens * tokens,
+        ),
+    )(triple, triple, triple)
+
+
+def attention_backward(triple, head_out, log_total, mixed_grad, first_pair, pair_count):
+    tokens, width = (triple.shape[0], triple.shape[1] // 3)
+    pairs = width // (2 * HEAD_DIM)
+    score_scale = HEAD_DIM**-0.5
+
+    def kernel(
+        query_ref, key_ref, value_ref, out_ref, total_ref, grad_ref, dq_ref, dk_ref, dv_ref, sum_ref
+    ):
+        query = query_ref[...] * jnp.bfloat16(score_scale)
+        grad = grad_ref[...]
+        product = grad.astype(jnp.float32) * out_ref[...].astype(jnp.float32)
+        ones = jnp.ones((8, 2 * HEAD_DIM), jnp.float32)
+        deltas = [
+            lax.dot_general(
+                head_lanes(ones, head),
+                product,
+                NT,
+                precision=lax.Precision.HIGHEST,
+                preferred_element_type=jnp.float32,
+            )[0:1, :]
+            for head in range(2)
+        ]
+        for begin, rows in row_chunks(tokens):
+            keys = key_ref[begin : begin + rows, :]
+            values = value_ref[begin : begin + rows, :]
+            key_grads, value_grads = ([], [])
+            for head in range(2):
+                keys_here = head_lanes(keys, head)
+                scores = lax.dot_general(
+                    keys_here, query, NT, preferred_element_type=jnp.float32
+                )
+                probs = jnp.exp(scores - total_ref[0, head : head + 1, :])
+                prob_grad = lax.dot_general(
+                    head_lanes(values, head), grad, NT, preferred_element_type=jnp.float32
+                )
+                score_grad = (probs * (prob_grad - deltas[head])).astype(jnp.bfloat16)
+                value_grads.append(
+                    jnp.dot(
+                        probs.astype(jnp.bfloat16), grad, preferred_element_type=jnp.float32
+                    )
+                )
+                key_grads.append(jnp.dot(score_grad, query, preferred_element_type=jnp.float32))
+                query_grad = lax.dot_general(
+                    score_grad, keys_here, TN, preferred_element_type=jnp.float32
+                )
+                if begin == 0 and head == 0:
+                    sum_ref[...] = query_grad
+                else:
+                    sum_ref[...] += query_grad
+            lane = lax.broadcasted_iota(jnp.int32, key_grads[0].shape, 1)
+            dk_ref[begin : begin + rows, :] = jnp.where(
+                lane < HEAD_DIM, key_grads[0], key_grads[1]
+            ).astype(jnp.bfloat16)
+            dv_ref[begin : begin + rows, :] = jnp.where(
+                lane < HEAD_DIM, value_grads[0], value_grads[1]
+            ).astype(jnp.bfloat16)
+        dq_ref[...] = (sum_ref[...] * score_scale).astype(jnp.bfloat16)
+
+    def part(index):
+        return pl.BlockSpec((tokens, 2 * HEAD_DIM), lambda i: (0, index * pairs + first_pair + i))
+
+    return pl.pallas_call(
+        kernel,
+        grid=(pair_count,),
+        in_specs=[
+            part(0),
+            part(1),
+            part(2),
+            part(0),
+            pl.BlockSpec((1, 2, tokens), lambda i: (first_pair + i, 0, 0)),
+            part(0),
+        ],
+        out_specs=[pl.BlockSpec((tokens, 2 * HEAD_DIM), lambda i: (0, i))] * 3,
+        out_shape=[jax.ShapeDtypeStruct((tokens, pair_count * 2 * HEAD_DIM), jnp.bfloat16)] * 3,
+        scratch_shapes=[pltpu.VMEM((tokens, 2 * HEAD_DIM), jnp.float32)],
+        compiler_params=pltpu.CompilerParams(vmem_limit_bytes=48 << 20),
+        cost_estimate=pl.CostEstimate(
+            flops=40 * pair_count * tokens * tokens * HEAD_DIM,
+            bytes_accessed=32 * tokens * pair_count * HEAD_DIM,
+            transcendentals=2 * pair_count * tokens * tokens,
+        ),
+    )(triple, triple, triple, head_out, log_total, mixed_grad)
+
+
+SWAPPED = ("w1", "u1", "i1", "s1")
+HALVED = {"u0": (1, 0, 2, 3), "w0": (2, 1, 0, 3)}
+PLAN = (
+    "+D0", "D0", "+P0", "+D1", "P0", "+R0", "D1", "+P1", "R0", "P1", "+R1", "+E", "R0", "+D2", "R1",
+    "D2", "+P2", "R0", "R1", "P2", "+P3", "R0", "+U0", "R1", "E", "R1", "+W0", "skip 0", "U0", "full 0",
+    "W0", "P3", "+L", "hid 0", "U0", "W0", "skip 1", "qkv 0", "U0", "attend 0", "W0", "L", "out 0", "U0",
+    "+U1", "second_norm 0", "W0", "+W1", "up 0", "U1", "down_held 0", "down 0", "W1", "full 1", "next 0",
+    "U1", "hid 1", "W1", "qkv 1", "U1", "attend 1", "W1", "out 1", "U1", "second_norm 1", "W1",
+    "grad_rows 1", "up 1", "down_grad 1", "+w1", "down_held 1", "act 1", "second 1", "up_grad 1", "+u1",
+    "middle 1", "mixed 1", "out_grad 1", "heads0 1", "w1", "heads1 1", "first 1", "qkv_grad 1", "+i1",
+    "u1", "wu", "hidden_grad 1", "joined 1", "grad_rows 0", "skip_grad 1", "act 0", "skip_sum 1", "+s1",
+    "second 0", "up_grad 0", "+u0", "i1", "down_grad 0", "+w0", "down 1", "middle 0", "next 1", "+O",
+    "mixed 0", "out_grad 0", "s1", "is", "heads0 0", "u0", "O", "+G1", "heads1 0", "w0", "first 0",
+    "qkv_grad 0", "+i0", "u0", "G1", "hidden_grad 0", "i0", "skip_grad 0", "w0", "skip_sum 0", "+s0",
+    "i0", "joined 0", "+G0", "u0", "s0", "i0", "w0", "s0", "i0", "u0", "s0", "i0", "w0", "s0", "G0", "s0",
+)
+
+
+def fast_body(
+    fsdp_size,
+    inputs,
+    skip_inputs,
+    skip_weight,
+    skip_bias,
+    first_gain,
+    first_shift,
+    attention_in,
+    attention_out,
+    out_bias,
+    second_gain,
+    second_shift,
+    up_weight,
+    up_bias,
+    down_weight,
+    down_bias,
+    cotangent,
+):
+    net = CoreNetwork(fsdp_size)
+    core, to_core, diagonal = (net.core, net.to_core, net.diagonal)
+    count, width = inputs.shape
+    shard_rows = attention_in.shape[1]
+    skip_rows, skip_width = skip_weight.shape[1:]
+    qkv_width = attention_in.shape[2] * attention_in.shape[3]
+    up_width = up_weight.shape[2]
+    down_width = down_weight.shape[1]
+    f32, low_type = (jnp.float32, jnp.bfloat16)
+
+    small_values = (
+        skip_bias,
+        first_gain,
+        first_shift,
+        out_bias,
+        second_gain,
+        second_shift,
+        up_bias,
+        down_bias,
+    )
+    small_widths = [value.shape[1] for value in small_values]
+    small_total = sum(small_widths) * LAYERS
+    small_lanes = -(-small_total // (128 * shard_rows)) * 128
+    packed_small = jnp.concatenate([value.reshape(-1) for value in small_values])
+    packed_small = jnp.pad(packed_small, (0, shard_rows * small_lanes - small_total))
+    packed_small = packed_small.reshape(shard_rows, small_lanes)
+    out_width = attention_out.shape[1]
+    slab_rows = skip_rows // shard_rows
+    first_width = slab_rows * skip_width + qkv_width + out_width
+    first_pieces = [
+        (0, skip_width, slab_rows),
+        (slab_rows * skip_width, qkv_width, 1),
+        (slab_rows * skip_width + qkv_width, out_width, 1),
+    ]
+
+    def first_pack(layer_index, more):
+        shard = skip_weight[layer_index].reshape(slab_rows, shard_rows, skip_width)
+        return jnp.concatenate(
+            [shard[i] for i in range(slab_rows)]
+            + [attention_in[layer_index].reshape(shard_rows, -1), attention_out[layer_index].T]
+            + more,
+            1,
+        )
+
+    def second_pack(layer_index):
+        return jnp.concatenate([up_weight[layer_index], down_weight[layer_index].T], 1)
+
+    sequence = Sequence()
+    sources = {
+        "D0": lambda: first_pack(0, [packed_small]),
+        "D2": lambda: second_pack(0),
+        "D1": lambda: jnp.concatenate([first_pack(1, []), second_pack(1)], 1),
+        "E": lambda: jnp.concatenate([inputs, skip_inputs[0]], 1),
+        "L": lambda: jnp.concatenate([skip_inputs[1], cotangent], 1),
+        "O": lambda: stream_lows[LAYERS],
+        "G1": lambda: grads[1]["skip_part"],
+        "G0": lambda: jnp.concatenate([grads[0]["input"], grads[0]["skip_part"]], 1),
+    }
+    moves, pairs, gathers, reduces, blocks, sums = ({}, {}, {}, {}, {}, {})
+
+    def moved(key, value):
+        blocks[key] = value
+        if key == "D0":
+            blocks["P0"] = value
+        elif key == "D2":
+            blocks["P2"] = value
+        elif key == "D1":
+            blocks["P1"] = value[:, :first_width]
+            blocks["P3"] = value[:, first_width:]
+
+    def paired(own, other):
+        return jnp.where(
+            net.column == 0,
+            jnp.concatenate([own, other], 0),
+            jnp.concatenate([other, own], 0),
+        )
+
+    def small_of(layer_index, all_small):
+        values, begin = ([], 0)
+        for size in small_widths:
+            values.append(
+                all_small[:, begin + layer_index * size : begin + (layer_index + 1) * size].reshape(
+                    -1
+                )
+            )
+            begin += LAYERS * size
+        values[6] = lax.dynamic_slice_in_dim(values[6], core * up_width, up_width)
+        return values
+
+    weights = [{}, {}]
+    smalls = [None, None]
+    kept = [{}, {}]
+    streams = [None] * (LAYERS + 1)
+    stream_lows = [None] * (LAYERS + 1)
+
+    def send(now, name, value):
+        now[name] = to_core(sequence.mark(value))
+
+    def received(now, name):
+        return sequence.at(now.pop(name))
+
+    def rows_with(own, other):
+        return jnp.concatenate([own, other], 0)
+
+    def skip_step(index):
+        held, now = (weights[index], kept[index])
+        if index == 0:
+            held["half"], held["qkv"], held["out"], small_here = gathers["R0"].whole(
+                first_pieces + [(first_width, small_lanes, 1)]
+            )
+            small_here = small_here.reshape(2 * net.chips, -1)
+            small_other = to_core(small_here)
+            all_small = jnp.where(
+                core == 0,
+                jnp.stack([small_here, small_other], 1),
+                jnp.stack([small_other, small_here], 1),
+            ).reshape(2 * fsdp_size, -1)
+            for layer_index in range(LAYERS):
+                smalls[layer_index] = small_of(layer_index, all_small)
+        else:
+            held["half"], held["qkv"], held["out"] = gathers["R1"].whole(first_pieces)
+        send(now, "skip_other", held["half"])
+
+    def in_columns(own, other):
+        return jnp.where(
+            core == 0, jnp.concatenate([own, other], 1), jnp.concatenate([other, own], 1)
+        )
+
+    def full_step(index):
+        held, other = (weights[index], received(kept[index], "skip_other"))
+        held["skip"] = sequence.mark(in_columns(held["half"], other))
+
+    def hid_step(index):
+        held, now, small = (weights[index], kept[index], smalls[index])
+        if index == 0:
+            stream_lows[0] = blocks["E"][:, :width]
+            streams[0] = stream_lows[0].astype(f32)
+            skip_here = blocks["E"][:, width:]
+        else:
+            skip_here = blocks["L"][:, :width]
+        now["joined"] = jnp.concatenate([sequence.at(stream_lows[index]), skip_here], 1)
+        part = jnp.dot(now["joined"], held["skip"], preferred_element_type=f32)
+        now["hidden"] = part + small[0]
+        now["first_norm"] = norm_apply(now["hidden"], small[1], small[2]).astype(low_type)
+        send(now, "first_other", now["first_norm"])
+
+    def qkv_step(index):
+        held, now = (weights[index], kept[index])
+        now["rows_first"] = rows_with(now["first_norm"], received(now, "first_other"))
+        now["triple"] = sequence.mark(
+            jnp.dot(now["rows_first"], held["qkv"], preferred_element_type=f32).astype(low_type)
+        )
+
+    def attend_step(index):
+        now = kept[index]
+        now["head_out"], now["log_total"] = attention_forward(sequence.at(now["triple"]))
+        sequence.mark(now["head_out"])
+
+    def out_step(index):
+        held, now = (weights[index], kept[index])
+        part = jnp.einsum(
+            "th,dh->td", sequence.at(now["head_out"]), held["out"], preferred_element_type=f32
+        )
+        now["mixed_own"] = part[:count]
+        send(now, "mixed_other", part[count:].astype(low_type))
+
+    def second_norm_step(index):
+        now, small = (kept[index], smalls[index])
+        branch = now["mixed_own"] + received(now, "mixed_other").astype(f32)
+        now["middle"] = now["hidden"] + branch + small[3]
+        now["second_norm"] = norm_apply(now["middle"], small[4], small[5]).astype(low_type)
+        send(now, "second_other", now["second_norm"])
+
+    def up_step(index):
+        held, now = (weights[index], kept[index])
+        held["up"] = gathers["U%d" % index].whole([(0, up_width, 1)])[0]
+        now["rows_second"] = rows_with(now["second_norm"], received(now, "second_other"))
+        preact = (
+            jnp.dot(now["rows_second"], held["up"], preferred_element_type=f32) + smalls[index][6]
+        )
+        below = 0.5 + 0.5 * lax.erf(preact * (0.5**0.5))
+        now["activated"] = (preact * below).astype(low_type)
+        now["slope"] = (below + preact * jnp.exp(-0.5 * preact * preact) * GAUSS).astype(low_type)
+        sequence.mark(now["activated"])
+
+    def down_held_step(index):
+        weights[index]["down"] = gathers["W%d" % index].whole([(0, down_width, 1)])[0]
+
+    def down_step(index):
+        now = kept[index]
+        part = jnp.einsum(
+            "tf,df->td",
+            sequence.at(now["activated"]),
+            weights[index]["down"],
+            preferred_element_type=f32,
+        )
+        now["branch_own"] = part[:count]
+        send(now, "branch_other", part[count:].astype(low_type))
+
+    def next_step(index):
+        now = kept[index]
+        branch = now["branch_own"] + received(now, "branch_other").astype(f32)
+        streams[index + 1] = now["middle"] + branch + smalls[index][7]
+        stream_lows[index + 1] = sequence.mark(streams[index + 1].astype(low_type))
+
+    grads = [{}, {}]
+    summed = {}
+
+    def grad_rows_step(index):
+        now = grads[index]
+        if index == LAYERS - 1:
+            now["stream_low"] = blocks["L"][:, width:]
+            now["stream"] = now["stream_low"].astype(f32)
+        else:
+            now["stream_low"] = now["stream"].astype(low_type)
+        now["down_bias"] = jnp.sum(now["stream"], 0)
+        send(now, "stream_other", now["stream_low"])
+
+    def grad_rows(index):
+        now = grads[index]
+        if "rows" not in now:
+            now["rows"] = rows_with(now["stream_low"], received(now, "stream_other"))
+            return now["rows"]
+        return sequence.at(now["rows"])
+
+    def down_grad_step(index):
+        now = grads[index]
+        now["down"] = sequence.mark(
+            jnp.einsum(
+                "td,tf->df",
+                grad_rows(index),
+                kept[index]["activated"],
+                preferred_element_type=f32,
+            ).astype(low_type)
+        )
+        sums["w%d" % index] = [now["down"]]
+
+    def act_step(index):
+        now = grads[index]
+        act_grad = jnp.dot(
+            grad_rows(index), weights[index]["down"], preferred_element_type=f32
+        )
+        pre_grad = act_grad * kept[index]["slope"]
+        now["up_bias"] = jnp.sum(pre_grad, 0)
+        now["pre_low"] = sequence.mark(pre_grad.astype(low_type))
+
+    def second_step(index):
+        now = grads[index]
+        part = jnp.einsum(
+            "tf,df->td",
+            sequence.at(now["pre_low"]),
+            weights[index]["up"],
+            preferred_element_type=f32,
+        )
+        now["second_own"] = part[:count]
+        send(now, "second_other", part[count:].astype(low_type))
+
+    def up_grad_step(index):
+        now = grads[index]
+        now["up"] = sequence.mark(
+            jnp.einsum(
+                "td,tf->df",
+                sequence.at(kept[index]["rows_second"]),
+                now["pre_low"],
+                preferred_element_type=f32,
+            ).astype(low_type)
+        )
+        sums["u%d" % index] = [now["up"]]
+
+    def middle_step(index):
+        now, small = (grads[index], smalls[index])
+        second_grad = now["second_own"] + received(now, "second_other").astype(f32)
+        unused, pull = jax.vjp(norm_apply, kept[index]["middle"], small[4], small[5])
+        norm_grad, now["second_gain"], now["second_shift"] = pull(second_grad)
+        now["middle"] = now["stream"] + norm_grad
+        now["out_bias"] = jnp.sum(now["middle"], 0)
+        now["middle_low"] = now["middle"].astype(low_type)
+        send(now, "middle_other", now["middle_low"])
+
+    def mixed_step(index):
+        now = grads[index]
+        now["middle_rows"] = rows_with(now["middle_low"], received(now, "middle_other"))
+        now["mixed"] = sequence.mark(
+            jnp.dot(
+                now["middle_rows"], weights[index]["out"], preferred_element_type=f32
+            ).astype(low_type)
+        )
+
+    def out_grad_step(index):
+        now = grads[index]
+        now["out"] = sequence.mark(
+            jnp.einsum(
+                "td,th->dh",
+                sequence.at(now["middle_rows"]),
+                kept[index]["head_out"],
+                preferred_element_type=f32,
+            ).astype(low_type)
+        )
+
+    def attend_grad_step(index, part):
+        now, old = (grads[index], kept[index])
+        pairs = old["log_total"].shape[0]
+        first, last = (pairs * part // 2, pairs * (part + 1) // 2)
+        now["heads%d" % part] = attention_backward(
+            old["triple"],
+            old["head_out"],
+            old["log_total"],
+            sequence.at(now["mixed"]),
+            first,
+            last - first,
+        )
+        sequence.mark(now["heads%d" % part][0])
+
+    def first_step(index):
+        now = grads[index]
+        now["triple"] = jnp.concatenate(
+            [part for both in zip(now["heads0"], now["heads1"]) for part in both], 1
+        )
+        part = jnp.einsum(
+            "tc,dc->td",
+            sequence.at(now["triple"]),
+            weights[index]["qkv"],
+            preferred_element_type=f32,
+        )
+        now["first_own"] = part[:count]
+        send(now, "first_other", part[count:].astype(low_type))
+
+    def qkv_grad_step(index):
+        now = grads[index]
+        now["qkv"] = sequence.mark(
+            jnp.einsum(
+                "td,tc->dc",
+                sequence.at(kept[index]["rows_first"]),
+                now["triple"],
+                preferred_element_type=f32,
+            ).astype(low_type)
+        )
+        sums["i%d" % index] = [now["qkv"], now["out"]]
+
+    def hidden_grad_step(index):
+        now, small = (grads[index], smalls[index])
+        first_grad = now["first_own"] + received(now, "first_other").astype(f32)
+        unused, pull = jax.vjp(norm_apply, kept[index]["hidden"], small[1], small[2])
+        norm_grad, now["first_gain"], now["first_shift"] = pull(first_grad)
+        hidden_grad = now["middle"] + norm_grad
+        now["skip_bias"] = jnp.sum(hidden_grad, 0)
+        now["hidden_low"] = sequence.mark(hidden_grad.astype(low_type))
+
+    def joined_step(index):
+        now = grads[index]
+        joined_grad = jnp.einsum(
+            "te,ce->tc",
+            sequence.at(now["hidden_low"]),
+            weights[index]["skip"],
+            preferred_element_type=f32,
+        )
+        now["skip_part"] = joined_grad[:, width:].astype(low_type)
+        before = joined_grad[:, :width]
+        if index:
+            grads[index - 1]["stream"] = before
+        else:
+            now["input"] = before.astype(low_type)
+        sequence.mark(now["skip_part"])
+
+    def skip_grad_step(index):
+        now = grads[index]
+        full = jnp.einsum(
+            "tc,te->ce",
+            kept[index]["joined"],
+            sequence.at(now["hidden_low"]),
+            preferred_element_type=f32,
+        ).astype(low_type)
+        now["skip_keep"] = lax.dynamic_slice_in_dim(full, core * skip_width, skip_width, 1)
+        send(
+            now,
+            "skip_other",
+            lax.dynamic_slice_in_dim(full, (1 - core) * skip_width, skip_width, 1),
+        )
+
+    def skip_sum_step(index):
+        now = grads[index]
+        other = received(now, "skip_other").astype(f32)
+        now["skip"] = sequence.mark((now["skip_keep"].astype(f32) + other).astype(low_type))
+        slabs = now["skip"].reshape(-1, slab_rows, shard_rows, skip_width)
+        sums["s%d" % index] = [
+            slabs[:, i].reshape(-1, skip_width) for i in range(slab_rows)
+        ]
+
+    steps = {
+        "skip": skip_step,
+        "full": full_step,
+        "hid": hid_step,
+        "qkv": qkv_step,
+        "attend": attend_step,
+        "out": out_step,
+        "second_norm": second_norm_step,
+        "up": up_step,
+        "down_held": down_held_step,
+        "down": down_step,
+        "next": next_step,
+        "grad_rows": grad_rows_step,
+        "down_grad": down_grad_step,
+        "act": act_step,
+        "second": second_step,
+        "up_grad": up_grad_step,
+        "middle": middle_step,
+        "out_grad": out_grad_step,
+        "mixed": mixed_step,
+        "heads0": lambda index: attend_grad_step(index, 0),
+        "heads1": lambda index: attend_grad_step(index, 1),
+        "first": first_step,
+        "qkv_grad": qkv_grad_step,
+        "hidden_grad": hidden_grad_step,
+        "joined": joined_step,
+        "skip_grad": skip_grad_step,
+        "skip_sum": skip_sum_step,
+    }
+
+    for item in PLAN:
+        key = item[1:]
+        if " " in item:
+            name, index = item.split()
+            steps[name](int(index))
+        elif item[0] == "+":
+            if key in sources:
+                own = sources[key]()
+                moves[key] = (own, net.diagonal_other(sequence.at(own)))
+            elif key[0] == "P":
+                pairs[key] = (blocks[key], net.to_column(sequence.at(blocks[key])))
+            elif key[0] in "RUW":
+                gathers[key] = RingGather(net, sequence.at(blocks[key]))
+            elif key in ("w1", "u1", "i1", "s1"):
+                reduces[key] = Swap(net, sequence.at(sums[key]))
+            else:
+                tensors = sequence.at(sums[key])
+                if key in HALVED:
+                    bits = [bit for bit in HALVED[key] if bit < net.bits]
+                    bits += range(len(bits), net.bits)
+                    reduces[key] = HalvingSum(net, tensors, bits)
+                else:
+                    reduces[key] = RingSum(net, tensors, False)
+        elif item in moves:
+            own, other = moves.pop(item)
+            moved(item, sequence.mark(net.choose(own, sequence.at(other))))
+        elif item in pairs:
+            own, other = pairs.pop(item)
+            other = sequence.at(other)
+            both = sequence.mark(paired(own, other))
+            if key in "01":
+                blocks["R" + key] = both
+            else:
+                layer = str(int(key) - 2)
+                blocks["U" + layer], blocks["W" + layer] = (both[:, :up_width], both[:, up_width:])
+        elif item in gathers:
+            gathers[item].advance(sequence)
+        elif item in reduces:
+            reduces[item].advance(sequence)
+        else:
+            chosen = [reduces[letter + "1"] for letter in item]
+            own = jnp.concatenate([v for swap in chosen for v in swap.tensors], 1)
+            other = sequence.at([v for swap in chosen for v in swap.coming])
+            operand = sequence.mark(net.choose(own, jnp.concatenate(other, 1)))
+            summed[item] = lax.psum_scatter(operand, "fsdp", scatter_dimension=0, tiled=True)
+    output = blocks["O"].astype(f32)
+
+    def back(*keys):
+        return diagonal(jnp.concatenate([reduces[key].total for key in keys], 1)).astype(f32)
+
+    def slabs_below(value):
+        return jnp.concatenate(
+            [value[:, i * skip_width : (i + 1) * skip_width] for i in range(slab_rows)], 0
+        )
+
+    second_one = summed["wu"].astype(f32)
+    first_one = summed["is"].astype(f32)
+    second_zero = back("w0", "u0")
+    inner_zero = back("i0")
+    skip_zero = back("s0")
+    inner_one = first_one[:, : qkv_width + out_width]
+    skip_grads = (slabs_below(skip_zero), slabs_below(first_one[:, qkv_width + out_width :]))
+    down_grads = (second_zero[:, :down_width].T, second_one[:, :down_width].T)
+    up_grads = (second_zero[:, down_width:], second_one[:, down_width:])
+    out_grads = (inner_zero[:, qkv_width:].T, inner_one[:, qkv_width:].T)
+    qkv_grads = [v[:, :qkv_width].reshape(attention_in.shape[1:]) for v in (inner_zero, inner_one)]
+
+    names = (
+        "skip_bias",
+        "first_gain",
+        "first_shift",
+        "out_bias",
+        "second_gain",
+        "second_shift",
+        "up_bias",
+        "down_bias",
+    )
+    parts = []
+    for now in grads:
+        full = jnp.zeros((2 * up_width,), f32)
+        now["up_bias"] = lax.dynamic_update_slice_in_dim(full, now["up_bias"], core * up_width, 0)
+        parts += [now[name].astype(f32).reshape(2 * fsdp_size, -1) for name in names]
+    small_sums = net.sum_small(jnp.concatenate(parts, 1)).reshape(LAYERS, -1)
+    small_out, begin = ({}, 0)
+    for name, size in zip(names, small_widths):
+        small_out[name] = small_sums[:, begin : begin + size]
+        begin += size
+    return (
+        output,
+        blocks["G0"][:, :width].astype(f32),
+        jnp.stack([blocks["G0"][:, width:].astype(f32), blocks["G1"].astype(f32)]),
+        jnp.stack(skip_grads),
+        small_out["skip_bias"],
+        small_out["first_gain"],
+        small_out["first_shift"],
+        jnp.stack(qkv_grads),
+        jnp.stack(out_grads),
+        small_out["out_bias"],
+        small_out["second_gain"],
+        small_out["second_shift"],
+        jnp.stack(up_grads),
+        small_out["up_bias"],
+        jnp.stack(down_grads),
+        small_out["down_bias"],
+    )
+
+
 def solution(mesh):
     placed = (
         P(("fsdp", "tp"), None),
@@ -405,7 +1435,7 @@
         P(("fsdp", "tp"), None),
     )
     return jax.shard_map(
-        body,
+        choose_body(mesh),
         mesh=mesh,
         in_specs=placed,
         out_specs=(

time: 2390 us -> 973 us (0.41)
  waiting for transfers between devices: 1420 us -> 255 us
  matrix products: 451 us -> 154 us
  blocking collectives: 253 us -> 0 us
  starting transfers between devices: 10.2 us -> 159 us
  Pallas kernels: 0 us -> 129 us
  local copies, waits for them, and re-layouts: 74.2 us -> 101 us
    reduce_scatter x20 -> x2, waiting for transfers between devices: 888 us -> 0.02 us  [fast_body(): lax.psum_scatter(operand, 'fsdp', scatter_dimension=0, tiled=True)]
    all_gather x20 -> x0, waiting for transfers between devices: 516 us -> none  [the longest x6 227 us: rows_of(): return lax.all_gather(normed, 'tp', axis=0, tiled=True)]
    dot_general x54 -> x30, matrix products: 451 us -> 154 us  [the longest x2 21.4 us: act_step(): jnp.dot(grad_rows(index), weights[index]['down'], preferred_element_type=...]
    ppermute x0 -> x121, waiting for transfers between devices: none -> 255 us  [the longest x64 190 us: along_ring(): return lax.ppermute(value, 'fsdp', self.ring_pairs[step])]
    ppermute x0 -> x121, starting transfers between devices: none -> 159 us  [the longest x17 63.7 us: diagonal_other(): return lax.ppermute(value, BOTH, self.diagonal_pairs)]
    all_gather x2 -> x0, blocking collectives: 129 us -> none  [fetch_layer(): lax.all_gather(up_bias[layer_index], ('fsdp', 'tp'), axis=0, tiled=True)]
    pallas_call x0 -> x12, Pallas kernels: none -> 129 us  [the longest x4 76.8 us: attention_backward(): pl.pallas_call(kernel, grid=(pair_count,), in_specs=[part(0), part(1), pa...]
    unnamed x2 -> x0, blocking collectives: 90.6 us -> none
  transfers between devices with their start and end apart: 42 -> 123, of which waited for: 34 -> 49; matrix products, arithmetic and copies ran while one was open for 14% -> 30% of each run, Pallas kernels for 0% -> 13%
where the time goes in v2:
time: 973 us; the launch traced here: 963 us
  waiting for transfers between devices  255 us (26%)
  starting transfers between devices  159 us (16%)
  matrix products  154 us (16%)
  other arithmetic  132 us (14%)
  Pallas kernels  129 us (13%)
  local copies, waits for them, and re-layouts  101 us (10%)
  between operations  33.6 us (3%)
    ppermute x64, waiting for transfers between devices, along_ring(): return lax.ppermute(value, 'fsdp', self.ring_pairs[step])  190 us
    pallas_call x4, Pallas kernels, attention_backward(): pl.pallas_call(kernel, grid=(pair_count,), in_specs=[part(0), part(1), pa...  76.8 us
    ppermute x17, starting transfers between devices, diagonal_other(): return lax.ppermute(value, BOTH, self.diagonal_pairs)  63.7 us
    ppermute x64, starting transfers between devices, along_ring(): return lax.ppermute(value, 'fsdp', self.ring_pairs[step])  57.6 us
    pallas_call x2, Pallas kernels, attention_forward(): pl.pallas_call(kernel, grid=(pairs,), in_specs=[part(0), part(1), part(2)...  37.9 us
    ppermute x17, waiting for transfers between devices, diagonal_other(): return lax.ppermute(value, BOTH, self.diagonal_pairs)  37.2 us
    unnamed x430, local copies, waits for them, and re-layouts  35.9 us
    select_n x9, other arithmetic, choose(): return jnp.where(self.core == self.column, own, other)  31.1 us
  transfers between devices with their start and end apart: 123, of which 49 were waited for; matrix products, arithmetic and copies ran while one was open for 30% of the time, Pallas kernels for 13%

profile of v2, /device:TPU:1, one launch (start us, length us, event | category | flops | bytes accessed | tf_op | source)
XLA Modules:
  0.0 963.0 jit_solution(16511074714728735212)
XLA Ops:
  15.4 5.5 collective-permute-done
  24.8 7.3 collective-permute-done.2
  33.7 8.7 collective-permute-done.1
  42.6 8.3 collective-permute-done.4.refs_2_
  55.1 14.3 %collective-permute-done.10.refs_5_ = bf16[128,3200]{1,0:T(8,128)(2,1)} collective-permute-done((bf16[128,3200]{1,0:T(8,128)(2,1)S(1)}, bf16[128,3200]{1,0:T(8,128)(2,1)}, u32[]{:S(2)}, u32[]{:S(2)}) %collective-permute-start.10) | collective-permute-done | bytes 819232 | tf_op jit(solution)/shard_map/ppermute | solution.py:624
  69.6 9.2 collective-permute-start.15
  80.3 6.1 collective-permute-done.7.refs_2_
  93.8 10.2 %collective-permute-done.13.refs_0_ = bf16[128,3200]{1,0:T(8,128)(2,1)S(1)} collective-permute-done((bf16[128,3200]{1,0:T(8,128)(2,1)S(1)}, bf16[128,3200]{1,0:T(8,128)(2,1)S(1)}, u32[]{:S(2)}, u32[]{:S(2)}) %collective-permute-start.13) | collective-permute-done | bytes 819232 | tf_op jit(solution)/shard_map/ppermute | solution.py:624
  104.0 9.2 collective-permute-start.6
  136.8 6.6 collective-permute-start.26
  159.1 10.0 %collective-permute-done.22.refs_7_ = bf16[128,1536]{1,0:T(8,128)(2,1)S(1)} collective-permute-done((bf16[128,1536]{1,0:T(8,128)(2,1)S(1)}, bf16[128,1536]{1,0:T(8,128)(2,1)S(1)}, u32[]{:S(2)}, u32[]{:S(2)}) %collective-permute-start.22) | collective-permute-done | bytes 393248 | tf_op jit(solution)/shard_map/ppermute | solution.py:624
  174.9 5.2 maximum_select_fusion.2
  200.5 7.0 collective-permute-done.31.refs_1_
  225.4 4.9 convolution_convert_fusion.1.query_ref.key_ref.value_ref
  234.8 19.0 %shard_map.344 = (bf16[1104,512]{1,0:T(8,128)(2,1)S(1)}, f32[4,2,1104]{2,1,0:T(2,128)S(1)}) custom-call(bf16[1104,1536]{1,0:T(8,128)(2,1)S(1)} %convolution_convert_fusion.1.query_ref.key_ref.value_ref, bf16[1104,1536]{1,0:T(8,128)(2,1)S(1)} %convolution_convert_fusion.1.query_ref.key_ref.value_ref, ...), custom_call_target="tpu_custom_call" | custom-call | flops 4992270336 | bytes 4521984 | tf_op jit(solution)/shard_map/pallas_call | solution.py:754
  293.0 9.9 %multiply_convert_fusion.1 = (bf16[1104,2048]{1,0:T(8,128)(2,1)S(1)}, f32[1104,2048]{1,0:T(8,128)}) fusion(f32[2048]{0:T(1024)S(1)} %dynamic-slice_convert_fusion.3, bf16[1024,2048]{1,0:T(8,128)(2,1)S(1)} %shard_map.345, bf16[552,1024]{1,0:T(8,128)(2,1)} %collective-permute-done.43, bf16[552,1024]{1,0:T(8,128)(2,1)} %add_convert_fusion.4), kind=kOutput, calls=%fused_computation.18 | convolution fusion | flops 4648599552 | bytes 20029440 | tf_op jit(solution)/shard_map/dot_general | solution.py:1071
  303.4 4.9 fusion.77
  317.7 6.7 collective-permute-done.50.refs_2_
  325.2 5.0 maximum_select_fusion.3
  345.4 10.5 %collective-permute-done.55.refs_1_ = bf16[128,2048]{1,0:T(8,128)(2,1)S(1)} collective-permute-done((bf16[128,2048]{1,0:T(8,128)(2,1)S(1)}, bf16[128,2048]{1,0:T(8,128)(2,1)S(1)}, u32[]{:S(2)}, u32[]{:S(2)}) %collective-permute-start.55) | collective-permute-done | bytes 524320 | tf_op jit(solution)/shard_map/ppermute | solution.py:624
  358.8 5.0 convolution_convert_fusion.query_ref.key_ref.value_ref
  368.1 18.9 %shard_map.347 = (bf16[1104,512]{1,0:T(8,128)(2,1)S(1)}, f32[4,2,1104]{2,1,0:T(2,128)S(1)}) custom-call(bf16[1104,1536]{1,0:T(8,128)(2,1)S(1)} %convolution_convert_fusion.query_ref.key_ref.value_ref, bf16[1104,1536]{1,0:T(8,128)(2,1)S(1)} %convolution_convert_fusion.query_ref.key_ref.value_ref, ...), custom_call_target="tpu_custom_call" | custom-call | flops 4992270336 | bytes 4521984 | tf_op jit(solution)/shard_map/pallas_call | solution.py:754
  394.9 6.0 collective-permute-done.62.refs_7_
  416.9 9.1 multiply_convert_fusion
  426.0 7.4 convolution_convert_fusion.7
  433.6 9.4 fusion.62
  443.1 4.9 fusion.79
  452.4 7.3 convolution_convert_fusion.6
  495.6 19.1 %shard_map.350 = (bf16[1104,256]{1,0:T(8,128)(2,1)S(1)}, bf16[1104,256]{1,0:T(8,128)(2,1)S(1)}, bf16[1104,256]{1,0:T(8,128)(2,1)S(1)}) custom-call(bf16[1104,1536]{1,0:T(8,128)(2,1)} %copy-done.67, bf16[1104,1536]{1,0:T(8,128)(2,1)} %copy-done.67, bf16[1104,1536]{1,0:T(8,128)(2,1)} %copy-done.67, bf16[1104,512]{1,0:T(8,128)(2,1)S(1)} %copy-done.65, ...), custom_call_target="tpu_custom_call" | custom-call | flops 6240337920 | bytes 4521984 | tf_op jit(solution)/shard_map/pallas_call | solution.py:833
  514.7 19.3 %shard_map.351 = (bf16[1104,256]{1,0:T(8,128)(2,1)S(1)}, bf16[1104,256]{1,0:T(8,128)(2,1)S(1)}, bf16[1104,256]{1,0:T(8,128)(2,1)S(1)}) custom-call(bf16[1104,1536]{1,0:T(8,128)(2,1)} %copy-done.67, bf16[1104,1536]{1,0:T(8,128)(2,1)} %copy-done.67, bf16[1104,1536]{1,0:T(8,128)(2,1)} %copy-done.67, bf16[1104,512]{1,0:T(8,128)(2,1)S(1)} %copy-done.65, ...), custom_call_target="tpu_custom_call" | custom-call | flops 6240337920 | bytes 4521984 | tf_op jit(solution)/shard_map/pallas_call | solution.py:833
  541.2 8.0 convolution_convert_fusion.9
  549.3 9.4 maximum_select_fusion
  588.7 11.9 %fusion.63 = (f32[2048]{0:T(1024)S(1)}, bf16[1104,2048]{1,0:T(8,128)(2,1)S(1)}) fusion(f32[1104,2048]{1,0:T(8,128)} %get-tuple-element.588, bf16[1024,2048]{1,0:T(8,128)(2,1)} %copy-done.2, bf16[552,1024]{1,0:T(8,128)(2,1)} %collective-permute-done.73, bf16[552,1024]{1,0:T(8,128)(2,1)S(1)} %get-tuple-element.483), kind=kOutput, calls=%fused_computation.342 | convolution fusion | flops 4664424448 | bytes 20029440 | tf_op jit(solution)/shard_map/dot_general | solution.py:1132
  613.0 8.4 convolution_convert_fusion.4
  621.4 10.5 %collective-permute-done.75 = bf16[1024,512]{1,0:T(8,128)(2,1)} collective-permute-done((bf16[1024,512]{1,0:T(8,128)(2,1)}, bf16[1024,512]{1,0:T(8,128)(2,1)}, u32[]{:S(2)}, u32[]{:S(2)}) %collective-permute-start.75) | collective-permute-done | bytes 1048608 | tf_op jit(solution)/shard_map/ppermute | solution.py:630
  632.0 6.2 convolution_convert_fusion.3
  638.2 4.9 fusion.83
  678.7 10.6 %maximum_select_fusion.1 = bf16[1024,3072]{1,0:T(8,128)(2,1)} fusion(bf16[1024,512]{1,0:T(8,128)(2,1)} %bitcast.27, bf16[1024,512]{1,0:T(8,128)(2,1)} %bitcast.26, bf16[1024,512]{1,0:T(8,128)(2,1)S(1)} %copy-done.149, bf16[1024,1536]{1,0:T(8,128)(2,1)S(1)} %copy-done.116, bf16[1024,512]{1,0:T(8,128)(2,1)} %collective-permute-done.83, ...), kind=kLoop, calls=%fused_computation.23 | loop fusion | flops 53477376 | bytes 18874368 | tf_op jit(solution)/shard_map/jit(_where)/select_n | solution.py:633
  689.3 19.2 %shard_map.352 = (bf16[1104,256]{1,0:T(8,128)(2,1)S(1)}, bf16[1104,256]{1,0:T(8,128)(2,1)S(1)}, bf16[1104,256]{1,0:T(8,128)(2,1)S(1)}) custom-call(bf16[1104,1536]{1,0:T(8,128)(2,1)} %copy-done.66, bf16[1104,1536]{1,0:T(8,128)(2,1)} %copy-done.66, bf16[1104,1536]{1,0:T(8,128)(2,1)} %copy-done.66, bf16[1104,512]{1,0:T(8,128)(2,1)S(1)} %copy-done.63, ...), custom_call_target="tpu_custom_call" | custom-call | flops 6240337920 | bytes 4521984 | tf_op jit(solution)/shard_map/pallas_call | solution.py:833
  717.6 19.2 %shard_map.353 = (bf16[1104,256]{1,0:T(8,128)(2,1)S(1)}, bf16[1104,256]{1,0:T(8,128)(2,1)S(1)}, bf16[1104,256]{1,0:T(8,128)(2,1)S(1)}) custom-call(bf16[1104,1536]{1,0:T(8,128)(2,1)} %copy-done.66, bf16[1104,1536]{1,0:T(8,128)(2,1)} %copy-done.66, bf16[1104,1536]{1,0:T(8,128)(2,1)} %copy-done.66, bf16[1104,512]{1,0:T(8,128)(2,1)S(1)} %copy-done.63, ...), custom_call_target="tpu_custom_call" | custom-call | flops 6240337920 | bytes 4521984 | tf_op jit(solution)/shard_map/pallas_call | solution.py:833
  762.2 9.5 collective-permute-done.87
  775.8 9.0 collective-permute-done.86
  800.7 5.1 convolution_convert_fusion.2
  825.8 28.8 %collective-permute-done.91 = bf16[128,2048]{1,0:T(8,128)(2,1)} collective-permute-done((bf16[128,2048]{1,0:T(8,128)(2,1)}, bf16[128,2048]{1,0:T(8,128)(2,1)}, u32[]{:S(2)}, u32[]{:S(2)}) %collective-permute-start.91) | collective-permute-done | bytes 524320 | tf_op jit(solution)/shard_map/ppermute | solution.py:624
  865.9 9.5 collective-permute-done.95
  881.6 11.5 %collective-permute-done.99 = bf16[128,1024]{1,0:T(8,128)(2,1)S(1)} collective-permute-done((bf16[128,1024]{1,0:T(8,128)(2,1)S(1)}, bf16[128,1024]{1,0:T(8,128)(2,1)S(1)}, u32[]{:S(2)}, u32[]{:S(2)}) %collective-permute-start.99) | collective-permute-done | bytes 262176 | tf_op jit(solution)/shard_map/ppermute | solution.py:624
  895.8 8.5 collective-permute-done.107
  912.1 5.8 collective-permute-start.108
  (916 shorter events, 458.4 us)
Async XLA Ops:
  7.3 939.8 %reduce-scatter.5.cloned.1.call-start = ((), (), s32[]{:S(2)}) async-start(), calls=%async_computation.3 | async-start | bytes 8912896 | tf_op jit(solution)/shard_map/reduce_scatter | solution.py:1355
  53.6 32.9 %collective-permute-start.7 = (bf16[128,3072]{1,0:T(8,128)(2,1)S(1)}, bf16[128,3072]{1,0:T(8,128)(2,1)}, u32[]{:S(2)}, u32[]{:S(2)}) collective-permute-start(bf16[128,3072]{1,0:T(8,128)(2,1)S(1)} %maximum_select_fusion.7.refs_3_), channel_id=1, source_target_pairs={{0,8},{2,10},{8,16},{10,18},{16,24},{18,26},{24,28},{26,30},{28,20... | collective-permute-start | bytes 2359304 | tf_op jit(solution)/shard_map/ppermute | solution.py:624
  54.9 31.5 %collective-permute-start.8 = (bf16[128,3072]{1,0:T(8,128)(2,1)S(1)}, bf16[128,3072]{1,0:T(8,128)(2,1)}, u32[]{:S(2)}, u32[]{:S(2)}) collective-permute-start(bf16[128,3072]{1,0:T(8,128)(2,1)S(1)} %maximum_select_fusion.7.refs_3_), channel_id=1, source_target_pairs={{0,4},{2,6},{8,0},{10,2},{16,8},{18,10},{24,16},{26,18},{28,24},{3... | collective-permute-start | bytes 2359304 | tf_op jit(solution)/shard_map/ppermute | solution.py:624
  78.8 25.2 %collective-permute-start.13 = (bf16[128,3200]{1,0:T(8,128)(2,1)S(1)}, bf16[128,3200]{1,0:T(8,128)(2,1)S(1)}, u32[]{:S(2)}, u32[]{:S(2)}) collective-permute-start(bf16[128,3200]{1,0:T(8,128)(2,1)S(1)} %collective-permute-done.9.refs_1_), channel_id=1, source_target_pairs={{0,8},{2,10},{8,16},{10,18},{16,24},{18,26},{24,28},{26,30},{28,20... | collective-permute-start | bytes 2457608 | tf_op jit(solution)/shard_map/ppermute | solution.py:624
  80.3 35.7 %collective-permute-start.14 = (bf16[128,3200]{1,0:T(8,128)(2,1)}, bf16[128,3200]{1,0:T(8,128)(2,1)S(1)}, u32[]{:S(2)}, u32[]{:S(2)}) collective-permute-start(bf16[128,3200]{1,0:T(8,128)(2,1)} %collective-permute-done.10.refs_5_), channel_id=1, source_target_pairs={{0,4},{2,6},{8,0},{10,2},{16,8},{18,10},{24,16},{26,18},{28,24},{3... | collective-permute-start | bytes 2457608 | tf_op jit(solution)/shard_map/ppermute | solution.py:624
  86.4 34.4 %collective-permute-start.11 = (bf16[128,3072]{1,0:T(8,128)(2,1)}, bf16[128,3072]{1,0:T(8,128)(2,1)}, u32[]{:S(2)}, u32[]{:S(2)}) collective-permute-start(bf16[128,3072]{1,0:T(8,128)(2,1)} %collective-permute-done.7.refs_2_), channel_id=1, source_target_pairs={{0,8},{2,10},{8,16},{10,18},{16,24},{18,26},{24,28},{26,30},{28,20... | collective-permute-start | bytes 2359304 | tf_op jit(solution)/shard_map/ppermute | solution.py:624
  87.6 34.3 %collective-permute-start.12 = (bf16[128,3072]{1,0:T(8,128)(2,1)}, bf16[128,3072]{1,0:T(8,128)(2,1)}, u32[]{:S(2)}, u32[]{:S(2)}) collective-permute-start(bf16[128,3072]{1,0:T(8,128)(2,1)} %collective-permute-done.8.refs_4_), channel_id=1, source_target_pairs={{0,4},{2,6},{8,0},{10,2},{16,8},{18,10},{24,16},{26,18},{28,24},{3... | collective-permute-start | bytes 2359304 | tf_op jit(solution)/shard_map/ppermute | solution.py:624
  88.8 34.4 %collective-permute-start.20 = (bf16[64,4096]{1,0:T(8,128)(2,1)}, bf16[64,4096]{1,0:T(8,128)(2,1)}, u32[]{:S(2)}, u32[]{:S(2)}) collective-permute-start(bf16[64,4096]{1,0:T(8,128)(2,1)} %broadcast_select_fusion.6), channel_id=1, source_target_pairs={{0,1},{1,0},{2,3},{3,2},{4,5},{5,4},{6,7},{7,6},{8,9},{9,8},{10,11... | collective-permute-start | bytes 1572872 | tf_op jit(solution)/shard_map/ppermute | solution.py:640
  104.0 50.5 %collective-permute-start.6 = (bf16[552,2048]{1,0:T(8,128)(2,1)}, bf16[552,2048]{1,0:T(8,128)(2,1)}, u32[]{:S(2)}, u32[]{:S(2)}) collective-permute-start(bf16[552,2048]{1,0:T(8,128)(2,1)} %get-tuple-element.222), channel_id=1, source_target_pairs={{2,1},{1,2},{6,5},{5,6},{10,9},{9,10},{14,13},{13,14},{18,17},{17,... | collective-permute-start | bytes 6782984 | tf_op jit(solution)/shard_map/ppermute | solution.py:630
  121.9 29.8 %collective-permute-start.16 = (bf16[128,3072]{1,0:T(8,128)(2,1)}, bf16[128,3072]{1,0:T(8,128)(2,1)}, u32[]{:S(2)}, u32[]{:S(2)}) collective-permute-start(bf16[128,3072]{1,0:T(8,128)(2,1)} %collective-permute-done.11.refs_1_), channel_id=1, source_target_pairs={{0,8},{2,10},{8,16},{10,18},{16,24},{18,26},{24,28},{26,30},{28,20... | collective-permute-start | bytes 2359304 | tf_op jit(solution)/shard_map/ppermute | solution.py:624
  123.2 29.1 %collective-permute-start.17 = (bf16[128,3072]{1,0:T(8,128)(2,1)}, bf16[128,3072]{1,0:T(8,128)(2,1)}, u32[]{:S(2)}, u32[]{:S(2)}) collective-permute-start(bf16[128,3072]{1,0:T(8,128)(2,1)} %collective-permute-done.12.refs_5_), channel_id=1, source_target_pairs={{0,4},{2,6},{8,0},{10,2},{16,8},{18,10},{24,16},{26,18},{28,24},{3... | collective-permute-start | bytes 2359304 | tf_op jit(solution)/shard_map/ppermute | solution.py:624
  136.8 38.1 %collective-permute-start.26 = (bf16[2048,512]{1,0:T(8,128)(2,1)}, bf16[2048,512]{1,0:T(8,128)(2,1)}, u32[]{:S(2)}, u32[]{:S(2)}) collective-permute-start(bf16[2048,512]{1,0:T(8,128)(2,1)} %get-tuple-element.245), channel_id=1, source_target_pairs={{0,2},{2,0},{4,6},{6,4},{8,10},{10,8},{12,14},{14,12},{16,18},{18,... | collective-permute-start | bytes 6291464 | tf_op jit(solution)/shard_map/ppermute | solution.py:618
  147.5 26.7 %collective-permute-start.27 = (bf16[128,2048]{1,0:T(8,128)(2,1)S(1)}, bf16[128,2048]{1,0:T(8,128)(2,1)S(1)}, u32[]{:S(2)}, u32[]{:S(2)}) collective-permute-start(bf16[128,2048]{1,0:T(8,128)(2,1)S(1)} %get-tuple-element.246.refs_3_), channel_id=1, source_target_pairs={{0,8},{2,10},{8,16},{10,18},{16,24},{18,26},{24,28},{26,30},{28,20... | collective-permute-start | bytes 1572872 | tf_op jit(solution)/shard_map/ppermute | solution.py:624
  191.3 33.5 %collective-permute-start.30 = (bf16[552,1024]{1,0:T(8,128)(2,1)S(1)}, bf16[552,1024]{1,0:T(8,128)(2,1)S(1)}, u32[]{:S(2)}, u32[]{:S(2)}) collective-permute-start(bf16[552,1024]{1,0:T(8,128)(2,1)S(1)} %add_convert_fusion.5), channel_id=1, source_target_pairs={{0,2},{2,0},{4,6},{6,4},{8,10},{10,8},{12,14},{14,12},{16,18},{18,... | collective-permute-start | bytes 3391496 | tf_op jit(solution)/shard_map/ppermute | solution.py:618
  195.3 58.5 %collective-permute-start.35 = (bf16[552,2048]{1,0:T(8,128)(2,1)S(1)}, bf16[552,2048]{1,0:T(8,128)(2,1)}, u32[]{:S(2)}, u32[]{:S(2)}) collective-permute-start(bf16[552,2048]{1,0:T(8,128)(2,1)S(1)} %copy-done.124), channel_id=1, source_target_pairs={{2,1},{1,2},{6,5},{5,6},{10,9},{9,10},{14,13},{13,14},{18,17},{17,... | collective-permute-start | bytes 6782984 | tf_op jit(solution)/shard_map/ppermute | solution.py:630
  223.6 30.2 %collective-permute-start.38 = (bf16[128,2048]{1,0:T(8,128)(2,1)S(1)}, bf16[128,2048]{1,0:T(8,128)(2,1)S(1)}, u32[]{:S(2)}, u32[]{:S(2)}) collective-permute-start(bf16[128,2048]{1,0:T(8,128)(2,1)S(1)} %collective-permute-done.36.refs_1_), channel_id=1, source_target_pairs={{0,8},{2,10},{8,16},{10,18},{16,24},{18,26},{24,28},{26,30},{28,20... | collective-permute-start | bytes 1572872 | tf_op jit(solution)/shard_map/ppermute | solution.py:624
  224.8 29.0 %collective-permute-start.39 = (bf16[128,2048]{1,0:T(8,128)(2,1)S(1)}, bf16[128,2048]{1,0:T(8,128)(2,1)S(1)}, u32[]{:S(2)}, u32[]{:S(2)}) collective-permute-start(bf16[128,2048]{1,0:T(8,128)(2,1)S(1)} %collective-permute-done.37.refs_5_), channel_id=1, source_target_pairs={{0,4},{2,6},{8,0},{10,2},{16,8},{18,10},{24,16},{26,18},{28,24},{3... | collective-permute-start | bytes 1572872 | tf_op jit(solution)/shard_map/ppermute | solution.py:624
  278.6 46.6 %collective-permute-start.49 = (bf16[2048,512]{1,0:T(8,128)(2,1)}, bf16[2048,512]{1,0:T(8,128)(2,1)}, u32[]{:S(2)}, u32[]{:S(2)}) collective-permute-start(bf16[2048,512]{1,0:T(8,128)(2,1)} %get-tuple-element.255), channel_id=1, source_target_pairs={{0,2},{2,0},{4,6},{6,4},{8,10},{10,8},{12,14},{14,12},{16,18},{18,... | collective-permute-start | bytes 6291464 | tf_op jit(solution)/shard_map/ppermute | solution.py:618
  344.0 23.2 %collective-permute-start.57 = (bf16[128,2048]{1,0:T(8,128)(2,1)S(1)}, bf16[128,2048]{1,0:T(8,128)(2,1)S(1)}, u32[]{:S(2)}, u32[]{:S(2)}) collective-permute-start(bf16[128,2048]{1,0:T(8,128)(2,1)S(1)} %collective-permute-done.52.refs_1_), channel_id=1, source_target_pairs={{0,8},{2,10},{8,16},{10,18},{16,24},{18,26},{24,28},{26,30},{28,20... | collective-permute-start | bytes 1572872 | tf_op jit(solution)/shard_map/ppermute | solution.py:624
  356.9 30.2 %collective-permute-start.59 = (bf16[128,2048]{1,0:T(8,128)(2,1)S(1)}, bf16[128,2048]{1,0:T(8,128)(2,1)S(1)}, u32[]{:S(2)}, u32[]{:S(2)}) collective-permute-start(bf16[128,2048]{1,0:T(8,128)(2,1)S(1)} %collective-permute-done.55.refs_1_), channel_id=1, source_target_pairs={{0,8},{2,10},{8,16},{10,18},{16,24},{18,26},{24,28},{26,30},{28,20... | collective-permute-start | bytes 1572872 | tf_op jit(solution)/shard_map/ppermute | solution.py:624
  357.1 30.0 %collective-permute-start.60 = (bf16[128,2048]{1,0:T(8,128)(2,1)S(1)}, bf16[128,2048]{1,0:T(8,128)(2,1)S(1)}, u32[]{:S(2)}, u32[]{:S(2)}) collective-permute-start(bf16[128,2048]{1,0:T(8,128)(2,1)S(1)} %collective-permute-done.56.refs_5_), channel_id=1, source_target_pairs={{0,4},{2,6},{8,0},{10,2},{16,8},{18,10},{24,16},{26,18},{28,24},{3... | collective-permute-start | bytes 1572872 | tf_op jit(solution)/shard_map/ppermute | solution.py:624
  449.5 65.1 %collective-permute-start.70 = (bf16[1024,2048]{1,0:T(8,128)(2,1)}, bf16[1024,2048]{1,0:T(8,128)(2,1)}, u32[]{:S(2)}, u32[]{:S(2)}) collective-permute-start(bf16[1024,2048]{1,0:T(8,128)(2,1)} %convolution_convert_fusion.7), channel_id=1, source_target_pairs={{2,1},{1,2},{6,5},{5,6},{10,9},{9,10},{14,13},{13,14},{18,17},{17,... | collective-permute-start | bytes 12582920 | tf_op jit(solution)/shard_map/ppermute | solution.py:630
  463.1 25.7 %collective-permute-start.69 = (bf16[552,1024]{1,0:T(8,128)(2,1)S(1)}, bf16[552,1024]{1,0:T(8,128)(2,1)}, u32[]{:S(2)}, u32[]{:S(2)}) collective-permute-start(bf16[552,1024]{1,0:T(8,128)(2,1)S(1)} %fusion.50), channel_id=1, source_target_pairs={{0,2},{2,0},{4,6},{6,4},{8,10},{10,8},{12,14},{14,12},{16,18},{18,... | collective-permute-start | bytes 3391496 | tf_op jit(solution)/shard_map/ppermute | solution.py:618
  485.2 64.1 %collective-permute-start.72 = (bf16[1024,2048]{1,0:T(8,128)(2,1)S(1)}, bf16[1024,2048]{1,0:T(8,128)(2,1)}, u32[]{:S(2)}, u32[]{:S(2)}) collective-permute-start(bf16[1024,2048]{1,0:T(8,128)(2,1)S(1)} %copy-done.114), channel_id=1, source_target_pairs={{2,1},{1,2},{6,5},{5,6},{10,9},{9,10},{14,13},{13,14},{18,17},{17,... | collective-permute-start | bytes 12582920 | tf_op jit(solution)/shard_map/ppermute | solution.py:630
  577.7 25.8 %collective-permute-start.76 = (bf16[2048,512]{1,0:T(8,128)(2,1)}, bf16[2048,512]{1,0:T(8,128)(2,1)}, u32[]{:S(2)}, u32[]{:S(2)}) collective-permute-start(bf16[2048,512]{1,0:T(8,128)(2,1)} %constant_dynamic-slice_fusion.6), channel_id=1, source_target_pairs={{0,2},{2,0},{4,6},{6,4},{8,10},{10,8},{12,14},{14,12},{16,18},{18,... | collective-permute-start | bytes 6291464 | tf_op jit(solution)/shard_map/ppermute | solution.py:618
  581.5 368.9 %reduce-scatter.3.cloned.1.call-start = ((), (), s32[]{:S(2)}) async-start(), calls=%async_computation.2 | async-start | bytes 6684672 | tf_op jit(solution)/shard_map/reduce_scatter | solution.py:1355
  581.5 50.4 %collective-permute-start.74 = (bf16[1024,1536]{1,0:T(8,128)(2,1)}, bf16[1024,1536]{1,0:T(8,128)(2,1)}, u32[]{:S(2)}, u32[]{:S(2)}) collective-permute-start(bf16[1024,1536]{1,0:T(8,128)(2,1)} %convolution_convert_fusion.9), channel_id=1, source_target_pairs={{2,1},{1,2},{6,5},{5,6},{10,9},{9,10},{14,13},{13,14},{18,17},{17,... | collective-permute-start | bytes 9437192 | tf_op jit(solution)/shard_map/ppermute | solution.py:630
  584.1 47.8 %collective-permute-start.75 = (bf16[1024,512]{1,0:T(8,128)(2,1)}, bf16[1024,512]{1,0:T(8,128)(2,1)}, u32[]{:S(2)}, u32[]{:S(2)}) collective-permute-start(bf16[1024,512]{1,0:T(8,128)(2,1)} %convolution_convert_fusion.14), channel_id=1, source_target_pairs={{2,1},{1,2},{6,5},{5,6},{10,9},{9,10},{14,13},{13,14},{18,17},{17,... | collective-permute-start | bytes 3145736 | tf_op jit(solution)/shard_map/ppermute | solution.py:630
  612.9 30.5 %collective-permute-start.78 = (bf16[552,1024]{1,0:T(8,128)(2,1)S(1)}, bf16[552,1024]{1,0:T(8,128)(2,1)S(1)}, u32[]{:S(2)}, u32[]{:S(2)}) collective-permute-start(bf16[552,1024]{1,0:T(8,128)(2,1)S(1)} %slice.749), channel_id=1, source_target_pairs={{0,2},{2,0},{4,6},{6,4},{8,10},{10,8},{12,14},{14,12},{16,18},{18,... | collective-permute-start | bytes 3391496 | tf_op jit(solution)/shard_map/ppermute | solution.py:618
  650.7 27.5 %collective-permute-start.82 = (bf16[1024,512]{1,0:T(8,128)(2,1)}, bf16[1024,512]{1,0:T(8,128)(2,1)}, u32[]{:S(2)}, u32[]{:S(2)}) collective-permute-start(bf16[1024,512]{1,0:T(8,128)(2,1)} %bitcast.26), channel_id=1, source_target_pairs={{2,1},{1,2},{6,5},{5,6},{10,9},{9,10},{14,13},{13,14},{18,17},{17,... | collective-permute-start | bytes 3145736 | tf_op jit(solution)/shard_map/ppermute | solution.py:630
  653.1 25.5 %collective-permute-start.83 = (bf16[1024,512]{1,0:T(8,128)(2,1)}, bf16[1024,512]{1,0:T(8,128)(2,1)}, u32[]{:S(2)}, u32[]{:S(2)}) collective-permute-start(bf16[1024,512]{1,0:T(8,128)(2,1)} %bitcast.27), channel_id=1, source_target_pairs={{2,1},{1,2},{6,5},{5,6},{10,9},{9,10},{14,13},{13,14},{18,17},{17,... | collective-permute-start | bytes 3145736 | tf_op jit(solution)/shard_map/ppermute | solution.py:630
  659.6 52.1 %collective-permute-start.80 = (bf16[2,2,2,64,2048]{4,3,0,1,2:T(8,128)(2,1)}, bf16[2,2,2,64,2048]{4,3,0,1,2:T(8,128)(2,1)}, u32[]{:S(2)}, u32[]{:S(2)}) collective-permute-start(bf16[2,2,2,64,2048]{4,3,0,1,2:T(8,128)(2,1)} %bitcast.258), channel_id=1, source_target_pairs={{0,4},{2,6},{4,0},{6,2},{8,12},{10,14},{12,8},{14,10},{16,20},{18,... | collective-permute-start | bytes 6291464 | tf_op jit(solution)/shard_map/ppermute | solution.py:643
  664.4 72.5 %collective-permute-start.84 = (bf16[2,2,2,64,2048]{4,3,0,2,1:T(8,128)(2,1)}, bf16[2,2,2,64,2048]{4,3,0,2,1:T(8,128)(2,1)}, u32[]{:S(2)}, u32[]{:S(2)}) collective-permute-start(bf16[2,2,2,64,2048]{4,3,0,2,1:T(8,128)(2,1)} %bitcast.257), channel_id=1, source_target_pairs={{0,8},{2,10},{4,12},{6,14},{8,0},{10,2},{12,4},{14,6},{16,24},{18,... | collective-permute-start | bytes 6291464 | tf_op jit(solution)/shard_map/ppermute | solution.py:643
  667.8 46.3 %collective-permute-start.79 = (bf16[552,1024]{1,0:T(8,128)(2,1)S(1)}, bf16[552,1024]{1,0:T(8,128)(2,1)}, u32[]{:S(2)}, u32[]{:S(2)}) collective-permute-start(bf16[552,1024]{1,0:T(8,128)(2,1)S(1)} %fusion.14), channel_id=1, source_target_pairs={{2,1},{1,2},{6,5},{5,6},{10,9},{9,10},{14,13},{13,14},{18,17},{17,... | collective-permute-start | bytes 3391496 | tf_op jit(solution)/shard_map/ppermute | solution.py:630
  746.1 41.1 %collective-permute-start.85 = (bf16[552,1024]{1,0:T(8,128)(2,1)}, bf16[552,1024]{1,0:T(8,128)(2,1)S(1)}, u32[]{:S(2)}, u32[]{:S(2)}) collective-permute-start(bf16[552,1024]{1,0:T(8,128)(2,1)} %slice.747), channel_id=1, source_target_pairs={{0,2},{2,0},{4,6},{6,4},{8,10},{10,8},{12,14},{14,12},{16,18},{18,... | collective-permute-start | bytes 3391496 | tf_op jit(solution)/shard_map/ppermute | solution.py:618
  747.1 24.5 %collective-permute-start.87 = (bf16[2,2,64,2048]{3,2,0,1:T(8,128)(2,1)}, bf16[2,2,64,2048]{3,2,0,1:T(8,128)(2,1)}, u32[]{:S(2)}, u32[]{:S(2)}) collective-permute-start(bf16[2,2,64,2048]{3,2,0,1:T(8,128)(2,1)} %dynamic-slice_bitcast_fusion.1), channel_id=1, source_target_pairs={{0,1},{1,0},{2,3},{3,2},{4,5},{5,4},{6,7},{7,6},{8,9},{9,8},{10,11... | collective-permute-start | bytes 3145736 | tf_op jit(solution)/shard_map/ppermute | solution.py:640
  753.0 31.8 %collective-permute-start.86 = (bf16[552,1024]{1,0:T(8,128)(2,1)}, bf16[552,1024]{1,0:T(8,128)(2,1)}, u32[]{:S(2)}, u32[]{:S(2)}) collective-permute-start(bf16[552,1024]{1,0:T(8,128)(2,1)} %get-tuple-element.373), channel_id=1, source_target_pairs={{2,1},{1,2},{6,5},{5,6},{10,9},{9,10},{14,13},{13,14},{18,17},{17,... | collective-permute-start | bytes 3391496 | tf_op jit(solution)/shard_map/ppermute | solution.py:630
  759.7 33.8 %collective-permute-start.88 = (bf16[128,1024]{1,0:T(8,128)(2,1)}, bf16[128,1024]{1,0:T(8,128)(2,1)}, u32[]{:S(2)}, u32[]{:S(2)}) collective-permute-start(bf16[128,1024]{1,0:T(8,128)(2,1)} %get-tuple-element.559), channel_id=1, source_target_pairs={{0,8},{2,10},{8,16},{10,18},{16,24},{18,26},{24,28},{26,30},{28,20... | collective-permute-start | bytes 786440 | tf_op jit(solution)/shard_map/ppermute | solution.py:624
  760.6 32.9 %collective-permute-start.89 = (bf16[128,1024]{1,0:T(8,128)(2,1)}, bf16[128,1024]{1,0:T(8,128)(2,1)}, u32[]{:S(2)}, u32[]{:S(2)}) collective-permute-start(bf16[128,1024]{1,0:T(8,128)(2,1)} %get-tuple-element.558), channel_id=1, source_target_pairs={{0,4},{2,6},{8,0},{10,2},{16,8},{18,10},{24,16},{26,18},{28,24},{3... | collective-permute-start | bytes 786440 | tf_op jit(solution)/shard_map/ppermute | solution.py:624
  771.7 41.0 %collective-permute-start.93 = (bf16[2,2,64,2048]{3,2,0,1:T(8,128)(2,1)}, bf16[2,2,64,2048]{3,2,0,1:T(8,128)(2,1)}, u32[]{:S(2)}, u32[]{:S(2)}) collective-permute-start(bf16[2,2,64,2048]{3,2,0,1:T(8,128)(2,1)} %dynamic-slice_bitcast_fusion), channel_id=1, source_target_pairs={{0,4},{2,6},{4,0},{6,2},{8,12},{10,14},{12,8},{14,10},{16,20},{18,... | collective-permute-start | bytes 3145736 | tf_op jit(solution)/shard_map/ppermute | solution.py:643
  812.6 50.1 %collective-permute-start.97 = (bf16[2,64,2048]{2,1,0:T(8,128)(2,1)}, bf16[2,64,2048]{2,1,0:T(8,128)(2,1)}, u32[]{:S(2)}, u32[]{:S(2)}) collective-permute-start(bf16[2,64,2048]{2,1,0:T(8,128)(2,1)} %dynamic-slice_bitcast_fusion.3), channel_id=1, source_target_pairs={{0,8},{2,10},{4,12},{6,14},{8,0},{10,2},{12,4},{14,6},{16,24},{18,... | collective-permute-start | bytes 1572872 | tf_op jit(solution)/shard_map/ppermute | solution.py:643
  812.6 42.1 %collective-permute-start.91 = (bf16[128,2048]{1,0:T(8,128)(2,1)}, bf16[128,2048]{1,0:T(8,128)(2,1)}, u32[]{:S(2)}, u32[]{:S(2)}) collective-permute-start(bf16[128,2048]{1,0:T(8,128)(2,1)} %add_convert_fusion.10), channel_id=1, source_target_pairs={{0,4},{2,6},{8,0},{10,2},{16,8},{18,10},{24,16},{26,18},{28,24},{3... | collective-permute-start | bytes 1572872 | tf_op jit(solution)/shard_map/ppermute | solution.py:624
  812.7 42.0 %collective-permute-start.90 = (bf16[128,2048]{1,0:T(8,128)(2,1)}, bf16[128,2048]{1,0:T(8,128)(2,1)}, u32[]{:S(2)}, u32[]{:S(2)}) collective-permute-start(bf16[128,2048]{1,0:T(8,128)(2,1)} %add_convert_fusion.11), channel_id=1, source_target_pairs={{0,8},{2,10},{8,16},{10,18},{16,24},{18,26},{24,28},{26,30},{28,20... | collective-permute-start | bytes 1572872 | tf_op jit(solution)/shard_map/ppermute | solution.py:624
  819.9 61.0 %collective-permute-start.100 = (bf16[2,64,2048]{2,1,0:T(8,128)(2,1)}, bf16[2,64,2048]{2,1,0:T(8,128)(2,1)S(1)}, u32[]{:S(2)}, u32[]{:S(2)}) collective-permute-start(bf16[2,64,2048]{2,1,0:T(8,128)(2,1)} %dynamic-slice_bitcast_fusion.2), channel_id=1, source_target_pairs={{0,1},{1,0},{2,3},{3,2},{4,5},{5,4},{6,7},{7,6},{8,9},{9,8},{10,11... | collective-permute-start | bytes 1572872 | tf_op jit(solution)/shard_map/ppermute | solution.py:640
  855.9 23.2 %collective-permute-start.102 = (bf16[128,2048]{1,0:T(8,128)(2,1)S(1)}, bf16[128,2048]{1,0:T(8,128)(2,1)S(1)}, u32[]{:S(2)}, u32[]{:S(2)}) collective-permute-start(bf16[128,2048]{1,0:T(8,128)(2,1)S(1)} %add_convert_fusion.8), channel_id=1, source_target_pairs={{0,4},{2,6},{8,0},{10,2},{16,8},{18,10},{24,16},{26,18},{28,24},{3... | collective-permute-start | bytes 1572872 | tf_op jit(solution)/shard_map/ppermute | solution.py:624
  875.4 33.4 %collective-permute-start.105 = (bf16[64,2048]{1,0:T(8,128)(2,1)S(1)}, bf16[64,2048]{1,0:T(8,128)(2,1)S(1)}, u32[]{:S(2)}, u32[]{:S(2)}) collective-permute-start(bf16[64,2048]{1,0:T(8,128)(2,1)S(1)} %dynamic-slice_bitcast_fusion.13), channel_id=1, source_target_pairs={{0,16},{2,18},{4,20},{6,22},{8,24},{10,26},{12,28},{14,30},{16,0},... | collective-permute-start | bytes 786440 | tf_op jit(solution)/shard_map/ppermute | solution.py:643
  875.4 63.1 %collective-permute-start.94 = (bf16[552,2048]{1,0:T(8,128)(2,1)}, bf16[552,2048]{1,0:T(8,128)(2,1)S(1)}, u32[]{:S(2)}, u32[]{:S(2)}) collective-permute-start(bf16[552,2048]{1,0:T(8,128)(2,1)} %convolution_convert_fusion.10), channel_id=1, source_target_pairs={{2,1},{1,2},{6,5},{5,6},{10,9},{9,10},{14,13},{13,14},{18,17},{17,... | collective-permute-start | bytes 6782984 | tf_op jit(solution)/shard_map/ppermute | solution.py:630
  880.9 23.4 %collective-permute-start.107 = (bf16[128,2048]{1,0:T(8,128)(2,1)S(1)}, bf16[128,2048]{1,0:T(8,128)(2,1)S(1)}, u32[]{:S(2)}, u32[]{:S(2)}) collective-permute-start(bf16[128,2048]{1,0:T(8,128)(2,1)S(1)} %add_convert_fusion.6), channel_id=1, source_target_pairs={{0,4},{2,6},{8,0},{10,2},{16,8},{18,10},{24,16},{26,18},{28,24},{3... | collective-permute-start | bytes 1572872 | tf_op jit(solution)/shard_map/ppermute | solution.py:624
  (281 other events, 3192.4 us)
Sparse Core Ops, SparseCore 0:
  581.6 117.3 reduce-scatter.4
  761.3 101.5 reduce-scatter.2

commit v3 on v2

--- a/solution.py
+++ b/solution.py
@@ -3,6 +3,7 @@
 from jax import lax
 from jax.experimental import pallas as pl
 from jax.experimental.pallas import tpu as pltpu
+from jax.sharding import Mesh
 from jax.sharding import PartitionSpec as P
 
 HEAD_DIM = 64
@@ -387,15 +388,10 @@
     )
 
 
-BOTH = ("fsdp", "tp")
+FSDP = ("chip", "core")
+BOTH = ("chip", "core", "tp")
+NETWORK = ("chip", "tp")
 GAUSS = 0.3989422804014327
-
-
-def choose_body(mesh):
-    fsdp_size, tp_size = (mesh.shape["fsdp"], mesh.shape["tp"])
-    if tp_size != 2 or fsdp_size < 4 or fsdp_size & (fsdp_size - 1):
-        return general_body
-    return lambda *arrays: fast_body(fsdp_size, *arrays)
 
 
 class Sequence:
@@ -471,8 +467,59 @@
             [net.order[(net.order.index(q) + offset) % net.chips] for offset in offsets]
             for q in range(net.chips)
         ]
-        places = lax.dynamic_index_in_dim(jnp.asarray(table, jnp.int32), net.chip, 0, False)
+        places = lax.dynamic_index_in_dim(jnp.asarray(table, jnp.int32), net.chip, 0, False, allow_negative_indices=False)
         return copy_kernel(places, operands, jobs, shapes)
+
+
+def add_blocks(places, tensors, blocks, ahead, behind):
+    rows = tensors[0].shape[0] // blocks
+    widths = [t.shape[1] for t in tensors]
+    total = sum(widths)
+    spans = ((0, ahead.shape[1]), (total - behind.shape[1], total))
+
+    def kernel(at_ref, *refs):
+        count = len(tensors)
+        for side in range(2):
+            got_ref, out_ref = (refs[2 * count + side], refs[2 * count + 2 + side])
+            low, high = spans[side]
+            begin = 0
+            for index, width in enumerate(widths):
+                block_ref = refs[side * count + index]
+                first, last = (max(begin, low), min(begin + width, high))
+                if first >= last:
+                    out_ref[:, begin : begin + width] = block_ref[...]
+                else:
+                    if first > begin:
+                        out_ref[:, begin:first] = block_ref[:, : first - begin]
+                    if last < begin + width:
+                        out_ref[:, last : begin + width] = block_ref[:, last - begin :]
+                    own = block_ref[:, first - begin : last - begin].astype(jnp.float32)
+                    got = got_ref[:, first - low : last - low].astype(jnp.float32)
+                    out_ref[:, first:last] = (own + got).astype(jnp.bfloat16)
+                begin += width
+
+    def whole(value):
+        return pl.BlockSpec(value.shape, lambda i, at: (0, 0))
+
+    def block(width, side):
+        return pl.BlockSpec((rows, width), lambda i, at: (at[side], 0))
+
+    out = jax.ShapeDtypeStruct((rows, total), jnp.bfloat16)
+    return pl.pallas_call(
+        kernel,
+        grid_spec=pltpu.PrefetchScalarGridSpec(
+            num_scalar_prefetch=1,
+            grid=(1,),
+            in_specs=[block(width, side) for side in range(2) for width in widths]
+            + [whole(ahead), whole(behind)],
+            out_specs=[whole(out), whole(out)],
+        ),
+        out_shape=[out, out],
+        compiler_params=pltpu.CompilerParams(vmem_limit_bytes=24 << 20),
+        cost_estimate=pl.CostEstimate(
+            flops=2 * rows * total, bytes_accessed=12 * rows * total, transcendentals=0
+        ),
+    )(places, *tensors, *tensors, ahead, behind)
 
 
 class RingSum:
@@ -482,7 +529,7 @@
         if columns_first:
             self.stage = "columns"
             self.coming = [
-                net.to_column(lax.dynamic_index_in_dim(v, 1 - net.column, 1, False))
+                net.to_column(lax.dynamic_index_in_dim(v, 1 - net.column, 1, False, allow_negative_indices=False))
                 for v in self.views
             ]
         else:
@@ -491,7 +538,7 @@
 
     def block(self, offset):
         at = self.net.chip_at(offset)
-        parts = [lax.dynamic_index_in_dim(v, at, 0, False) for v in self.views]
+        parts = [lax.dynamic_index_in_dim(v, at, 0, False, allow_negative_indices=False) for v in self.views]
         return jnp.concatenate(parts, 1)
 
     def begin(self):
@@ -508,7 +555,7 @@
         if self.stage == "columns":
             self.views = [
                 (
-                    lax.dynamic_index_in_dim(v, net.column, 1, False).astype(jnp.float32)
+                    lax.dynamic_index_in_dim(v, net.column, 1, False, allow_negative_indices=False).astype(jnp.float32)
                     + other.astype(jnp.float32)
                 ).astype(jnp.bfloat16)
                 for v, other in zip(self.views, got)
@@ -521,25 +568,21 @@
             self.total = sequence.mark(total.astype(jnp.bfloat16))
             return
         ahead, behind = got
-        if self.distance == net.half_ring:
-            low, high = (ahead, behind)
-            ahead = jnp.concatenate([low, jnp.zeros(high.shape, low.dtype)], 1)
-            behind = jnp.concatenate([jnp.zeros(low.shape, low.dtype), high], 1)
-        ahead, behind = (ahead.astype(jnp.float32), behind.astype(jnp.float32))
         self.distance -= 1
         if self.distance:
-            ahead = (self.block(self.distance).astype(jnp.float32) + ahead).astype(jnp.bfloat16)
-            behind = (self.block(-self.distance).astype(jnp.float32) + behind).astype(jnp.bfloat16)
-            sequence.mark((ahead, behind))
+            places = jnp.stack([net.chip_at(self.distance), net.chip_at(-self.distance)])
+            flat = [v.reshape(-1, v.shape[2]) for v in self.views]
+            ahead, behind = sequence.mark(add_blocks(places, flat, net.chips, ahead, behind))
             self.coming = (net.along_ring(ahead, 1), net.along_ring(behind, -1))
             return
+        ahead, behind = (ahead.astype(jnp.float32), behind.astype(jnp.float32))
         total = self.block(0).astype(jnp.float32) + ahead + behind
         if self.columns_first:
             self.total = sequence.mark(total.astype(jnp.bfloat16))
             return
         half_rows = total.shape[0] // 2
-        self.keep = lax.dynamic_slice_in_dim(total, net.column * half_rows, half_rows, 0)
-        send = lax.dynamic_slice_in_dim(total, (1 - net.column) * half_rows, half_rows, 0)
+        self.keep = lax.dynamic_slice_in_dim(total, net.column * half_rows, half_rows, 0, allow_negative_indices=False)
+        send = lax.dynamic_slice_in_dim(total, (1 - net.column) * half_rows, half_rows, 0, allow_negative_indices=False)
         send = sequence.mark(send.astype(jnp.bfloat16))
         self.stage, self.coming = ("last", net.to_column(send))
 
@@ -559,7 +602,7 @@
         side = self.net.side(bit)
 
         def half(which):
-            parts = [lax.dynamic_index_in_dim(v, which, axis, False) for v in self.views]
+            parts = [lax.dynamic_index_in_dim(v, which, axis, False, allow_negative_indices=False) for v in self.views]
             return jnp.concatenate(parts, -1)
 
         self.keep = half(side)
@@ -575,6 +618,99 @@
             self.cut()
 
 
+class HalvingSum:
+    def __init__(self, net, tensors, bits):
+        self.net, self.bits, self.round = (net, bits, 0)
+        count = len(bits)
+        self.views = [t.reshape((2,) * count + (-1, t.shape[1])) for t in tensors]
+        self.left = list(reversed(range(count)))
+        self.cut()
+
+    def cut(self):
+        bit = self.bits[self.round]
+        axis = self.left.index(bit)
+        self.left.remove(bit)
+        side = self.net.side(bit)
+
+        def half(which):
+            parts = [lax.dynamic_index_in_dim(v, which, axis, False, allow_negative_indices=False) for v in self.views]
+            return jnp.concatenate(parts, -1)
+
+        self.keep = half(side)
+        self.coming = self.net.to_partner(half(1 - side), bit)
+
+    def advance(self, sequence):
+        got = sequence.at(self.coming)
+        total = self.keep.astype(jnp.float32) + got.astype(jnp.float32)
+        self.round += 1
+        self.total = sequence.mark(total.astype(jnp.bfloat16))
+        if self.round < len(self.bits):
+            self.views = [self.total]
+            self.cut()
+
+
+class HalvingSum:
+    def __init__(self, net, tensors, bits):
+        self.net, self.bits, self.round = (net, bits, 0)
+        count = len(bits)
+        self.views = [t.reshape((2,) * count + (-1, t.shape[1])) for t in tensors]
+        self.left = list(reversed(range(count)))
+        self.cut()
+
+    def cut(self):
+        bit = self.bits[self.round]
+        axis = self.left.index(bit)
+        self.left.remove(bit)
+        side = self.net.side(bit)
+
+        def half(which):
+            parts = [lax.dynamic_index_in_dim(v, which, axis, False, allow_negative_indices=False) for v in self.views]
+            return jnp.concatenate(parts, -1)
+
+        self.keep = half(side)
+        self.coming = self.net.to_partner(half(1 - side), bit)
+
+    def advance(self, sequence):
+        got = sequence.at(self.coming)
+        total = self.keep.astype(jnp.float32) + got.astype(jnp.float32)
+        self.round += 1
+        self.total = sequence.mark(total.astype(jnp.bfloat16))
+        if self.round < len(self.bits):
+            self.views = [self.total]
+            self.cut()
+
+
+class HalvingSum:
+    def __init__(self, net, tensors, bits):
+        self.net, self.bits, self.round = (net, bits, 0)
+        count = len(bits)
+        self.views = [t.reshape((2,) * count + (-1, t.shape[1])) for t in tensors]
+        self.left = list(reversed(range(count)))
+        self.cut()
+
+    def cut(self):
+        bit = self.bits[self.round]
+        axis = self.left.index(bit)
+        self.left.remove(bit)
+        side = self.net.side(bit)
+
+        def half(which):
+            parts = [lax.dynamic_index_in_dim(v, which, axis, False, allow_negative_indices=False) for v in self.views]
+            return jnp.concatenate(parts, -1)
+
+        self.keep = half(side)
+        self.coming = self.net.to_partner(half(1 - side), bit)
+
+    def advance(self, sequence):
+        got = sequence.at(self.coming)
+        total = self.keep.astype(jnp.float32) + got.astype(jnp.float32)
+        self.round += 1
+        self.total = sequence.mark(total.astype(jnp.bfloat16))
+        if self.round < len(self.bits):
+            self.views = [self.total]
+            self.cut()
+
+
 class Swap:
     def __init__(self, net, tensors):
         self.net, self.tensors = (net, tensors)
@@ -587,8 +723,8 @@
 class CoreNetwork:
     def __init__(self, fsdp_size):
         self.chips = fsdp_size // 2
-        self.core = lax.axis_index("fsdp") % 2
-        self.chip = lax.axis_index("fsdp") // 2
+        self.core = lax.axis_index("core")
+        self.chip = lax.axis_index("chip")
         self.column = lax.axis_index("tp")
         self.bits = self.chips.bit_length()
         half = self.chips // 2
@@ -599,7 +735,7 @@
             for q in range(self.chips)
         ]
         self.chips_here = lax.dynamic_index_in_dim(
-            jnp.asarray(table, jnp.int32), self.chip, 0, False
+            jnp.asarray(table, jnp.int32), self.chip, 0, False, allow_negative_indices=False
         )
         self.ring_pairs = {}
         for step in (1, -1):
@@ -615,13 +751,13 @@
             self.diagonal_pairs += [(one, two), (two, one)]
 
     def to_core(self, value):
-        return lax.ppermute(value, "fsdp", self.core_pairs)
+        return lax.ppermute(value, FSDP, self.core_pairs)
 
     def chip_at(self, offset):
         return self.chips_here[offset % self.chips]
 
     def along_ring(self, value, step):
-        return lax.ppermute(value, "fsdp", self.ring_pairs[step])
+        return lax.ppermute(value, FSDP, self.ring_pairs[step])
 
     def to_column(self, value):
         return self.to_partner(value, 0)
@@ -640,7 +776,7 @@
             return lax.ppermute(value, "tp", [(0, 1), (1, 0)])
         flip = 1 << (bit - 1)
         pairs = [(q * 2 + c, (q ^ flip) * 2 + c) for q in range(self.chips) for c in range(2)]
-        return lax.ppermute(value, "fsdp", pairs)
+        return lax.ppermute(value, FSDP, pairs)
 
     def side(self, bit):
         return self.column if bit == 0 else (self.chip >> (bit - 1)) & 1
@@ -853,8 +989,8 @@
     )(triple, triple, triple, head_out, log_total, mixed_grad)
 
 
-SWAPPED = ("w1", "u1", "i1", "s1")
-HALVED = {"u0": (1, 0, 2, 3), "w0": (2, 1, 0, 3)}
+SWAPPED = ("i1", "s1")
+HALVED = {"w1": (0, 2, 1, 3), "u1": (1, 0, 2, 3), "u0": (1, 0, 2, 3), "w0": (2, 1, 0, 3)}
 PLAN = (
     "+D0", "D0", "+P0", "+D1", "P0", "+R0", "D1", "+P1", "R0", "P1", "+R1", "+E", "R0", "+D2", "R1",
     "D2", "+P2", "R0", "R1", "P2", "+P3", "R0", "+U0", "R1", "E", "R1", "+W0", "skip 0", "U0", "full 0",
@@ -862,12 +998,13 @@
     "+U1", "second_norm 0", "W0", "+W1", "up 0", "U1", "down_held 0", "down 0", "W1", "full 1", "next 0",
     "U1", "hid 1", "W1", "qkv 1", "U1", "attend 1", "W1", "out 1", "U1", "second_norm 1", "W1",
     "grad_rows 1", "up 1", "down_grad 1", "+w1", "down_held 1", "act 1", "second 1", "up_grad 1", "+u1",
-    "middle 1", "mixed 1", "out_grad 1", "heads0 1", "w1", "heads1 1", "first 1", "qkv_grad 1", "+i1",
-    "u1", "wu", "hidden_grad 1", "joined 1", "grad_rows 0", "skip_grad 1", "act 0", "skip_sum 1", "+s1",
-    "second 0", "up_grad 0", "+u0", "i1", "down_grad 0", "+w0", "down 1", "middle 0", "next 1", "+O",
-    "mixed 0", "out_grad 0", "s1", "is", "heads0 0", "u0", "O", "+G1", "heads1 0", "w0", "first 0",
-    "qkv_grad 0", "+i0", "u0", "G1", "hidden_grad 0", "i0", "skip_grad 0", "w0", "skip_sum 0", "+s0",
-    "i0", "joined 0", "+G0", "u0", "s0", "i0", "w0", "s0", "i0", "u0", "s0", "i0", "w0", "s0", "G0", "s0",
+    "middle 1", "mixed 1", "out_grad 1", "heads0 1", "heads1 1", "w1", "u1", "first 1",
+    "qkv_grad 1", "+i1", "hidden_grad 1", "joined 1", "w1", "grad_rows 0", "skip_grad 1", "u1", "act 0",
+    "w1", "u1", "skip_sum 1", "+s1", "second 0", "w1", "up_grad 0", "u1", "+u0", "down_grad 0",
+    "+w0", "middle 0", "mixed 0", "out_grad 0", "i1", "heads0 0", "u0", "s1", "is", "+G1", "heads1 0",
+    "w0", "first 0", "qkv_grad 0", "+i0", "u0", "hidden_grad 0", "i0", "G1", "skip_grad 0", "joined 0",
+    "+G0", "w0", "skip_sum 0", "+s0", "i0", "u0", "s0", "down 1", "i0", "w0", "s0", "next 1", "+O", "i0",
+    "s0", "u0", "i0", "s0", "G0", "w0", "s0", "O",
 )
 
 
@@ -976,7 +1113,7 @@
                 )
             )
             begin += LAYERS * size
-        values[6] = lax.dynamic_slice_in_dim(values[6], core * up_width, up_width)
+        values[6] = lax.dynamic_slice_in_dim(values[6], core * up_width, up_width, allow_negative_indices=False)
         return values
 
     weights = [{}, {}]
@@ -1256,23 +1393,23 @@
 
     def skip_grad_step(index):
         now = grads[index]
-        full = jnp.einsum(
-            "tc,te->ce",
-            kept[index]["joined"],
-            sequence.at(now["hidden_low"]),
-            preferred_element_type=f32,
-        ).astype(low_type)
-        now["skip_keep"] = lax.dynamic_slice_in_dim(full, core * skip_width, skip_width, 1)
-        send(
-            now,
-            "skip_other",
-            lax.dynamic_slice_in_dim(full, (1 - core) * skip_width, skip_width, 1),
-        )
+        low = sequence.at(now["hidden_low"])
+
+        def half(which):
+            columns = lax.dynamic_slice_in_dim(
+                low, which * skip_width, skip_width, 1, allow_negative_indices=False
+            )
+            return jnp.einsum(
+                "tc,te->ce", kept[index]["joined"], columns, preferred_element_type=f32
+            )
+
+        send(now, "skip_other", half(1 - core).astype(low_type))
+        now["skip_keep"] = half(core)
 
     def skip_sum_step(index):
         now = grads[index]
         other = received(now, "skip_other").astype(f32)
-        now["skip"] = sequence.mark((now["skip_keep"].astype(f32) + other).astype(low_type))
+        now["skip"] = sequence.mark((now["skip_keep"] + other).astype(low_type))
         slabs = now["skip"].reshape(-1, slab_rows, shard_rows, skip_width)
         sums["s%d" % index] = [
             slabs[:, i].reshape(-1, skip_width) for i in range(slab_rows)
@@ -1321,7 +1458,7 @@
                 pairs[key] = (blocks[key], net.to_column(sequence.at(blocks[key])))
             elif key[0] in "RUW":
                 gathers[key] = RingGather(net, sequence.at(blocks[key]))
-            elif key in ("w1", "u1", "i1", "s1"):
+            elif key in SWAPPED:
                 reduces[key] = Swap(net, sequence.at(sums[key]))
             else:
                 tensors = sequence.at(sums[key])
@@ -1352,7 +1489,7 @@
             own = jnp.concatenate([v for swap in chosen for v in swap.tensors], 1)
             other = sequence.at([v for swap in chosen for v in swap.coming])
             operand = sequence.mark(net.choose(own, jnp.concatenate(other, 1)))
-            summed[item] = lax.psum_scatter(operand, "fsdp", scatter_dimension=0, tiled=True)
+            summed[item] = lax.psum_scatter(operand, FSDP, scatter_dimension=0, tiled=True)
     output = blocks["O"].astype(f32)
 
     def back(*keys):
@@ -1363,9 +1500,9 @@
             [value[:, i * skip_width : (i + 1) * skip_width] for i in range(slab_rows)], 0
         )
 
-    second_one = summed["wu"].astype(f32)
     first_one = summed["is"].astype(f32)
     second_zero = back("w0", "u0")
+    second_one = back("w1", "u1")
     inner_zero = back("i0")
     skip_zero = back("s0")
     inner_one = first_one[:, : qkv_width + out_width]
@@ -1388,7 +1525,7 @@
     parts = []
     for now in grads:
         full = jnp.zeros((2 * up_width,), f32)
-        now["up_bias"] = lax.dynamic_update_slice_in_dim(full, now["up_bias"], core * up_width, 0)
+        now["up_bias"] = lax.dynamic_update_slice_in_dim(full, now["up_bias"], core * up_width, 0, allow_negative_indices=False)
         parts += [now[name].astype(f32).reshape(2 * fsdp_size, -1) for name in names]
     small_sums = net.sum_small(jnp.concatenate(parts, 1)).reshape(LAYERS, -1)
     small_out, begin = ({}, 0)
@@ -1416,45 +1553,22 @@
 
 
 def solution(mesh):
-    placed = (
-        P(("fsdp", "tp"), None),
-        P(None, ("fsdp", "tp"), None),
-        P(None, "fsdp", "tp"),
-        P(None, ("fsdp", "tp")),
-        P(None, ("fsdp", "tp")),
-        P(None, ("fsdp", "tp")),
-        P(None, "fsdp", None, "tp"),
-        P(None, "tp", "fsdp"),
-        P(None, ("fsdp", "tp")),
-        P(None, ("fsdp", "tp")),
-        P(None, ("fsdp", "tp")),
-        P(None, "fsdp", "tp"),
-        P(None, ("fsdp", "tp")),
-        P(None, "tp", "fsdp"),
-        P(None, ("fsdp", "tp")),
-        P(("fsdp", "tp"), None),
-    )
+    fsdp, tensor, body = ("fsdp", "tp", general_body)
+    size = mesh.shape["fsdp"]
+    if mesh.shape["tp"] == 2 and size >= 4 and size & (size - 1) == 0:
+        mesh = Mesh(mesh.devices.reshape(size // 2, 2, 2), BOTH)
+        fsdp, body = (FSDP, lambda *arrays: fast_body(size, *arrays))
+    both = (*(fsdp if fsdp == FSDP else (fsdp,)), tensor)
+    tokens, vector = (P(both, None), P(None, both))
+    layers = P(None, both, None)
+    rows, columns = (P(None, fsdp, tensor), P(None, tensor, fsdp))
+    qkv = P(None, fsdp, None, tensor)
+    weights = (rows, vector, vector, vector, qkv, columns, vector, vector, vector)
+    weights += (rows, vector, columns, vector)
     return jax.shard_map(
-        choose_body(mesh),
+        body,
         mesh=mesh,
-        in_specs=placed,
-        out_specs=(
-            P(("fsdp", "tp"), None),
-            P(("fsdp", "tp"), None),
-            P(None, ("fsdp", "tp"), None),
-            P(None, "fsdp", "tp"),
-            P(None, ("fsdp", "tp")),
-            P(None, ("fsdp", "tp")),
-            P(None, ("fsdp", "tp")),
-            P(None, "fsdp", None, "tp"),
-            P(None, "tp", "fsdp"),
-            P(None, ("fsdp", "tp")),
-            P(None, ("fsdp", "tp")),
-            P(None, ("fsdp", "tp")),
-            P(None, "fsdp", "tp"),
-            P(None, ("fsdp", "tp")),
-            P(None, "tp", "fsdp"),
-            P(None, ("fsdp", "tp")),
-        ),
+        in_specs=(tokens, layers, *weights, tokens),
+        out_specs=(tokens, tokens, layers, *weights),
         check_vma=False,
     )

time: 973 us -> 951 us (0.977)
  starting transfers between devices: 159 us -> 183 us
  waiting for transfers between devices: 255 us -> 233 us
  between operations: 33.6 us -> 17.8 us
  other arithmetic: 132 us -> 119 us
    ppermute x95 -> x101, waiting for transfers between devices: 200 us -> 179 us  [the longest x64 148 us: along_ring(): return lax.ppermute(value, FSDP, self.ring_pairs[step])]
    ppermute x17 -> x16, starting transfers between devices: 63.7 us -> 75.7 us  [diagonal_other(): return lax.ppermute(value, BOTH, self.diagonal_pairs)]
    select_n x9 -> x8, other arithmetic: 31.1 us -> 19.3 us  [choose(): return jnp.where(self.core == self.column, own, other)]
    ppermute x95 -> x101, starting transfers between devices: 90.4 us -> 101 us  [the longest x64 57.9 us: along_ring(): return lax.ppermute(value, FSDP, self.ring_pairs[step])]
    ppermute x17 -> x16, waiting for transfers between devices: 37.2 us -> 30.8 us  [diagonal_other(): return lax.ppermute(value, BOTH, self.diagonal_pairs)]
    ppermute x9 -> x11, waiting for transfers between devices: 17.3 us -> 23.2 us  [to_partner(): return lax.ppermute(value, 'tp', [(0, 1), (1, 0)])]
    unnamed x430 -> x408, local copies, waits for them, and re-layouts: 35.9 us -> 32.5 us
  transfers between devices with their start and end apart: 123 -> 129, of which waited for: 49 -> 49; matrix products, arithmetic and copies ran while one was open for 30% -> 29% of each run, Pallas kernels for 13% -> 15%
where the time goes in v3:
time: 951 us; the launch traced here: 940 us
  waiting for transfers between devices  233 us (25%)
  starting transfers between devices  183 us (19%)
  matrix products  151 us (16%)
  Pallas kernels  136 us (14%)
  other arithmetic  119 us (13%)
  local copies, waits for them, and re-layouts  99 us (10%)
  between operations  17.8 us (2%)
    ppermute x64, waiting for transfers between devices, along_ring(): return lax.ppermute(value, FSDP, self.ring_pairs[step])  148 us
    pallas_call x4, Pallas kernels, attention_backward(): pl.pallas_call(kernel, grid=(pair_count,), in_specs=[part(0), part(1), pa...  77.9 us
    ppermute x16, starting transfers between devices, diagonal_other(): return lax.ppermute(value, BOTH, self.diagonal_pairs)  75.7 us
    ppermute x64, starting transfers between devices, along_ring(): return lax.ppermute(value, FSDP, self.ring_pairs[step])  57.9 us
    pallas_call x2, Pallas kernels, attention_forward(): pl.pallas_call(kernel, grid=(pairs,), in_specs=[part(0), part(1), part(2)...  37.9 us
    unnamed x408, local copies, waits for them, and re-layouts  32.5 us
    ppermute x16, waiting for transfers between devices, diagonal_other(): return lax.ppermute(value, BOTH, self.diagonal_pairs)  30.8 us
    ppermute x22, starting transfers between devices, to_core(): return lax.ppermute(value, FSDP, self.core_pairs)  28.2 us
  transfers between devices with their start and end apart: 129, of which 49 were waited for; matrix products, arithmetic and copies ran while one was open for 29% of the time, Pallas kernels for 15%

profile of v3, /device:TPU:1, one launch (start us, length us, event | category | flops | bytes accessed | tf_op | source)
XLA Modules:
  0.0 939.7 jit_solution(3684551029012783546)
XLA Ops:
  15.4 5.5 collective-permute-done
  24.8 7.3 collective-permute-done.2
  33.7 8.7 collective-permute-done.1
  42.6 8.3 collective-permute-done.4.refs_2_
  55.1 14.3 %collective-permute-done.10.refs_5_ = bf16[128,3200]{1,0:T(8,128)(2,1)} collective-permute-done((bf16[128,3200]{1,0:T(8,128)(2,1)S(1)}, bf16[128,3200]{1,0:T(8,128)(2,1)}, u32[]{:S(2)}, u32[]{:S(2)}) %collective-permute-start.10) | collective-permute-done | bytes 819232 | tf_op jit(solution)/shard_map/ppermute | solution.py:760
  69.6 9.2 collective-permute-start.15
  80.3 6.1 collective-permute-done.7.refs_2_
  93.8 10.2 %collective-permute-done.13.refs_0_ = bf16[128,3200]{1,0:T(8,128)(2,1)S(1)} collective-permute-done((bf16[128,3200]{1,0:T(8,128)(2,1)S(1)}, bf16[128,3200]{1,0:T(8,128)(2,1)S(1)}, u32[]{:S(2)}, u32[]{:S(2)}) %collective-permute-start.13) | collective-permute-done | bytes 819232 | tf_op jit(solution)/shard_map/ppermute | solution.py:760
  104.0 9.2 collective-permute-start.6
  136.1 6.6 collective-permute-start.26
  160.2 8.3 collective-permute-done.22.refs_7_
  176.1 5.2 maximum_select_fusion.1
  181.3 5.1 collective-permute-done.24.refs_2_
  201.7 7.0 collective-permute-done.31.refs_1_
  226.5 4.9 convolution_convert_fusion.1.query_ref.key_ref.value_ref
  236.0 18.9 %shard_map.344 = (bf16[1104,512]{1,0:T(8,128)(2,1)S(1)}, f32[4,2,1104]{2,1,0:T(2,128)S(1)}) custom-call(bf16[1104,1536]{1,0:T(8,128)(2,1)S(1)} %convolution_convert_fusion.1.query_ref.key_ref.value_ref, bf16[1104,1536]{1,0:T(8,128)(2,1)S(1)} %convolution_convert_fusion.1.query_ref.key_ref.value_ref, ...), custom_call_target="tpu_custom_call" | custom-call | flops 4992270336 | bytes 4521984 | tf_op jit(solution)/shard_map/pallas_call | solution.py:890
  264.9 6.6 collective-permute-done.41.refs_7_
  294.3 9.9 %multiply_convert_fusion.1 = (bf16[1104,2048]{1,0:T(8,128)(2,1)S(1)}, f32[1104,2048]{1,0:T(8,128)}) fusion(f32[2048]{0:T(1024)S(1)} %dynamic-slice_convert_fusion.3, bf16[1024,2048]{1,0:T(8,128)(2,1)S(1)} %shard_map.345, bf16[552,1024]{1,0:T(8,128)(2,1)} %collective-permute-done.43, bf16[552,1024]{1,0:T(8,128)(2,1)} %add_convert_fusion.4), kind=kOutput, calls=%fused_computation.18 | convolution fusion | flops 4648599552 | bytes 20029440 | tf_op jit(solution)/shard_map/dot_general | solution.py:1208
  317.8 7.5 collective-permute-done.50.refs_2_
  330.6 5.9 collective-permute-done.52.refs_1_
  346.3 10.8 %collective-permute-done.55.refs_1_ = bf16[128,2048]{1,0:T(8,128)(2,1)S(1)} collective-permute-done((bf16[128,2048]{1,0:T(8,128)(2,1)}, bf16[128,2048]{1,0:T(8,128)(2,1)S(1)}, u32[]{:S(2)}, u32[]{:S(2)}) %collective-permute-start.55) | collective-permute-done | bytes 524320 | tf_op jit(solution)/shard_map/ppermute | solution.py:760
  359.8 4.9 convolution_convert_fusion.query_ref.key_ref.value_ref
  368.3 18.9 %shard_map.347 = (bf16[1104,512]{1,0:T(8,128)(2,1)S(1)}, f32[4,2,1104]{2,1,0:T(2,128)S(1)}) custom-call(bf16[1104,1536]{1,0:T(8,128)(2,1)S(1)} %convolution_convert_fusion.query_ref.key_ref.value_ref, bf16[1104,1536]{1,0:T(8,128)(2,1)S(1)} %convolution_convert_fusion.query_ref.key_ref.value_ref, ...), custom_call_target="tpu_custom_call" | custom-call | flops 4992270336 | bytes 4521984 | tf_op jit(solution)/shard_map/pallas_call | solution.py:890
  423.8 8.3 multiply_convert_fusion
  432.1 6.1 convolution_convert_fusion.5
  438.4 8.2 fusion.81
  454.6 6.5 convolution_convert_fusion.4
  487.4 19.2 %shard_map.350 = (bf16[1104,256]{1,0:T(8,128)(2,1)S(1)}, bf16[1104,256]{1,0:T(8,128)(2,1)S(1)}, bf16[1104,256]{1,0:T(8,128)(2,1)S(1)}) custom-call(bf16[1104,1536]{1,0:T(8,128)(2,1)} %copy-done.68, bf16[1104,1536]{1,0:T(8,128)(2,1)} %copy-done.68, bf16[1104,1536]{1,0:T(8,128)(2,1)} %copy-done.68, bf16[1104,512]{1,0:T(8,128)(2,1)S(1)} %copy-done.66, ...), custom_call_target="tpu_custom_call" | custom-call | flops 6240337920 | bytes 4521984 | tf_op jit(solution)/shard_map/pallas_call | solution.py:969
  506.7 19.7 %shard_map.351 = (bf16[1104,256]{1,0:T(8,128)(2,1)S(1)}, bf16[1104,256]{1,0:T(8,128)(2,1)S(1)}, bf16[1104,256]{1,0:T(8,128)(2,1)S(1)}) custom-call(bf16[1104,1536]{1,0:T(8,128)(2,1)} %copy-done.68, bf16[1104,1536]{1,0:T(8,128)(2,1)} %copy-done.68, bf16[1104,1536]{1,0:T(8,128)(2,1)} %copy-done.68, bf16[1104,512]{1,0:T(8,128)(2,1)S(1)} %copy-done.66, ...), custom_call_target="tpu_custom_call" | custom-call | flops 6240337920 | bytes 4521984 | tf_op jit(solution)/shard_map/pallas_call | solution.py:969
  540.8 5.8 convolution_convert_fusion.7
  576.6 10.0 %fusion.82 = (f32[2048]{0:T(1024)S(1)}, bf16[1104,2048]{1,0:T(8,128)(2,1)S(1)}) fusion(f32[1104,2048]{1,0:T(8,128)} %get-tuple-element.598, bf16[1024,2048]{1,0:T(8,128)(2,1)S(1)} %copy-done.7, bf16[552,1024]{1,0:T(8,128)(2,1)} %collective-permute-done.73, bf16[552,1024]{1,0:T(8,128)(2,1)S(1)} %get-tuple-element.513), kind=kOutput, calls=%fused_computation.349 | convolution fusion | flops 4664424448 | bytes 20029440 | tf_op jit(solution)/shard_map/dot_general | solution.py:1269
  602.3 5.9 collective-permute-done.81
  608.2 6.1 convolution_convert_fusion.3
  618.9 6.2 convolution_convert_fusion.2
  640.9 9.2 collective-permute-done.127
  663.0 19.7 %shard_map.352 = (bf16[1104,256]{1,0:T(8,128)(2,1)S(1)}, bf16[1104,256]{1,0:T(8,128)(2,1)S(1)}, bf16[1104,256]{1,0:T(8,128)(2,1)S(1)}) custom-call(bf16[1104,1536]{1,0:T(8,128)(2,1)} %copy-done.67, bf16[1104,1536]{1,0:T(8,128)(2,1)} %copy-done.67, bf16[1104,1536]{1,0:T(8,128)(2,1)} %copy-done.67, bf16[1104,512]{1,0:T(8,128)(2,1)S(1)} %copy-done.64, ...), custom_call_target="tpu_custom_call" | custom-call | flops 6240337920 | bytes 4521984 | tf_op jit(solution)/shard_map/pallas_call | solution.py:969
  686.4 7.7 maximum_select_fusion
  695.7 19.4 %shard_map.353 = (bf16[1104,256]{1,0:T(8,128)(2,1)S(1)}, bf16[1104,256]{1,0:T(8,128)(2,1)S(1)}, bf16[1104,256]{1,0:T(8,128)(2,1)S(1)}) custom-call(bf16[1104,1536]{1,0:T(8,128)(2,1)} %copy-done.67, bf16[1104,1536]{1,0:T(8,128)(2,1)} %copy-done.67, bf16[1104,1536]{1,0:T(8,128)(2,1)} %copy-done.67, bf16[1104,512]{1,0:T(8,128)(2,1)S(1)} %copy-done.64, ...), custom_call_target="tpu_custom_call" | custom-call | flops 6240337920 | bytes 4521984 | tf_op jit(solution)/shard_map/pallas_call | solution.py:969
  724.7 6.7 convolution_convert_fusion.6.refs_0_.refs_2_
  741.8 6.8 collective-permute-done.90
  767.8 5.0 convolution_convert_fusion.9
  778.7 19.8 %collective-permute-done.121 = f32[8,704]{1,0:T(8,128)S(1)} collective-permute-done((f32[8,704]{1,0:T(8,128)S(1)}, f32[8,704]{1,0:T(8,128)S(1)}, u32[]{:S(2)}, u32[]{:S(2)}) %collective-permute-start.121) | collective-permute-done | bytes 22560 | tf_op jit(solution)/shard_map/ppermute | solution.py:779
  825.6 7.6 collective-permute-done.96.refs_4_
  848.4 5.7 collective-permute-done.102.refs_4_
  854.0 6.6 collective-permute-start.110
  864.4 6.8 collective-permute-done.110
  882.1 12.5 %collective-permute-start.107 = (bf16[552,1024]{1,0:T(8,128)(2,1)S(1)}, bf16[552,1024]{1,0:T(8,128)(2,1)}, u32[]{:S(2)}, u32[]{:S(2)}) collective-permute-start(bf16[552,1024]{1,0:T(8,128)(2,1)S(1)} %fusion.16), channel_id=1, source_target_pairs={{2,1},{1,2},{6,5},{5,6},{10,9},{9,10},{14,13},{13,14},{18,17},{17,... | collective-permute-start | bytes 3391496 | tf_op jit(solution)/shard_map/ppermute | solution.py:766
  907.3 5.6 collective-permute-done.116
  (919 shorter events, 481.7 us)
Async XLA Ops:
  7.3 920.1 %reduce-scatter.2.cloned.1.call-start = ((), (), s32[]{:S(2)}) async-start(), calls=%async_computation.1 | async-start | bytes 6684672 | tf_op jit(solution)/shard_map/reduce_scatter | solution.py:1492
  53.6 32.9 %collective-permute-start.7 = (bf16[128,3072]{1,0:T(8,128)(2,1)S(1)}, bf16[128,3072]{1,0:T(8,128)(2,1)}, u32[]{:S(2)}, u32[]{:S(2)}) collective-permute-start(bf16[128,3072]{1,0:T(8,128)(2,1)S(1)} %maximum_select_fusion.6.refs_3_), channel_id=1, source_target_pairs={{0,8},{2,10},{8,16},{10,18},{16,24},{18,26},{24,28},{26,30},{28,20... | collective-permute-start | bytes 2359304 | tf_op jit(solution)/shard_map/ppermute | solution.py:760
  54.9 31.5 %collective-permute-start.8 = (bf16[128,3072]{1,0:T(8,128)(2,1)S(1)}, bf16[128,3072]{1,0:T(8,128)(2,1)}, u32[]{:S(2)}, u32[]{:S(2)}) collective-permute-start(bf16[128,3072]{1,0:T(8,128)(2,1)S(1)} %maximum_select_fusion.6.refs_3_), channel_id=1, source_target_pairs={{0,4},{2,6},{8,0},{10,2},{16,8},{18,10},{24,16},{26,18},{28,24},{3... | collective-permute-start | bytes 2359304 | tf_op jit(solution)/shard_map/ppermute | solution.py:760
  78.8 25.2 %collective-permute-start.13 = (bf16[128,3200]{1,0:T(8,128)(2,1)S(1)}, bf16[128,3200]{1,0:T(8,128)(2,1)S(1)}, u32[]{:S(2)}, u32[]{:S(2)}) collective-permute-start(bf16[128,3200]{1,0:T(8,128)(2,1)S(1)} %collective-permute-done.9.refs_1_), channel_id=1, source_target_pairs={{0,8},{2,10},{8,16},{10,18},{16,24},{18,26},{24,28},{26,30},{28,20... | collective-permute-start | bytes 2457608 | tf_op jit(solution)/shard_map/ppermute | solution.py:760
  80.3 35.7 %collective-permute-start.14 = (bf16[128,3200]{1,0:T(8,128)(2,1)}, bf16[128,3200]{1,0:T(8,128)(2,1)S(1)}, u32[]{:S(2)}, u32[]{:S(2)}) collective-permute-start(bf16[128,3200]{1,0:T(8,128)(2,1)} %collective-permute-done.10.refs_5_), channel_id=1, source_target_pairs={{0,4},{2,6},{8,0},{10,2},{16,8},{18,10},{24,16},{26,18},{28,24},{3... | collective-permute-start | bytes 2457608 | tf_op jit(solution)/shard_map/ppermute | solution.py:760
  86.4 34.4 %collective-permute-start.11 = (bf16[128,3072]{1,0:T(8,128)(2,1)}, bf16[128,3072]{1,0:T(8,128)(2,1)}, u32[]{:S(2)}, u32[]{:S(2)}) collective-permute-start(bf16[128,3072]{1,0:T(8,128)(2,1)} %collective-permute-done.7.refs_2_), channel_id=1, source_target_pairs={{0,8},{2,10},{8,16},{10,18},{16,24},{18,26},{24,28},{26,30},{28,20... | collective-permute-start | bytes 2359304 | tf_op jit(solution)/shard_map/ppermute | solution.py:760
  87.6 34.3 %collective-permute-start.12 = (bf16[128,3072]{1,0:T(8,128)(2,1)}, bf16[128,3072]{1,0:T(8,128)(2,1)}, u32[]{:S(2)}, u32[]{:S(2)}) collective-permute-start(bf16[128,3072]{1,0:T(8,128)(2,1)} %collective-permute-done.8.refs_4_), channel_id=1, source_target_pairs={{0,4},{2,6},{8,0},{10,2},{16,8},{18,10},{24,16},{26,18},{28,24},{3... | collective-permute-start | bytes 2359304 | tf_op jit(solution)/shard_map/ppermute | solution.py:760
  88.8 34.4 %collective-permute-start.20 = (bf16[64,4096]{1,0:T(8,128)(2,1)}, bf16[64,4096]{1,0:T(8,128)(2,1)}, u32[]{:S(2)}, u32[]{:S(2)}) collective-permute-start(bf16[64,4096]{1,0:T(8,128)(2,1)} %broadcast_select_fusion.5), channel_id=1, source_target_pairs={{0,1},{1,0},{2,3},{3,2},{4,5},{5,4},{6,7},{7,6},{8,9},{9,8},{10,11... | collective-permute-start | bytes 1572872 | tf_op jit(solution)/shard_map/ppermute | solution.py:776
  104.0 51.4 %collective-permute-start.6 = (bf16[552,2048]{1,0:T(8,128)(2,1)}, bf16[552,2048]{1,0:T(8,128)(2,1)}, u32[]{:S(2)}, u32[]{:S(2)}) collective-permute-start(bf16[552,2048]{1,0:T(8,128)(2,1)} %get-tuple-element.238), channel_id=1, source_target_pairs={{2,1},{1,2},{6,5},{5,6},{10,9},{9,10},{14,13},{13,14},{18,17},{17,... | collective-permute-start | bytes 6782984 | tf_op jit(solution)/shard_map/ppermute | solution.py:766
  121.9 30.8 %collective-permute-start.16 = (bf16[128,3072]{1,0:T(8,128)(2,1)}, bf16[128,3072]{1,0:T(8,128)(2,1)}, u32[]{:S(2)}, u32[]{:S(2)}) collective-permute-start(bf16[128,3072]{1,0:T(8,128)(2,1)} %collective-permute-done.11.refs_1_), channel_id=1, source_target_pairs={{0,8},{2,10},{8,16},{10,18},{16,24},{18,26},{24,28},{26,30},{28,20... | collective-permute-start | bytes 2359304 | tf_op jit(solution)/shard_map/ppermute | solution.py:760
  123.2 30.1 %collective-permute-start.17 = (bf16[128,3072]{1,0:T(8,128)(2,1)}, bf16[128,3072]{1,0:T(8,128)(2,1)}, u32[]{:S(2)}, u32[]{:S(2)}) collective-permute-start(bf16[128,3072]{1,0:T(8,128)(2,1)} %collective-permute-done.12.refs_5_), channel_id=1, source_target_pairs={{0,4},{2,6},{8,0},{10,2},{16,8},{18,10},{24,16},{26,18},{28,24},{3... | collective-permute-start | bytes 2359304 | tf_op jit(solution)/shard_map/ppermute | solution.py:760
  136.1 40.0 %collective-permute-start.26 = (bf16[2048,512]{1,0:T(8,128)(2,1)}, bf16[2048,512]{1,0:T(8,128)(2,1)}, u32[]{:S(2)}, u32[]{:S(2)}) collective-permute-start(bf16[2048,512]{1,0:T(8,128)(2,1)} %get-tuple-element.261), channel_id=1, source_target_pairs={{0,2},{2,0},{4,6},{6,4},{8,10},{10,8},{12,14},{14,12},{16,18},{18,... | collective-permute-start | bytes 6291464 | tf_op jit(solution)/shard_map/ppermute | solution.py:754
  146.7 28.8 %collective-permute-start.27 = (bf16[128,2048]{1,0:T(8,128)(2,1)S(1)}, bf16[128,2048]{1,0:T(8,128)(2,1)S(1)}, u32[]{:S(2)}, u32[]{:S(2)}) collective-permute-start(bf16[128,2048]{1,0:T(8,128)(2,1)S(1)} %get-tuple-element.262.refs_3_), channel_id=1, source_target_pairs={{0,8},{2,10},{8,16},{10,18},{16,24},{18,26},{24,28},{26,30},{28,20... | collective-permute-start | bytes 1572872 | tf_op jit(solution)/shard_map/ppermute | solution.py:760
  192.7 33.3 %collective-permute-start.30 = (bf16[552,1024]{1,0:T(8,128)(2,1)S(1)}, bf16[552,1024]{1,0:T(8,128)(2,1)S(1)}, u32[]{:S(2)}, u32[]{:S(2)}) collective-permute-start(bf16[552,1024]{1,0:T(8,128)(2,1)S(1)} %add_convert_fusion.5), channel_id=1, source_target_pairs={{0,2},{2,0},{4,6},{6,4},{8,10},{10,8},{12,14},{14,12},{16,18},{18,... | collective-permute-start | bytes 3391496 | tf_op jit(solution)/shard_map/ppermute | solution.py:754
  196.5 58.6 %collective-permute-start.35 = (bf16[552,2048]{1,0:T(8,128)(2,1)}, bf16[552,2048]{1,0:T(8,128)(2,1)}, u32[]{:S(2)}, u32[]{:S(2)}) collective-permute-start(bf16[552,2048]{1,0:T(8,128)(2,1)} %get-tuple-element.280), channel_id=1, source_target_pairs={{2,1},{1,2},{6,5},{5,6},{10,9},{9,10},{14,13},{13,14},{18,17},{17,... | collective-permute-start | bytes 6782984 | tf_op jit(solution)/shard_map/ppermute | solution.py:766
  224.8 30.2 %collective-permute-start.38 = (bf16[128,2048]{1,0:T(8,128)(2,1)S(1)}, bf16[128,2048]{1,0:T(8,128)(2,1)S(1)}, u32[]{:S(2)}, u32[]{:S(2)}) collective-permute-start(bf16[128,2048]{1,0:T(8,128)(2,1)S(1)} %collective-permute-done.36.refs_1_), channel_id=1, source_target_pairs={{0,8},{2,10},{8,16},{10,18},{16,24},{18,26},{24,28},{26,30},{28,20... | collective-permute-start | bytes 1572872 | tf_op jit(solution)/shard_map/ppermute | solution.py:760
  226.0 29.0 %collective-permute-start.39 = (bf16[128,2048]{1,0:T(8,128)(2,1)S(1)}, bf16[128,2048]{1,0:T(8,128)(2,1)S(1)}, u32[]{:S(2)}, u32[]{:S(2)}) collective-permute-start(bf16[128,2048]{1,0:T(8,128)(2,1)S(1)} %collective-permute-done.37.refs_5_), channel_id=1, source_target_pairs={{0,4},{2,6},{8,0},{10,2},{16,8},{18,10},{24,16},{26,18},{28,24},{3... | collective-permute-start | bytes 1572872 | tf_op jit(solution)/shard_map/ppermute | solution.py:760
  279.7 46.3 %collective-permute-start.49 = (bf16[2048,512]{1,0:T(8,128)(2,1)}, bf16[2048,512]{1,0:T(8,128)(2,1)}, u32[]{:S(2)}, u32[]{:S(2)}) collective-permute-start(bf16[2048,512]{1,0:T(8,128)(2,1)} %copy-done.8), channel_id=1, source_target_pairs={{0,2},{2,0},{4,6},{6,4},{8,10},{10,8},{12,14},{14,12},{16,18},{18,... | collective-permute-start | bytes 6291464 | tf_op jit(solution)/shard_map/ppermute | solution.py:754
  357.1 30.2 %collective-permute-start.59 = (bf16[128,2048]{1,0:T(8,128)(2,1)S(1)}, bf16[128,2048]{1,0:T(8,128)(2,1)S(1)}, u32[]{:S(2)}, u32[]{:S(2)}) collective-permute-start(bf16[128,2048]{1,0:T(8,128)(2,1)S(1)} %collective-permute-done.55.refs_1_), channel_id=1, source_target_pairs={{0,8},{2,10},{8,16},{10,18},{16,24},{18,26},{24,28},{26,30},{28,20... | collective-permute-start | bytes 1572872 | tf_op jit(solution)/shard_map/ppermute | solution.py:760
  357.2 30.1 %collective-permute-start.60 = (bf16[128,2048]{1,0:T(8,128)(2,1)S(1)}, bf16[128,2048]{1,0:T(8,128)(2,1)S(1)}, u32[]{:S(2)}, u32[]{:S(2)}) collective-permute-start(bf16[128,2048]{1,0:T(8,128)(2,1)S(1)} %collective-permute-done.56.refs_5_), channel_id=1, source_target_pairs={{0,4},{2,6},{8,0},{10,2},{16,8},{18,10},{24,16},{26,18},{28,24},{3... | collective-permute-start | bytes 1572872 | tf_op jit(solution)/shard_map/ppermute | solution.py:760
  472.4 54.0 %collective-permute-start.71 = (bf16[2,2,2,64,2048]{4,3,0,2,1:T(8,128)(2,1)}, bf16[2,2,2,64,2048]{4,3,0,2,1:T(8,128)(2,1)}, u32[]{:S(2)}, u32[]{:S(2)}) collective-permute-start(bf16[2,2,2,64,2048]{4,3,0,2,1:T(8,128)(2,1)} %bitcast.259), channel_id=1, source_target_pairs={{0,1},{1,0},{2,3},{3,2},{4,5},{5,4},{6,7},{7,6},{8,9},{9,8},{10,11... | collective-permute-start | bytes 6291464 | tf_op jit(solution)/shard_map/ppermute | solution.py:776
  477.7 51.3 %collective-permute-start.70 = (bf16[2,2,2,64,2048]{4,3,0,1,2:T(8,128)(2,1)}, bf16[2,2,2,64,2048]{4,3,0,1,2:T(8,128)(2,1)}, u32[]{:S(2)}, u32[]{:S(2)}) collective-permute-start(bf16[2,2,2,64,2048]{4,3,0,1,2:T(8,128)(2,1)} %bitcast.260), channel_id=1, source_target_pairs={{0,4},{2,6},{4,0},{6,2},{8,12},{10,14},{12,8},{14,10},{16,20},{18,... | collective-permute-start | bytes 6291464 | tf_op jit(solution)/shard_map/ppermute | solution.py:779
  539.2 24.8 %collective-permute-start.77 = (bf16[2,2,64,2048]{3,2,0,1:T(8,128)(2,1)S(1)}, bf16[2,2,64,2048]{3,2,0,1:T(8,128)(2,1)S(1)}, u32[]{:S(2)}, u32[]{:S(2)}) collective-permute-start(bf16[2,2,64,2048]{3,2,0,1:T(8,128)(2,1)S(1)} %dynamic-slice_bitcast_fusion.2), channel_id=1, source_target_pairs={{0,8},{2,10},{4,12},{6,14},{8,0},{10,2},{12,4},{14,6},{16,24},{18,... | collective-permute-start | bytes 3145736 | tf_op jit(solution)/shard_map/ppermute | solution.py:779
  540.8 27.8 %collective-permute-start.74 = (bf16[2,2,64,2048]{3,2,0,1:T(8,128)(2,1)S(1)}, bf16[2,2,64,2048]{3,2,0,1:T(8,128)(2,1)S(1)}, u32[]{:S(2)}, u32[]{:S(2)}) collective-permute-start(bf16[2,2,64,2048]{3,2,0,1:T(8,128)(2,1)S(1)} %dynamic-slice_bitcast_fusion.3), channel_id=1, source_target_pairs={{0,1},{1,0},{2,3},{3,2},{4,5},{5,4},{6,7},{7,6},{8,9},{9,8},{10,11... | collective-permute-start | bytes 3145736 | tf_op jit(solution)/shard_map/ppermute | solution.py:776
  546.7 116.3 %collective-permute-start.83 = (bf16[1024,1536]{1,0:T(8,128)(2,1)}, bf16[1024,1536]{1,0:T(8,128)(2,1)}, u32[]{:S(2)}, u32[]{:S(2)}) collective-permute-start(bf16[1024,1536]{1,0:T(8,128)(2,1)} %convolution_convert_fusion.7), channel_id=1, source_target_pairs={{2,1},{1,2},{6,5},{5,6},{10,9},{9,10},{14,13},{13,14},{18,17},{17,... | collective-permute-start | bytes 9437192 | tf_op jit(solution)/shard_map/ppermute | solution.py:766
  550.6 112.4 %collective-permute-start.84 = (bf16[1024,512]{1,0:T(8,128)(2,1)}, bf16[1024,512]{1,0:T(8,128)(2,1)}, u32[]{:S(2)}, u32[]{:S(2)}) collective-permute-start(bf16[1024,512]{1,0:T(8,128)(2,1)} %convolution_convert_fusion.14), channel_id=1, source_target_pairs={{2,1},{1,2},{6,5},{5,6},{10,9},{9,10},{14,13},{13,14},{18,17},{17,... | collective-permute-start | bytes 3145736 | tf_op jit(solution)/shard_map/ppermute | solution.py:766
  590.1 24.3 %collective-permute-start.80 = (bf16[64,2048]{1,0:T(8,128)(2,1)S(1)}, bf16[64,2048]{1,0:T(8,128)(2,1)S(1)}, u32[]{:S(2)}, u32[]{:S(2)}) collective-permute-start(bf16[64,2048]{1,0:T(8,128)(2,1)S(1)} %dynamic-slice_bitcast_fusion.13), channel_id=1, source_target_pairs={{0,16},{2,18},{4,20},{6,22},{8,24},{10,26},{12,28},{14,30},{16,0},... | collective-permute-start | bytes 786440 | tf_op jit(solution)/shard_map/ppermute | solution.py:779
  600.8 33.9 %collective-permute-start.79 = (bf16[552,1024]{1,0:T(8,128)(2,1)S(1)}, bf16[552,1024]{1,0:T(8,128)(2,1)S(1)}, u32[]{:S(2)}, u32[]{:S(2)}) collective-permute-start(bf16[552,1024]{1,0:T(8,128)(2,1)S(1)} %slice.766), channel_id=1, source_target_pairs={{0,2},{2,0},{4,6},{6,4},{8,10},{10,8},{12,14},{14,12},{16,18},{18,... | collective-permute-start | bytes 3391496 | tf_op jit(solution)/shard_map/ppermute | solution.py:754
  617.7 64.9 %collective-permute-start.87 = (bf16[2,2,2,64,2048]{4,3,0,1,2:T(8,128)(2,1)}, bf16[2,2,2,64,2048]{4,3,0,1,2:T(8,128)(2,1)}, u32[]{:S(2)}, u32[]{:S(2)}) collective-permute-start(bf16[2,2,2,64,2048]{4,3,0,1,2:T(8,128)(2,1)} %bitcast.258), channel_id=1, source_target_pairs={{0,4},{2,6},{4,0},{6,2},{8,12},{10,14},{12,8},{14,10},{16,20},{18,... | collective-permute-start | bytes 6291464 | tf_op jit(solution)/shard_map/ppermute | solution.py:779
  626.7 59.7 %collective-permute-start.85 = (bf16[1024,512]{1,0:T(8,128)(2,1)}, bf16[1024,512]{1,0:T(8,128)(2,1)}, u32[]{:S(2)}, u32[]{:S(2)}) collective-permute-start(bf16[1024,512]{1,0:T(8,128)(2,1)} %bitcast.43), channel_id=1, source_target_pairs={{2,1},{1,2},{6,5},{5,6},{10,9},{9,10},{14,13},{13,14},{18,17},{17,... | collective-permute-start | bytes 3145736 | tf_op jit(solution)/shard_map/ppermute | solution.py:766
  653.0 33.4 %collective-permute-start.86 = (bf16[1024,512]{1,0:T(8,128)(2,1)}, bf16[1024,512]{1,0:T(8,128)(2,1)S(1)}, u32[]{:S(2)}, u32[]{:S(2)}) collective-permute-start(bf16[1024,512]{1,0:T(8,128)(2,1)} %bitcast.44), channel_id=1, source_target_pairs={{2,1},{1,2},{6,5},{5,6},{10,9},{9,10},{14,13},{13,14},{18,17},{17,... | collective-permute-start | bytes 3145736 | tf_op jit(solution)/shard_map/ppermute | solution.py:766
  663.0 52.1 %collective-permute-start.88 = (bf16[2,2,2,64,2048]{4,3,0,2,1:T(8,128)(2,1)}, bf16[2,2,2,64,2048]{4,3,0,2,1:T(8,128)(2,1)}, u32[]{:S(2)}, u32[]{:S(2)}) collective-permute-start(bf16[2,2,2,64,2048]{4,3,0,2,1:T(8,128)(2,1)} %bitcast.257), channel_id=1, source_target_pairs={{0,8},{2,10},{4,12},{6,14},{8,0},{10,2},{12,4},{14,6},{16,24},{18,... | collective-permute-start | bytes 6291464 | tf_op jit(solution)/shard_map/ppermute | solution.py:779
  724.1 25.9 %collective-permute-start.89 = (bf16[552,1024]{1,0:T(8,128)(2,1)S(1)}, bf16[552,1024]{1,0:T(8,128)(2,1)S(1)}, u32[]{:S(2)}, u32[]{:S(2)}) collective-permute-start(bf16[552,1024]{1,0:T(8,128)(2,1)S(1)} %slice.765), channel_id=1, source_target_pairs={{0,2},{2,0},{4,6},{6,4},{8,10},{10,8},{12,14},{14,12},{16,18},{18,... | collective-permute-start | bytes 3391496 | tf_op jit(solution)/shard_map/ppermute | solution.py:754
  724.1 24.5 %collective-permute-start.90 = (bf16[2,2,64,2048]{3,2,0,1:T(8,128)(2,1)S(1)}, bf16[2,2,64,2048]{3,2,0,1:T(8,128)(2,1)S(1)}, u32[]{:S(2)}, u32[]{:S(2)}) collective-permute-start(bf16[2,2,64,2048]{3,2,0,1:T(8,128)(2,1)S(1)} %dynamic-slice_bitcast_fusion.1), channel_id=1, source_target_pairs={{0,1},{1,0},{2,3},{3,2},{4,5},{5,4},{6,7},{7,6},{8,9},{9,8},{10,11... | collective-permute-start | bytes 3145736 | tf_op jit(solution)/shard_map/ppermute | solution.py:776
  736.9 24.7 %collective-permute-start.91 = (bf16[552,1024]{1,0:T(8,128)(2,1)S(1)}, bf16[552,1024]{1,0:T(8,128)(2,1)S(1)}, u32[]{:S(2)}, u32[]{:S(2)}) collective-permute-start(bf16[552,1024]{1,0:T(8,128)(2,1)S(1)} %copy-done.103), channel_id=1, source_target_pairs={{2,1},{1,2},{6,5},{5,6},{10,9},{9,10},{14,13},{13,14},{18,17},{17,... | collective-permute-start | bytes 3391496 | tf_op jit(solution)/shard_map/ppermute | solution.py:766
  748.6 29.7 %collective-permute-start.95 = (bf16[2,2,64,2048]{3,2,0,1:T(8,128)(2,1)}, bf16[2,2,64,2048]{3,2,0,1:T(8,128)(2,1)}, u32[]{:S(2)}, u32[]{:S(2)}) collective-permute-start(bf16[2,2,64,2048]{3,2,0,1:T(8,128)(2,1)} %dynamic-slice_bitcast_fusion), channel_id=1, source_target_pairs={{0,4},{2,6},{4,0},{6,2},{8,12},{10,14},{12,8},{14,10},{16,20},{18,... | collective-permute-start | bytes 3145736 | tf_op jit(solution)/shard_map/ppermute | solution.py:779
  749.9 68.4 %collective-permute-start.98 = (bf16[2,64,2048]{2,1,0:T(8,128)(2,1)}, bf16[2,64,2048]{2,1,0:T(8,128)(2,1)}, u32[]{:S(2)}, u32[]{:S(2)}) collective-permute-start(bf16[2,64,2048]{2,1,0:T(8,128)(2,1)} %dynamic-slice_bitcast_fusion.5), channel_id=1, source_target_pairs={{0,8},{2,10},{4,12},{6,14},{8,0},{10,2},{12,4},{14,6},{16,24},{18,... | collective-permute-start | bytes 1572872 | tf_op jit(solution)/shard_map/ppermute | solution.py:779
  772.8 39.7 %collective-permute-start.94 = (bf16[2048,512]{1,0:T(8,128)(2,1)}, bf16[2048,512]{1,0:T(8,128)(2,1)}, u32[]{:S(2)}, u32[]{:S(2)}) collective-permute-start(bf16[2048,512]{1,0:T(8,128)(2,1)} %convolution_convert_fusion.9), channel_id=1, source_target_pairs={{0,2},{2,0},{4,6},{6,4},{8,10},{10,8},{12,14},{14,12},{16,18},{18,... | collective-permute-start | bytes 6291464 | tf_op jit(solution)/shard_map/ppermute | solution.py:754
  772.8 43.4 %collective-permute-start.100 = (bf16[128,2048]{1,0:T(8,128)(2,1)}, bf16[128,2048]{1,0:T(8,128)(2,1)}, u32[]{:S(2)}, u32[]{:S(2)}) collective-permute-start(bf16[128,2048]{1,0:T(8,128)(2,1)} %get-tuple-element.398), channel_id=1, source_target_pairs={{0,4},{2,6},{8,0},{10,2},{16,8},{18,10},{24,16},{26,18},{28,24},{3... | collective-permute-start | bytes 1572872 | tf_op jit(solution)/shard_map/ppermute | solution.py:760
  772.8 25.7 %collective-permute-start.121 = (f32[8,704]{1,0:T(8,128)S(1)}, f32[8,704]{1,0:T(8,128)S(1)}, u32[]{:S(2)}, u32[]{:S(2)}) collective-permute-start(f32[8,704]{1,0:T(8,128)S(1)} %slice_select_fusion.1), channel_id=1, source_target_pairs={{0,8},{2,10},{4,12},{6,14},{8,0},{10,2},{12,4},{14,6},{16,24},{18,... | collective-permute-start | bytes 67592 | tf_op jit(solution)/shard_map/ppermute | solution.py:779
  778.3 37.9 %collective-permute-start.99 = (bf16[128,2048]{1,0:T(8,128)(2,1)}, bf16[128,2048]{1,0:T(8,128)(2,1)}, u32[]{:S(2)}, u32[]{:S(2)}) collective-permute-start(bf16[128,2048]{1,0:T(8,128)(2,1)} %get-tuple-element.397), channel_id=1, source_target_pairs={{0,8},{2,10},{8,16},{10,18},{16,24},{18,26},{24,28},{26,30},{28,20... | collective-permute-start | bytes 1572872 | tf_op jit(solution)/shard_map/ppermute | solution.py:760
  809.1 89.8 %collective-permute-start.118 = (bf16[552,2048]{1,0:T(8,128)(2,1)}, bf16[552,2048]{1,0:T(8,128)(2,1)}, u32[]{:S(2)}, u32[]{:S(2)}) collective-permute-start(bf16[552,2048]{1,0:T(8,128)(2,1)} %convolution_convert_fusion.8), channel_id=1, source_target_pairs={{2,1},{1,2},{6,5},{5,6},{10,9},{9,10},{14,13},{13,14},{18,17},{17,... | collective-permute-start | bytes 6782984 | tf_op jit(solution)/shard_map/ppermute | solution.py:766
  812.5 35.5 %collective-permute-start.104 = (bf16[2,64,2048]{2,1,0:T(8,128)(2,1)}, bf16[2,64,2048]{2,1,0:T(8,128)(2,1)S(1)}, u32[]{:S(2)}, u32[]{:S(2)}) collective-permute-start(bf16[2,64,2048]{2,1,0:T(8,128)(2,1)} %dynamic-slice_bitcast_fusion.4), channel_id=1, source_target_pairs={{0,1},{1,0},{2,3},{3,2},{4,5},{5,4},{6,7},{7,6},{8,9},{9,8},{10,11... | collective-permute-start | bytes 1572872 | tf_op jit(solution)/shard_map/ppermute | solution.py:776
  818.3 23.7 %collective-permute-start.105 = (bf16[128,2048]{1,0:T(8,128)(2,1)S(1)}, bf16[128,2048]{1,0:T(8,128)(2,1)S(1)}, u32[]{:S(2)}, u32[]{:S(2)}) collective-permute-start(bf16[128,2048]{1,0:T(8,128)(2,1)S(1)} %get-tuple-element.408), channel_id=1, source_target_pairs={{0,8},{2,10},{8,16},{10,18},{16,24},{18,26},{24,28},{26,30},{28,20... | collective-permute-start | bytes 1572872 | tf_op jit(solution)/shard_map/ppermute | solution.py:760
  842.0 39.7 %collective-permute-start.115 = (bf16[64,2048]{1,0:T(8,128)(2,1)S(1)}, bf16[64,2048]{1,0:T(8,128)(2,1)S(1)}, u32[]{:S(2)}, u32[]{:S(2)}) collective-permute-start(bf16[64,2048]{1,0:T(8,128)(2,1)S(1)} %dynamic-slice_bitcast_fusion.11), channel_id=1, source_target_pairs={{0,16},{2,18},{4,20},{6,22},{8,24},{10,26},{12,28},{14,30},{16,0},... | collective-permute-start | bytes 786440 | tf_op jit(solution)/shard_map/ppermute | solution.py:779
  874.2 26.6 %collective-permute-start.117 = (bf16[64,2048]{1,0:T(8,128)(2,1)S(1)}, bf16[64,2048]{1,0:T(8,128)(2,1)S(1)}, u32[]{:S(2)}, u32[]{:S(2)}) collective-permute-start(bf16[64,2048]{1,0:T(8,128)(2,1)S(1)} %dynamic-slice_bitcast_fusion.10), channel_id=1, source_target_pairs={{0,16},{2,18},{4,20},{6,22},{8,24},{10,26},{12,28},{14,30},{16,0},... | collective-permute-start | bytes 786440 | tf_op jit(solution)/shard_map/ppermute | solution.py:779
  882.1 42.5 %collective-permute-start.107 = (bf16[552,1024]{1,0:T(8,128)(2,1)S(1)}, bf16[552,1024]{1,0:T(8,128)(2,1)}, u32[]{:S(2)}, u32[]{:S(2)}) collective-permute-start(bf16[552,1024]{1,0:T(8,128)(2,1)S(1)} %fusion.16), channel_id=1, source_target_pairs={{2,1},{1,2},{6,5},{5,6},{10,9},{9,10},{14,13},{13,14},{18,17},{17,... | collective-permute-start | bytes 3391496 | tf_op jit(solution)/shard_map/ppermute | solution.py:766
  894.7 26.0 %collective-permute-start.125 = (bf16[64,2048]{1,0:T(8,128)(2,1)S(1)}, bf16[64,2048]{1,0:T(8,128)(2,1)S(1)}, u32[]{:S(2)}, u32[]{:S(2)}) collective-permute-start(bf16[64,2048]{1,0:T(8,128)(2,1)S(1)} %add_convert_fusion.6), channel_id=1, source_target_pairs={{2,1},{1,2},{6,5},{5,6},{10,9},{9,10},{14,13},{13,14},{18,17},{17,... | collective-permute-start | bytes 786440 | tf_op jit(solution)/shard_map/ppermute | solution.py:766
  (276 other events, 3044.7 us)
Sparse Core Ops, SparseCore 0:
  694.2 103.0 reduce-scatter.1

commit v4 on v3

--- a/solution.py
+++ b/solution.py
@@ -839,8 +839,8 @@
     )(places, *operands)
 
 
-def row_chunks(count):
-    return [(begin, min(384, count - begin)) for begin in range(0, count, 384)]
+def row_chunks(count, size):
+    return [(begin, min(size, count - begin)) for begin in range(0, count, size)]
 
 
 NT = (((1,), (1,)), ((), ()))
@@ -859,7 +859,7 @@
     def kernel(query_ref, key_ref, value_ref, out_ref, total_ref):
         keys = key_ref[...]
         values = value_ref[...]
-        for begin, rows in row_chunks(tokens):
+        for begin, rows in row_chunks(tokens, 640):
             query = query_ref[begin : begin + rows, :] * jnp.bfloat16(HEAD_DIM**-0.5)
             mixed, totals = ([], [])
             for head in range(2):
@@ -927,7 +927,7 @@
             )[0:1, :]
             for head in range(2)
         ]
-        for begin, rows in row_chunks(tokens):
+        for begin, rows in row_chunks(tokens, 256):
             keys = key_ref[begin : begin + rows, :]
             values = value_ref[begin : begin + rows, :]
             key_grads, value_grads = ([], [])

time: 951 us -> 945 us (level)
  transfers between devices with their start and end apart: 129 -> 129, of which waited for: 49 -> 49; matrix products, arithmetic and copies ran while one was open for 29% -> 29% of each run, Pallas kernels for 15% -> 14%
where the time goes in v4:
time: 945 us; the launch traced here: 934 us
  waiting for transfers between devices  236 us (25%)
  starting transfers between devices  180 us (19%)
  matrix products  152 us (16%)
  Pallas kernels  131 us (14%)
  other arithmetic  119 us (13%)
  local copies, waits for them, and re-layouts  99 us (10%)
  between operations  17.9 us (2%)
    ppermute x64, waiting for transfers between devices, along_ring(): return lax.ppermute(value, FSDP, self.ring_pairs[step])  149 us
    pallas_call x4, Pallas kernels, attention_backward(): pl.pallas_call(kernel, grid=(pair_count,), in_specs=[part(0), part(1), pa...  75.2 us
    ppermute x16, starting transfers between devices, diagonal_other(): return lax.ppermute(value, BOTH, self.diagonal_pairs)  73.7 us
    ppermute x64, starting transfers between devices, along_ring(): return lax.ppermute(value, FSDP, self.ring_pairs[step])  56.8 us
    pallas_call x2, Pallas kernels, attention_forward(): pl.pallas_call(kernel, grid=(pairs,), in_specs=[part(0), part(1), part(2)...  35.2 us
    unnamed x408, local copies, waits for them, and re-layouts  32.5 us
    ppermute x16, waiting for transfers between devices, diagonal_other(): return lax.ppermute(value, BOTH, self.diagonal_pairs)  30.8 us
    ppermute x15, waiting for transfers between devices, to_partner(): return lax.ppermute(value, FSDP, pairs)  29.3 us
  transfers between devices with their start and end apart: 129, of which 49 were waited for; matrix products, arithmetic and copies ran while one was open for 29% of the time, Pallas kernels for 14%

profile of v4, /device:TPU:1, one launch (start us, length us, event | category | flops | bytes accessed | tf_op | source)
XLA Modules:
  0.0 934.3 jit_solution(16836807947849308326)
XLA Ops:
  15.4 5.5 collective-permute-done
  24.8 7.3 collective-permute-done.2
  33.7 8.7 collective-permute-done.1
  42.6 8.3 collective-permute-done.4.refs_2_
  55.1 14.3 %collective-permute-done.10.refs_5_ = bf16[128,3200]{1,0:T(8,128)(2,1)} collective-permute-done((bf16[128,3200]{1,0:T(8,128)(2,1)S(1)}, bf16[128,3200]{1,0:T(8,128)(2,1)}, u32[]{:S(2)}, u32[]{:S(2)}) %collective-permute-start.10) | collective-permute-done | bytes 819232 | tf_op jit(solution)/shard_map/ppermute | solution.py:760
  69.6 9.2 collective-permute-start.15
  80.3 6.1 collective-permute-done.7.refs_2_
  93.8 10.2 %collective-permute-done.13.refs_0_ = bf16[128,3200]{1,0:T(8,128)(2,1)S(1)} collective-permute-done((bf16[128,3200]{1,0:T(8,128)(2,1)S(1)}, bf16[128,3200]{1,0:T(8,128)(2,1)S(1)}, u32[]{:S(2)}, u32[]{:S(2)}) %collective-permute-start.13) | collective-permute-done | bytes 819232 | tf_op jit(solution)/shard_map/ppermute | solution.py:760
  104.0 9.2 collective-permute-start.6
  136.1 6.6 collective-permute-start.26
  160.2 8.3 collective-permute-done.22.refs_7_
  176.2 5.2 maximum_select_fusion.1
  201.8 7.0 collective-permute-done.31.refs_1_
  226.9 4.9 convolution_convert_fusion.1.query_ref.key_ref.value_ref
  236.2 17.6 %shard_map.344 = (bf16[1104,512]{1,0:T(8,128)(2,1)S(1)}, f32[4,2,1104]{2,1,0:T(2,128)S(1)}) custom-call(bf16[1104,1536]{1,0:T(8,128)(2,1)S(1)} %convolution_convert_fusion.1.query_ref.key_ref.value_ref, bf16[1104,1536]{1,0:T(8,128)(2,1)S(1)} %convolution_convert_fusion.1.query_ref.key_ref.value_ref, ...), custom_call_target="tpu_custom_call" | custom-call | flops 4992270336 | bytes 4521984 | tf_op jit(solution)/shard_map/pallas_call | solution.py:890
  263.7 6.6 collective-permute-done.41.refs_7_
  292.8 9.9 %multiply_convert_fusion.1 = (bf16[1104,2048]{1,0:T(8,128)(2,1)S(1)}, f32[1104,2048]{1,0:T(8,128)}) fusion(f32[2048]{0:T(1024)S(1)} %dynamic-slice_convert_fusion.3, bf16[1024,2048]{1,0:T(8,128)(2,1)S(1)} %shard_map.345, bf16[552,1024]{1,0:T(8,128)(2,1)} %collective-permute-done.43, bf16[552,1024]{1,0:T(8,128)(2,1)} %add_convert_fusion.4), kind=kOutput, calls=%fused_computation.18 | convolution fusion | flops 4648599552 | bytes 20029440 | tf_op jit(solution)/shard_map/dot_general | solution.py:1208
  316.4 7.5 collective-permute-done.50.refs_2_
  329.1 5.9 collective-permute-done.52.refs_1_
  344.9 10.8 %collective-permute-done.55.refs_1_ = bf16[128,2048]{1,0:T(8,128)(2,1)S(1)} collective-permute-done((bf16[128,2048]{1,0:T(8,128)(2,1)}, bf16[128,2048]{1,0:T(8,128)(2,1)S(1)}, u32[]{:S(2)}, u32[]{:S(2)}) %collective-permute-start.55) | collective-permute-done | bytes 524320 | tf_op jit(solution)/shard_map/ppermute | solution.py:760
  358.4 4.9 convolution_convert_fusion.query_ref.key_ref.value_ref
  366.9 17.6 %shard_map.347 = (bf16[1104,512]{1,0:T(8,128)(2,1)S(1)}, f32[4,2,1104]{2,1,0:T(2,128)S(1)}) custom-call(bf16[1104,1536]{1,0:T(8,128)(2,1)S(1)} %convolution_convert_fusion.query_ref.key_ref.value_ref, bf16[1104,1536]{1,0:T(8,128)(2,1)S(1)} %convolution_convert_fusion.query_ref.key_ref.value_ref, ...), custom_call_target="tpu_custom_call" | custom-call | flops 4992270336 | bytes 4521984 | tf_op jit(solution)/shard_map/pallas_call | solution.py:890
  421.2 8.3 multiply_convert_fusion
  429.5 6.1 convolution_convert_fusion.5
  435.8 8.2 fusion.81
  452.0 6.2 convolution_convert_fusion.4
  484.6 18.6 %shard_map.350 = (bf16[1104,256]{1,0:T(8,128)(2,1)S(1)}, bf16[1104,256]{1,0:T(8,128)(2,1)S(1)}, bf16[1104,256]{1,0:T(8,128)(2,1)S(1)}) custom-call(bf16[1104,1536]{1,0:T(8,128)(2,1)} %copy-done.68, bf16[1104,1536]{1,0:T(8,128)(2,1)} %copy-done.68, bf16[1104,1536]{1,0:T(8,128)(2,1)} %copy-done.68, bf16[1104,512]{1,0:T(8,128)(2,1)S(1)} %copy-done.66, ...), custom_call_target="tpu_custom_call" | custom-call | flops 6240337920 | bytes 4521984 | tf_op jit(solution)/shard_map/pallas_call | solution.py:969
  503.2 19.3 %shard_map.351 = (bf16[1104,256]{1,0:T(8,128)(2,1)S(1)}, bf16[1104,256]{1,0:T(8,128)(2,1)S(1)}, bf16[1104,256]{1,0:T(8,128)(2,1)S(1)}) custom-call(bf16[1104,1536]{1,0:T(8,128)(2,1)} %copy-done.68, bf16[1104,1536]{1,0:T(8,128)(2,1)} %copy-done.68, bf16[1104,1536]{1,0:T(8,128)(2,1)} %copy-done.68, bf16[1104,512]{1,0:T(8,128)(2,1)S(1)} %copy-done.66, ...), custom_call_target="tpu_custom_call" | custom-call | flops 6240337920 | bytes 4521984 | tf_op jit(solution)/shard_map/pallas_call | solution.py:969
  537.0 5.8 convolution_convert_fusion.7
  572.8 10.0 %fusion.82 = (f32[2048]{0:T(1024)S(1)}, bf16[1104,2048]{1,0:T(8,128)(2,1)S(1)}) fusion(f32[1104,2048]{1,0:T(8,128)} %get-tuple-element.598, bf16[1024,2048]{1,0:T(8,128)(2,1)S(1)} %copy-done.7, bf16[552,1024]{1,0:T(8,128)(2,1)} %collective-permute-done.73, bf16[552,1024]{1,0:T(8,128)(2,1)S(1)} %get-tuple-element.513), kind=kOutput, calls=%fused_computation.349 | convolution fusion | flops 4664424448 | bytes 20029440 | tf_op jit(solution)/shard_map/dot_general | solution.py:1269
  598.4 5.9 collective-permute-done.81
  604.4 6.1 convolution_convert_fusion.3
  615.0 6.4 convolution_convert_fusion.2
  637.3 9.2 collective-permute-done.127
  659.3 18.7 %shard_map.352 = (bf16[1104,256]{1,0:T(8,128)(2,1)S(1)}, bf16[1104,256]{1,0:T(8,128)(2,1)S(1)}, bf16[1104,256]{1,0:T(8,128)(2,1)S(1)}) custom-call(bf16[1104,1536]{1,0:T(8,128)(2,1)} %copy-done.67, bf16[1104,1536]{1,0:T(8,128)(2,1)} %copy-done.67, bf16[1104,1536]{1,0:T(8,128)(2,1)} %copy-done.67, bf16[1104,512]{1,0:T(8,128)(2,1)S(1)} %copy-done.64, ...), custom_call_target="tpu_custom_call" | custom-call | flops 6240337920 | bytes 4521984 | tf_op jit(solution)/shard_map/pallas_call | solution.py:969
  681.7 7.7 maximum_select_fusion
  691.0 18.7 %shard_map.353 = (bf16[1104,256]{1,0:T(8,128)(2,1)S(1)}, bf16[1104,256]{1,0:T(8,128)(2,1)S(1)}, bf16[1104,256]{1,0:T(8,128)(2,1)S(1)}) custom-call(bf16[1104,1536]{1,0:T(8,128)(2,1)} %copy-done.67, bf16[1104,1536]{1,0:T(8,128)(2,1)} %copy-done.67, bf16[1104,1536]{1,0:T(8,128)(2,1)} %copy-done.67, bf16[1104,512]{1,0:T(8,128)(2,1)S(1)} %copy-done.64, ...), custom_call_target="tpu_custom_call" | custom-call | flops 6240337920 | bytes 4521984 | tf_op jit(solution)/shard_map/pallas_call | solution.py:969
  719.4 6.9 convolution_convert_fusion.6.refs_0_.refs_2_
  736.7 6.6 collective-permute-done.90
  762.5 5.0 convolution_convert_fusion.9
  773.2 20.8 %collective-permute-done.121 = f32[8,704]{1,0:T(8,128)S(1)} collective-permute-done((f32[8,704]{1,0:T(8,128)S(1)}, f32[8,704]{1,0:T(8,128)S(1)}, u32[]{:S(2)}, u32[]{:S(2)}) %collective-permute-start.121) | collective-permute-done | bytes 22560 | tf_op jit(solution)/shard_map/ppermute | solution.py:779
  821.7 7.5 collective-permute-done.96.refs_4_
  839.1 5.0 collective-permute-done.104
  844.5 5.3 collective-permute-done.102.refs_4_
  849.8 5.5 collective-permute-start.110
  860.4 5.4 collective-permute-done.110
  878.5 10.7 %collective-permute-start.107 = (bf16[552,1024]{1,0:T(8,128)(2,1)S(1)}, bf16[552,1024]{1,0:T(8,128)(2,1)}, u32[]{:S(2)}, u32[]{:S(2)}) collective-permute-start(bf16[552,1024]{1,0:T(8,128)(2,1)S(1)} %fusion.16), channel_id=1, source_target_pairs={{2,1},{1,2},{6,5},{5,6},{10,9},{9,10},{14,13},{13,14},{18,17},{17,... | collective-permute-start | bytes 3391496 | tf_op jit(solution)/shard_map/ppermute | solution.py:766
  901.9 5.4 collective-permute-done.116
  (919 shorter events, 485.5 us)
Async XLA Ops:
  7.3 914.6 %reduce-scatter.2.cloned.1.call-start = ((), (), s32[]{:S(2)}) async-start(), calls=%async_computation.1 | async-start | bytes 6684672 | tf_op jit(solution)/shard_map/reduce_scatter | solution.py:1492
  53.6 32.9 %collective-permute-start.7 = (bf16[128,3072]{1,0:T(8,128)(2,1)S(1)}, bf16[128,3072]{1,0:T(8,128)(2,1)}, u32[]{:S(2)}, u32[]{:S(2)}) collective-permute-start(bf16[128,3072]{1,0:T(8,128)(2,1)S(1)} %maximum_select_fusion.6.refs_3_), channel_id=1, source_target_pairs={{0,8},{2,10},{8,16},{10,18},{16,24},{18,26},{24,28},{26,30},{28,20... | collective-permute-start | bytes 2359304 | tf_op jit(solution)/shard_map/ppermute | solution.py:760
  54.9 31.5 %collective-permute-start.8 = (bf16[128,3072]{1,0:T(8,128)(2,1)S(1)}, bf16[128,3072]{1,0:T(8,128)(2,1)}, u32[]{:S(2)}, u32[]{:S(2)}) collective-permute-start(bf16[128,3072]{1,0:T(8,128)(2,1)S(1)} %maximum_select_fusion.6.refs_3_), channel_id=1, source_target_pairs={{0,4},{2,6},{8,0},{10,2},{16,8},{18,10},{24,16},{26,18},{28,24},{3... | collective-permute-start | bytes 2359304 | tf_op jit(solution)/shard_map/ppermute | solution.py:760
  78.8 25.2 %collective-permute-start.13 = (bf16[128,3200]{1,0:T(8,128)(2,1)S(1)}, bf16[128,3200]{1,0:T(8,128)(2,1)S(1)}, u32[]{:S(2)}, u32[]{:S(2)}) collective-permute-start(bf16[128,3200]{1,0:T(8,128)(2,1)S(1)} %collective-permute-done.9.refs_1_), channel_id=1, source_target_pairs={{0,8},{2,10},{8,16},{10,18},{16,24},{18,26},{24,28},{26,30},{28,20... | collective-permute-start | bytes 2457608 | tf_op jit(solution)/shard_map/ppermute | solution.py:760
  80.3 35.7 %collective-permute-start.14 = (bf16[128,3200]{1,0:T(8,128)(2,1)}, bf16[128,3200]{1,0:T(8,128)(2,1)S(1)}, u32[]{:S(2)}, u32[]{:S(2)}) collective-permute-start(bf16[128,3200]{1,0:T(8,128)(2,1)} %collective-permute-done.10.refs_5_), channel_id=1, source_target_pairs={{0,4},{2,6},{8,0},{10,2},{16,8},{18,10},{24,16},{26,18},{28,24},{3... | collective-permute-start | bytes 2457608 | tf_op jit(solution)/shard_map/ppermute | solution.py:760
  86.4 34.4 %collective-permute-start.11 = (bf16[128,3072]{1,0:T(8,128)(2,1)}, bf16[128,3072]{1,0:T(8,128)(2,1)}, u32[]{:S(2)}, u32[]{:S(2)}) collective-permute-start(bf16[128,3072]{1,0:T(8,128)(2,1)} %collective-permute-done.7.refs_2_), channel_id=1, source_target_pairs={{0,8},{2,10},{8,16},{10,18},{16,24},{18,26},{24,28},{26,30},{28,20... | collective-permute-start | bytes 2359304 | tf_op jit(solution)/shard_map/ppermute | solution.py:760
  87.6 34.3 %collective-permute-start.12 = (bf16[128,3072]{1,0:T(8,128)(2,1)}, bf16[128,3072]{1,0:T(8,128)(2,1)}, u32[]{:S(2)}, u32[]{:S(2)}) collective-permute-start(bf16[128,3072]{1,0:T(8,128)(2,1)} %collective-permute-done.8.refs_4_), channel_id=1, source_target_pairs={{0,4},{2,6},{8,0},{10,2},{16,8},{18,10},{24,16},{26,18},{28,24},{3... | collective-permute-start | bytes 2359304 | tf_op jit(solution)/shard_map/ppermute | solution.py:760
  88.8 34.4 %collective-permute-start.20 = (bf16[64,4096]{1,0:T(8,128)(2,1)}, bf16[64,4096]{1,0:T(8,128)(2,1)}, u32[]{:S(2)}, u32[]{:S(2)}) collective-permute-start(bf16[64,4096]{1,0:T(8,128)(2,1)} %broadcast_select_fusion.5), channel_id=1, source_target_pairs={{0,1},{1,0},{2,3},{3,2},{4,5},{5,4},{6,7},{7,6},{8,9},{9,8},{10,11... | collective-permute-start | bytes 1572872 | tf_op jit(solution)/shard_map/ppermute | solution.py:776
  104.0 51.4 %collective-permute-start.6 = (bf16[552,2048]{1,0:T(8,128)(2,1)}, bf16[552,2048]{1,0:T(8,128)(2,1)}, u32[]{:S(2)}, u32[]{:S(2)}) collective-permute-start(bf16[552,2048]{1,0:T(8,128)(2,1)} %get-tuple-element.238), channel_id=1, source_target_pairs={{2,1},{1,2},{6,5},{5,6},{10,9},{9,10},{14,13},{13,14},{18,17},{17,... | collective-permute-start | bytes 6782984 | tf_op jit(solution)/shard_map/ppermute | solution.py:766
  121.9 30.8 %collective-permute-start.16 = (bf16[128,3072]{1,0:T(8,128)(2,1)}, bf16[128,3072]{1,0:T(8,128)(2,1)}, u32[]{:S(2)}, u32[]{:S(2)}) collective-permute-start(bf16[128,3072]{1,0:T(8,128)(2,1)} %collective-permute-done.11.refs_1_), channel_id=1, source_target_pairs={{0,8},{2,10},{8,16},{10,18},{16,24},{18,26},{24,28},{26,30},{28,20... | collective-permute-start | bytes 2359304 | tf_op jit(solution)/shard_map/ppermute | solution.py:760
  123.2 30.1 %collective-permute-start.17 = (bf16[128,3072]{1,0:T(8,128)(2,1)}, bf16[128,3072]{1,0:T(8,128)(2,1)}, u32[]{:S(2)}, u32[]{:S(2)}) collective-permute-start(bf16[128,3072]{1,0:T(8,128)(2,1)} %collective-permute-done.12.refs_5_), channel_id=1, source_target_pairs={{0,4},{2,6},{8,0},{10,2},{16,8},{18,10},{24,16},{26,18},{28,24},{3... | collective-permute-start | bytes 2359304 | tf_op jit(solution)/shard_map/ppermute | solution.py:760
  136.1 40.1 %collective-permute-start.26 = (bf16[2048,512]{1,0:T(8,128)(2,1)}, bf16[2048,512]{1,0:T(8,128)(2,1)}, u32[]{:S(2)}, u32[]{:S(2)}) collective-permute-start(bf16[2048,512]{1,0:T(8,128)(2,1)} %get-tuple-element.261), channel_id=1, source_target_pairs={{0,2},{2,0},{4,6},{6,4},{8,10},{10,8},{12,14},{14,12},{16,18},{18,... | collective-permute-start | bytes 6291464 | tf_op jit(solution)/shard_map/ppermute | solution.py:754
  146.7 28.8 %collective-permute-start.27 = (bf16[128,2048]{1,0:T(8,128)(2,1)S(1)}, bf16[128,2048]{1,0:T(8,128)(2,1)S(1)}, u32[]{:S(2)}, u32[]{:S(2)}) collective-permute-start(bf16[128,2048]{1,0:T(8,128)(2,1)S(1)} %get-tuple-element.262.refs_3_), channel_id=1, source_target_pairs={{0,8},{2,10},{8,16},{10,18},{16,24},{18,26},{24,28},{26,30},{28,20... | collective-permute-start | bytes 1572872 | tf_op jit(solution)/shard_map/ppermute | solution.py:760
  192.8 33.3 %collective-permute-start.30 = (bf16[552,1024]{1,0:T(8,128)(2,1)S(1)}, bf16[552,1024]{1,0:T(8,128)(2,1)S(1)}, u32[]{:S(2)}, u32[]{:S(2)}) collective-permute-start(bf16[552,1024]{1,0:T(8,128)(2,1)S(1)} %add_convert_fusion.5), channel_id=1, source_target_pairs={{0,2},{2,0},{4,6},{6,4},{8,10},{10,8},{12,14},{14,12},{16,18},{18,... | collective-permute-start | bytes 3391496 | tf_op jit(solution)/shard_map/ppermute | solution.py:754
  196.6 57.3 %collective-permute-start.35 = (bf16[552,2048]{1,0:T(8,128)(2,1)}, bf16[552,2048]{1,0:T(8,128)(2,1)}, u32[]{:S(2)}, u32[]{:S(2)}) collective-permute-start(bf16[552,2048]{1,0:T(8,128)(2,1)} %get-tuple-element.280), channel_id=1, source_target_pairs={{2,1},{1,2},{6,5},{5,6},{10,9},{9,10},{14,13},{13,14},{18,17},{17,... | collective-permute-start | bytes 6782984 | tf_op jit(solution)/shard_map/ppermute | solution.py:766
  224.9 28.9 %collective-permute-start.38 = (bf16[128,2048]{1,0:T(8,128)(2,1)S(1)}, bf16[128,2048]{1,0:T(8,128)(2,1)S(1)}, u32[]{:S(2)}, u32[]{:S(2)}) collective-permute-start(bf16[128,2048]{1,0:T(8,128)(2,1)S(1)} %collective-permute-done.36.refs_1_), channel_id=1, source_target_pairs={{0,8},{2,10},{8,16},{10,18},{16,24},{18,26},{24,28},{26,30},{28,20... | collective-permute-start | bytes 1572872 | tf_op jit(solution)/shard_map/ppermute | solution.py:760
  226.1 27.7 %collective-permute-start.39 = (bf16[128,2048]{1,0:T(8,128)(2,1)S(1)}, bf16[128,2048]{1,0:T(8,128)(2,1)S(1)}, u32[]{:S(2)}, u32[]{:S(2)}) collective-permute-start(bf16[128,2048]{1,0:T(8,128)(2,1)S(1)} %collective-permute-done.37.refs_5_), channel_id=1, source_target_pairs={{0,4},{2,6},{8,0},{10,2},{16,8},{18,10},{24,16},{26,18},{28,24},{3... | collective-permute-start | bytes 1572872 | tf_op jit(solution)/shard_map/ppermute | solution.py:760
  278.5 46.1 %collective-permute-start.49 = (bf16[2048,512]{1,0:T(8,128)(2,1)}, bf16[2048,512]{1,0:T(8,128)(2,1)}, u32[]{:S(2)}, u32[]{:S(2)}) collective-permute-start(bf16[2048,512]{1,0:T(8,128)(2,1)} %copy-done.8), channel_id=1, source_target_pairs={{0,2},{2,0},{4,6},{6,4},{8,10},{10,8},{12,14},{14,12},{16,18},{18,... | collective-permute-start | bytes 6291464 | tf_op jit(solution)/shard_map/ppermute | solution.py:754
  355.7 28.9 %collective-permute-start.59 = (bf16[128,2048]{1,0:T(8,128)(2,1)S(1)}, bf16[128,2048]{1,0:T(8,128)(2,1)S(1)}, u32[]{:S(2)}, u32[]{:S(2)}) collective-permute-start(bf16[128,2048]{1,0:T(8,128)(2,1)S(1)} %collective-permute-done.55.refs_1_), channel_id=1, source_target_pairs={{0,8},{2,10},{8,16},{10,18},{16,24},{18,26},{24,28},{26,30},{28,20... | collective-permute-start | bytes 1572872 | tf_op jit(solution)/shard_map/ppermute | solution.py:760
  355.8 28.7 %collective-permute-start.60 = (bf16[128,2048]{1,0:T(8,128)(2,1)S(1)}, bf16[128,2048]{1,0:T(8,128)(2,1)S(1)}, u32[]{:S(2)}, u32[]{:S(2)}) collective-permute-start(bf16[128,2048]{1,0:T(8,128)(2,1)S(1)} %collective-permute-done.56.refs_5_), channel_id=1, source_target_pairs={{0,4},{2,6},{8,0},{10,2},{16,8},{18,10},{24,16},{26,18},{28,24},{3... | collective-permute-start | bytes 1572872 | tf_op jit(solution)/shard_map/ppermute | solution.py:760
  469.6 52.9 %collective-permute-start.71 = (bf16[2,2,2,64,2048]{4,3,0,2,1:T(8,128)(2,1)}, bf16[2,2,2,64,2048]{4,3,0,2,1:T(8,128)(2,1)}, u32[]{:S(2)}, u32[]{:S(2)}) collective-permute-start(bf16[2,2,2,64,2048]{4,3,0,2,1:T(8,128)(2,1)} %bitcast.259), channel_id=1, source_target_pairs={{0,1},{1,0},{2,3},{3,2},{4,5},{5,4},{6,7},{7,6},{8,9},{9,8},{10,11... | collective-permute-start | bytes 6291464 | tf_op jit(solution)/shard_map/ppermute | solution.py:776
  474.9 50.3 %collective-permute-start.70 = (bf16[2,2,2,64,2048]{4,3,0,1,2:T(8,128)(2,1)}, bf16[2,2,2,64,2048]{4,3,0,1,2:T(8,128)(2,1)}, u32[]{:S(2)}, u32[]{:S(2)}) collective-permute-start(bf16[2,2,2,64,2048]{4,3,0,1,2:T(8,128)(2,1)} %bitcast.260), channel_id=1, source_target_pairs={{0,4},{2,6},{4,0},{6,2},{8,12},{10,14},{12,8},{14,10},{16,20},{18,... | collective-permute-start | bytes 6291464 | tf_op jit(solution)/shard_map/ppermute | solution.py:779
  535.3 24.8 %collective-permute-start.77 = (bf16[2,2,64,2048]{3,2,0,1:T(8,128)(2,1)S(1)}, bf16[2,2,64,2048]{3,2,0,1:T(8,128)(2,1)S(1)}, u32[]{:S(2)}, u32[]{:S(2)}) collective-permute-start(bf16[2,2,64,2048]{3,2,0,1:T(8,128)(2,1)S(1)} %dynamic-slice_bitcast_fusion.2), channel_id=1, source_target_pairs={{0,8},{2,10},{4,12},{6,14},{8,0},{10,2},{12,4},{14,6},{16,24},{18,... | collective-permute-start | bytes 3145736 | tf_op jit(solution)/shard_map/ppermute | solution.py:779
  536.9 27.9 %collective-permute-start.74 = (bf16[2,2,64,2048]{3,2,0,1:T(8,128)(2,1)S(1)}, bf16[2,2,64,2048]{3,2,0,1:T(8,128)(2,1)S(1)}, u32[]{:S(2)}, u32[]{:S(2)}) collective-permute-start(bf16[2,2,64,2048]{3,2,0,1:T(8,128)(2,1)S(1)} %dynamic-slice_bitcast_fusion.3), channel_id=1, source_target_pairs={{0,1},{1,0},{2,3},{3,2},{4,5},{5,4},{6,7},{7,6},{8,9},{9,8},{10,11... | collective-permute-start | bytes 3145736 | tf_op jit(solution)/shard_map/ppermute | solution.py:776
  542.8 116.5 %collective-permute-start.83 = (bf16[1024,1536]{1,0:T(8,128)(2,1)}, bf16[1024,1536]{1,0:T(8,128)(2,1)}, u32[]{:S(2)}, u32[]{:S(2)}) collective-permute-start(bf16[1024,1536]{1,0:T(8,128)(2,1)} %convolution_convert_fusion.7), channel_id=1, source_target_pairs={{2,1},{1,2},{6,5},{5,6},{10,9},{9,10},{14,13},{13,14},{18,17},{17,... | collective-permute-start | bytes 9437192 | tf_op jit(solution)/shard_map/ppermute | solution.py:766
  546.7 112.6 %collective-permute-start.84 = (bf16[1024,512]{1,0:T(8,128)(2,1)}, bf16[1024,512]{1,0:T(8,128)(2,1)}, u32[]{:S(2)}, u32[]{:S(2)}) collective-permute-start(bf16[1024,512]{1,0:T(8,128)(2,1)} %convolution_convert_fusion.14), channel_id=1, source_target_pairs={{2,1},{1,2},{6,5},{5,6},{10,9},{9,10},{14,13},{13,14},{18,17},{17,... | collective-permute-start | bytes 3145736 | tf_op jit(solution)/shard_map/ppermute | solution.py:766
  586.2 24.3 %collective-permute-start.80 = (bf16[64,2048]{1,0:T(8,128)(2,1)S(1)}, bf16[64,2048]{1,0:T(8,128)(2,1)S(1)}, u32[]{:S(2)}, u32[]{:S(2)}) collective-permute-start(bf16[64,2048]{1,0:T(8,128)(2,1)S(1)} %dynamic-slice_bitcast_fusion.13), channel_id=1, source_target_pairs={{0,16},{2,18},{4,20},{6,22},{8,24},{10,26},{12,28},{14,30},{16,0},... | collective-permute-start | bytes 786440 | tf_op jit(solution)/shard_map/ppermute | solution.py:779
  597.0 34.1 %collective-permute-start.79 = (bf16[552,1024]{1,0:T(8,128)(2,1)S(1)}, bf16[552,1024]{1,0:T(8,128)(2,1)S(1)}, u32[]{:S(2)}, u32[]{:S(2)}) collective-permute-start(bf16[552,1024]{1,0:T(8,128)(2,1)S(1)} %slice.766), channel_id=1, source_target_pairs={{0,2},{2,0},{4,6},{6,4},{8,10},{10,8},{12,14},{14,12},{16,18},{18,... | collective-permute-start | bytes 3391496 | tf_op jit(solution)/shard_map/ppermute | solution.py:754
  613.9 64.1 %collective-permute-start.87 = (bf16[2,2,2,64,2048]{4,3,0,1,2:T(8,128)(2,1)}, bf16[2,2,2,64,2048]{4,3,0,1,2:T(8,128)(2,1)}, u32[]{:S(2)}, u32[]{:S(2)}) collective-permute-start(bf16[2,2,2,64,2048]{4,3,0,1,2:T(8,128)(2,1)} %bitcast.258), channel_id=1, source_target_pairs={{0,4},{2,6},{4,0},{6,2},{8,12},{10,14},{12,8},{14,10},{16,20},{18,... | collective-permute-start | bytes 6291464 | tf_op jit(solution)/shard_map/ppermute | solution.py:779
  623.0 58.8 %collective-permute-start.85 = (bf16[1024,512]{1,0:T(8,128)(2,1)}, bf16[1024,512]{1,0:T(8,128)(2,1)}, u32[]{:S(2)}, u32[]{:S(2)}) collective-permute-start(bf16[1024,512]{1,0:T(8,128)(2,1)} %bitcast.43), channel_id=1, source_target_pairs={{2,1},{1,2},{6,5},{5,6},{10,9},{9,10},{14,13},{13,14},{18,17},{17,... | collective-permute-start | bytes 3145736 | tf_op jit(solution)/shard_map/ppermute | solution.py:766
  649.3 32.4 %collective-permute-start.86 = (bf16[1024,512]{1,0:T(8,128)(2,1)}, bf16[1024,512]{1,0:T(8,128)(2,1)S(1)}, u32[]{:S(2)}, u32[]{:S(2)}) collective-permute-start(bf16[1024,512]{1,0:T(8,128)(2,1)} %bitcast.44), channel_id=1, source_target_pairs={{2,1},{1,2},{6,5},{5,6},{10,9},{9,10},{14,13},{13,14},{18,17},{17,... | collective-permute-start | bytes 3145736 | tf_op jit(solution)/shard_map/ppermute | solution.py:766
  659.3 50.4 %collective-permute-start.88 = (bf16[2,2,2,64,2048]{4,3,0,2,1:T(8,128)(2,1)}, bf16[2,2,2,64,2048]{4,3,0,2,1:T(8,128)(2,1)}, u32[]{:S(2)}, u32[]{:S(2)}) collective-permute-start(bf16[2,2,2,64,2048]{4,3,0,2,1:T(8,128)(2,1)} %bitcast.257), channel_id=1, source_target_pairs={{0,8},{2,10},{4,12},{6,14},{8,0},{10,2},{12,4},{14,6},{16,24},{18,... | collective-permute-start | bytes 6291464 | tf_op jit(solution)/shard_map/ppermute | solution.py:779
  718.8 25.9 %collective-permute-start.89 = (bf16[552,1024]{1,0:T(8,128)(2,1)S(1)}, bf16[552,1024]{1,0:T(8,128)(2,1)S(1)}, u32[]{:S(2)}, u32[]{:S(2)}) collective-permute-start(bf16[552,1024]{1,0:T(8,128)(2,1)S(1)} %slice.765), channel_id=1, source_target_pairs={{0,2},{2,0},{4,6},{6,4},{8,10},{10,8},{12,14},{14,12},{16,18},{18,... | collective-permute-start | bytes 3391496 | tf_op jit(solution)/shard_map/ppermute | solution.py:754
  718.9 24.5 %collective-permute-start.90 = (bf16[2,2,64,2048]{3,2,0,1:T(8,128)(2,1)S(1)}, bf16[2,2,64,2048]{3,2,0,1:T(8,128)(2,1)S(1)}, u32[]{:S(2)}, u32[]{:S(2)}) collective-permute-start(bf16[2,2,64,2048]{3,2,0,1:T(8,128)(2,1)S(1)} %dynamic-slice_bitcast_fusion.1), channel_id=1, source_target_pairs={{0,1},{1,0},{2,3},{3,2},{4,5},{5,4},{6,7},{7,6},{8,9},{9,8},{10,11... | collective-permute-start | bytes 3145736 | tf_op jit(solution)/shard_map/ppermute | solution.py:776
  731.8 24.6 %collective-permute-start.91 = (bf16[552,1024]{1,0:T(8,128)(2,1)S(1)}, bf16[552,1024]{1,0:T(8,128)(2,1)S(1)}, u32[]{:S(2)}, u32[]{:S(2)}) collective-permute-start(bf16[552,1024]{1,0:T(8,128)(2,1)S(1)} %copy-done.103), channel_id=1, source_target_pairs={{2,1},{1,2},{6,5},{5,6},{10,9},{9,10},{14,13},{13,14},{18,17},{17,... | collective-permute-start | bytes 3391496 | tf_op jit(solution)/shard_map/ppermute | solution.py:766
  743.3 29.7 %collective-permute-start.95 = (bf16[2,2,64,2048]{3,2,0,1:T(8,128)(2,1)}, bf16[2,2,64,2048]{3,2,0,1:T(8,128)(2,1)}, u32[]{:S(2)}, u32[]{:S(2)}) collective-permute-start(bf16[2,2,64,2048]{3,2,0,1:T(8,128)(2,1)} %dynamic-slice_bitcast_fusion), channel_id=1, source_target_pairs={{0,4},{2,6},{4,0},{6,2},{8,12},{10,14},{12,8},{14,10},{16,20},{18,... | collective-permute-start | bytes 3145736 | tf_op jit(solution)/shard_map/ppermute | solution.py:779
  744.6 69.8 %collective-permute-start.98 = (bf16[2,64,2048]{2,1,0:T(8,128)(2,1)}, bf16[2,64,2048]{2,1,0:T(8,128)(2,1)}, u32[]{:S(2)}, u32[]{:S(2)}) collective-permute-start(bf16[2,64,2048]{2,1,0:T(8,128)(2,1)} %dynamic-slice_bitcast_fusion.5), channel_id=1, source_target_pairs={{0,8},{2,10},{4,12},{6,14},{8,0},{10,2},{12,4},{14,6},{16,24},{18,... | collective-permute-start | bytes 1572872 | tf_op jit(solution)/shard_map/ppermute | solution.py:779
  767.5 41.1 %collective-permute-start.94 = (bf16[2048,512]{1,0:T(8,128)(2,1)}, bf16[2048,512]{1,0:T(8,128)(2,1)}, u32[]{:S(2)}, u32[]{:S(2)}) collective-permute-start(bf16[2048,512]{1,0:T(8,128)(2,1)} %convolution_convert_fusion.9), channel_id=1, source_target_pairs={{0,2},{2,0},{4,6},{6,4},{8,10},{10,8},{12,14},{14,12},{16,18},{18,... | collective-permute-start | bytes 6291464 | tf_op jit(solution)/shard_map/ppermute | solution.py:754
  767.5 44.9 %collective-permute-start.100 = (bf16[128,2048]{1,0:T(8,128)(2,1)}, bf16[128,2048]{1,0:T(8,128)(2,1)}, u32[]{:S(2)}, u32[]{:S(2)}) collective-permute-start(bf16[128,2048]{1,0:T(8,128)(2,1)} %get-tuple-element.398), channel_id=1, source_target_pairs={{0,4},{2,6},{8,0},{10,2},{16,8},{18,10},{24,16},{26,18},{28,24},{3... | collective-permute-start | bytes 1572872 | tf_op jit(solution)/shard_map/ppermute | solution.py:760
  767.6 26.4 %collective-permute-start.121 = (f32[8,704]{1,0:T(8,128)S(1)}, f32[8,704]{1,0:T(8,128)S(1)}, u32[]{:S(2)}, u32[]{:S(2)}) collective-permute-start(f32[8,704]{1,0:T(8,128)S(1)} %slice_select_fusion.1), channel_id=1, source_target_pairs={{0,8},{2,10},{4,12},{6,14},{8,0},{10,2},{12,4},{14,6},{16,24},{18,... | collective-permute-start | bytes 67592 | tf_op jit(solution)/shard_map/ppermute | solution.py:779
  773.0 39.3 %collective-permute-start.99 = (bf16[128,2048]{1,0:T(8,128)(2,1)}, bf16[128,2048]{1,0:T(8,128)(2,1)}, u32[]{:S(2)}, u32[]{:S(2)}) collective-permute-start(bf16[128,2048]{1,0:T(8,128)(2,1)} %get-tuple-element.397), channel_id=1, source_target_pairs={{0,8},{2,10},{8,16},{10,18},{16,24},{18,26},{24,28},{26,30},{28,20... | collective-permute-start | bytes 1572872 | tf_op jit(solution)/shard_map/ppermute | solution.py:760
  805.3 88.1 %collective-permute-start.118 = (bf16[552,2048]{1,0:T(8,128)(2,1)}, bf16[552,2048]{1,0:T(8,128)(2,1)}, u32[]{:S(2)}, u32[]{:S(2)}) collective-permute-start(bf16[552,2048]{1,0:T(8,128)(2,1)} %convolution_convert_fusion.8), channel_id=1, source_target_pairs={{2,1},{1,2},{6,5},{5,6},{10,9},{9,10},{14,13},{13,14},{18,17},{17,... | collective-permute-start | bytes 6782984 | tf_op jit(solution)/shard_map/ppermute | solution.py:766
  808.6 35.5 %collective-permute-start.104 = (bf16[2,64,2048]{2,1,0:T(8,128)(2,1)}, bf16[2,64,2048]{2,1,0:T(8,128)(2,1)S(1)}, u32[]{:S(2)}, u32[]{:S(2)}) collective-permute-start(bf16[2,64,2048]{2,1,0:T(8,128)(2,1)} %dynamic-slice_bitcast_fusion.4), channel_id=1, source_target_pairs={{0,1},{1,0},{2,3},{3,2},{4,5},{5,4},{6,7},{7,6},{8,9},{9,8},{10,11... | collective-permute-start | bytes 1572872 | tf_op jit(solution)/shard_map/ppermute | solution.py:776
  814.4 23.7 %collective-permute-start.105 = (bf16[128,2048]{1,0:T(8,128)(2,1)S(1)}, bf16[128,2048]{1,0:T(8,128)(2,1)S(1)}, u32[]{:S(2)}, u32[]{:S(2)}) collective-permute-start(bf16[128,2048]{1,0:T(8,128)(2,1)S(1)} %get-tuple-element.408), channel_id=1, source_target_pairs={{0,8},{2,10},{8,16},{10,18},{16,24},{18,26},{24,28},{26,30},{28,20... | collective-permute-start | bytes 1572872 | tf_op jit(solution)/shard_map/ppermute | solution.py:760
  838.1 40.2 %collective-permute-start.115 = (bf16[64,2048]{1,0:T(8,128)(2,1)S(1)}, bf16[64,2048]{1,0:T(8,128)(2,1)S(1)}, u32[]{:S(2)}, u32[]{:S(2)}) collective-permute-start(bf16[64,2048]{1,0:T(8,128)(2,1)S(1)} %dynamic-slice_bitcast_fusion.11), channel_id=1, source_target_pairs={{0,16},{2,18},{4,20},{6,22},{8,24},{10,26},{12,28},{14,30},{16,0},... | collective-permute-start | bytes 786440 | tf_op jit(solution)/shard_map/ppermute | solution.py:779
  870.1 25.2 %collective-permute-start.117 = (bf16[64,2048]{1,0:T(8,128)(2,1)S(1)}, bf16[64,2048]{1,0:T(8,128)(2,1)S(1)}, u32[]{:S(2)}, u32[]{:S(2)}) collective-permute-start(bf16[64,2048]{1,0:T(8,128)(2,1)S(1)} %dynamic-slice_bitcast_fusion.10), channel_id=1, source_target_pairs={{0,16},{2,18},{4,20},{6,22},{8,24},{10,26},{12,28},{14,30},{16,0},... | collective-permute-start | bytes 786440 | tf_op jit(solution)/shard_map/ppermute | solution.py:779
  878.5 40.7 %collective-permute-start.107 = (bf16[552,1024]{1,0:T(8,128)(2,1)S(1)}, bf16[552,1024]{1,0:T(8,128)(2,1)}, u32[]{:S(2)}, u32[]{:S(2)}) collective-permute-start(bf16[552,1024]{1,0:T(8,128)(2,1)S(1)} %fusion.16), channel_id=1, source_target_pairs={{2,1},{1,2},{6,5},{5,6},{10,9},{9,10},{14,13},{13,14},{18,17},{17,... | collective-permute-start | bytes 3391496 | tf_op jit(solution)/shard_map/ppermute | solution.py:766
  889.2 26.0 %collective-permute-start.125 = (bf16[64,2048]{1,0:T(8,128)(2,1)S(1)}, bf16[64,2048]{1,0:T(8,128)(2,1)S(1)}, u32[]{:S(2)}, u32[]{:S(2)}) collective-permute-start(bf16[64,2048]{1,0:T(8,128)(2,1)S(1)} %add_convert_fusion.6), channel_id=1, source_target_pairs={{2,1},{1,2},{6,5},{5,6},{10,9},{9,10},{14,13},{13,14},{18,17},{17,... | collective-permute-start | bytes 786440 | tf_op jit(solution)/shard_map/ppermute | solution.py:766
  (276 other events, 3031.8 us)
Sparse Core Ops, SparseCore 0:
  689.5 104.8 reduce-scatter.1
